TPU v7x, 32 devices: a whole 2x2x4 slice. The times are simulated.
32 devices in a mesh: dp: 16 (over z, y, x), blk: 2 (over core).
Axes of the slice: x: 2, y: 2, z: 4, core: 2. Of those that a mesh axis runs over, the one named last changes fastest.
Arguments:
- inputs: bfloat16 [16, 784, 768], P('dp', 'blk'), may hold values from -6 to 6
- segments: int32 [16, 784], P('dp', 'blk'), may hold values from 0 to 7, never falling along the last dimension, each value on 1 to 196 neighbouring positions
- positions: int32 [16, 784], P('dp', 'blk'), may hold values from 0 to 195
- pos_table: bfloat16 [196, 768], replicated, may hold values from -3 to 3
- ln1_gain: float32 [768], replicated, may hold values from 0.5 to 1.5
- ln1_shift: float32 [768], replicated, may hold values from -1.5 to 1.5
- qkv_weight: bfloat16 [768, 2304], replicated, may hold values from -0.21875 to 0.21875
- query_bias: float32 [768], replicated, may hold values from -1.5 to 1.5
- value_bias: float32 [768], replicated, may hold values from -1.5 to 1.5
- out_weight: bfloat16 [768, 768], replicated, may hold values from -1.25 to 1.25
- out_bias: float32 [768], replicated, may hold values from -1.5 to 1.5
- ln2_gain: float32 [768], replicated, may hold values from 0.5 to 1.5
- ln2_shift: float32 [768], replicated, may hold values from -1.5 to 1.5
- fc1_weight: bfloat16 [768, 3072], replicated, may hold values from -0.21875 to 0.21875
- fc1_bias: float32 [3072], replicated, may hold values from -1.5 to 1.5
- fc2_weight: bfloat16 [3072, 768], replicated, may hold values from -0.109375 to 0.109375
- fc2_bias: float32 [768], replicated, may hold values from -1.5 to 1.5
- cotangent: bfloat16 [16, 784, 768], P('dp', 'blk'), may hold values from -6 to 6
Outputs:
- result: bfloat16 [16, 784, 768], P('dp', 'blk')
- input_grad: bfloat16 [16, 784, 768], P('dp', 'blk')
- table_grad: float32 [196, 768], replicated
- ln1_gain_grad: float32 [768], replicated
- ln1_shift_grad: float32 [768], replicated
- qkv_grad: float32 [768, 2304], P(('dp', 'blk'))
- query_bias_grad: float32 [768], replicated
- value_bias_grad: float32 [768], replicated
- out_grad: float32 [768, 768], P(('dp', 'blk'))
- out_bias_grad: float32 [768], replicated
- ln2_gain_grad: float32 [768], replicated
- ln2_shift_grad: float32 [768], replicated
- fc1_grad: float32 [768, 3072], P(('dp', 'blk'))
- fc1_bias_grad: float32 [3072], replicated
- fc2_grad: float32 [3072, 768], P(('dp', 'blk'))
- fc2_bias_grad: float32 [768], replicated
Inputs may be any that keep to these rules, and one draw needn't show every extreme that they name: `segments`: crop ids of a row never fall, each crop has 1 to 196 tokens.
All inputs are finite; a program needn't handle non-finite values.
Results may differ from a plain program's by a relative error of at most 0.013.
Values may be sent and summed in bfloat16 or wider, within the bound.
No kernel may reach another device: no remote copies, remote signals or barrier semaphores. Data moves between devices by JAX's collectives and lax.ppermute only.
A program may use at most 192 MiB of HBM per device.

v0:
```python
import functools

import jax
import jax.numpy as jnp
from jax import lax
from jax.experimental import pallas as pl
from jax.experimental.pallas import tpu as pltpu
from jax.sharding import PartitionSpec as P

HD = 64
SEG_MOST = 196
EPS = 1e-06
inv_root_two = 0.7071067811865476
inv_root_two_pi = 0.3989422804014327
BF = jnp.bfloat16
F32 = jnp.float32
MIB = 1 << 20


def dot_nn(a, b):
    return jnp.dot(a, b, preferred_element_type=F32)


def dot_nt(a, b):
    return lax.dot_general(a, b, (((1,), (1,)), ((), ())), preferred_element_type=F32)


def dot_tn(a, b):
    return lax.dot_general(a, b, (((0,), (0,)), ((), ())), preferred_element_type=F32)


def normalise(hidden):
    mean = jnp.mean(hidden, -1, keepdims=True)
    centred = hidden - mean
    inv = lax.rsqrt(jnp.mean(centred * centred, -1, keepdims=True) + EPS)
    return centred * inv, inv


def norm_back(grad, normal, inv, gain):
    scaled = grad * gain
    centre = jnp.mean(scaled, -1, keepdims=True)
    along = jnp.mean(scaled * normal, -1, keepdims=True)
    return inv * (scaled - centre - normal * along)


def line(ref):
    return ref[...].reshape(1, -1)


def column_sum(v):
    return jnp.sum(v, axis=0, keepdims=True)


def params(vmem):
    return pltpu.CompilerParams(vmem_limit_bytes=vmem * MIB)


def cost(flops, bytes_accessed, trans=0):
    return pl.CostEstimate(
        flops=int(flops), bytes_accessed=int(bytes_accessed), transcendentals=int(trans)
    )


def whole(shape):
    return pl.BlockSpec(shape, lambda *_: (0,) * len(shape))


ANYWHERE = pl.BlockSpec(memory_space=pl.ANY)


def copies(pairs, sem):
    return [pltpu.make_async_copy(src, dst, sem.at[k]) for k, (src, dst) in enumerate(pairs)]


def started(pairs, sem):
    made = copies(pairs, sem)
    for copy in made:
        copy.start()
    return made


def done(made):
    for copy in made:
        copy.wait()


def lanes_of(shape, head):
    return (lax.broadcasted_iota(jnp.int32, shape, 1) % 128 < HD) == (head % 2 == 0)


def embedded(x_ref, pos_ref, table_ref):
    half = x_ref.shape[0]
    places = table_ref.shape[0]
    hot = (lax.broadcasted_iota(jnp.int32, (places, half), 0) == pos_ref[...]).astype(F32).astype(BF)
    return x_ref[...].astype(F32) + dot_tn(hot, table_ref[...])


def crop_lanes(seg_ref):
    half = seg_ref.shape[1]
    hot = (lax.broadcasted_iota(jnp.int32, (8, half), 0) == seg_ref[...]).astype(F32).astype(BF)
    eye = lax.broadcasted_iota(jnp.int32, (8, 128), 0) == lax.broadcasted_iota(jnp.int32, (8, 128), 1)
    return dot_tn(hot, eye.astype(F32).astype(BF)).astype(BF)


def front_kernel(block, blk_ref, *refs):
    sources, refs = refs[:21], refs[21:]
    (
        h0_out, n1_out, n1o_out, q_out, k_out, v_out, att_out, p_out, n2_out,
        gs_out, gk_out, as_out, ak_out, res_out, gn_out, h1_out, b1g_ref,
    ) = refs[:17]
    targets, refs = refs[17:38], refs[38:]
    (
        x_ref, xo_ref, seg_ref, sego_ref, pos_ref, poso_ref, cot_ref, table_ref,
        g1_ref, s1_ref, qb_ref, vb_ref, bo_ref, g2_ref, s2_ref, b1_ref, b2_ref, wqkv_ref, wo_ref, w1_ref, w2_ref,
    ) = targets
    (
        h0_ref, own_ref, n1_ref, n1o_ref, hoto_ref, q_ref, k_ref, v_ref, bias_ref,
        att_ref, p_ref, h1_ref, n2_ref, gp_ref, act_ref, mixed_ref, gn_ref, res_ref, bias_line_ref,
        in_sem, out_sem, late_sem,
    ) = refs
    half, width = x_ref.shape
    keys = k_ref.shape[0]
    halo = keys - half
    hidden = w1_ref.shape[1]
    blk = blk_ref[0]
    start = pl.multiple_of(blk * (half - halo), 16)
    loads = [pltpu.make_async_copy(src, dst, in_sem.at[k]) for k, (src, dst) in enumerate(zip(sources, targets))]
    outs = [
        pltpu.make_async_copy(src, dst, out_sem.at[k])
        for k, (src, dst) in enumerate(
            (
                (h0_ref, h0_out), (own_ref, n1_out), (n1o_ref, n1o_out), (q_ref, q_out), (k_ref, k_out),
                (v_ref, v_out), (att_ref, att_out), (n2_ref, n2_out), (res_ref, res_out), (gn_ref, gn_out),
                (h1_ref, h1_out), (p_ref, p_out),
            )
        )
    ]
    soon = (0, 4, 7, 1, 5, 8, 9, 17, 2, 3, 10, 11)
    then = (18, 19, 20, 6, 12, 13, 14, 15, 16)
    for k in soon:
        loads[k].start()
    for k in soon[:7]:
        loads[k].wait()
    hidden0 = embedded(x_ref, pos_ref, table_ref)
    h0_ref[...] = hidden0
    normal, _ = normalise(hidden0)
    own_ref[...] = (normal * line(g1_ref) + line(s1_ref)).astype(BF)
    n1_ref[:half, :] = own_ref[...]
    normal, _ = normalise(embedded(xo_ref, poso_ref, table_ref))
    n1o_ref[...] = (normal * line(g1_ref) + line(s1_ref)).astype(BF)
    n1_ref[half:, :] = n1o_ref[pl.ds(start, halo), :]
    for k in soon[7:]:
        loads[k].wait()
    for k in then:
        loads[k].start()
    hot = crop_lanes(seg_ref)
    hoto_ref[...] = crop_lanes(sego_ref)
    bias_ref[:, :half] = (dot_nt(hot, hot) - 1.0) * 1e9
    bias_ref[:, half:] = (dot_nt(hot, hoto_ref[pl.ds(start, halo), :]) - 1.0) * 1e9
    q = dot_nn(own_ref[...], wqkv_ref[:, :width]) + line(qb_ref)
    q_ref[...] = (q.astype(BF).astype(F32) * 0.125).astype(BF)
    k_ref[...] = dot_nn(n1_ref[...], wqkv_ref[:, width : 2 * width]).astype(BF)
    v_ref[...] = (dot_nn(n1_ref[...], wqkv_ref[:, 2 * width :]) + line(vb_ref)).astype(BF)
    for out in outs[:6]:
        out.start()
    rounds = 2
    pairs = width // 128 // rounds

    def heads(i, carry):
        for pair in range(pairs):
            cols = pl.ds(pl.multiple_of((i * pairs + pair) * 128, 128), 128)
            q = q_ref[:, cols]
            both = []
            for head in range(2):
                q_one = jnp.where(lanes_of(q.shape, head), q, jnp.zeros_like(q))
                scores = dot_nt(q_one, k_ref[:, cols]) + bias_ref[...]
                top = jnp.max(scores, -1, keepdims=True)
                weight = jnp.exp(scores - top)
                probs = (weight * (1.0 / jnp.sum(weight, -1, keepdims=True))).astype(BF)
                p_ref[2 * (i * pairs + pair) + head] = probs
                both.append(dot_nn(probs, v_ref[:, cols]))
            att_ref[:, cols] = jnp.where(lanes_of(both[0].shape, 0), both[0], both[1]).astype(BF)
        return carry

    lax.fori_loop(0, rounds, heads, 0)
    outs[6].start()
    outs[11].start()
    for k in then:
        loads[k].wait()
    hidden1 = h0_ref[...] + dot_nn(att_ref[...], wo_ref[...]) + line(bo_ref)
    h1_ref[...] = hidden1
    normal, _ = normalise(hidden1)
    n2_ref[...] = (normal * line(g2_ref) + line(s2_ref)).astype(BF)
    outs[7].start()
    outs[10].start()
    late = []
    chunk = 768
    part = chunk // 2
    mixed_ref[...] = hidden1 + line(b2_ref)
    gn_ref[...] = jnp.zeros_like(gn_ref)
    bias_line_ref[...] = line(b1_ref)

    def chunks(i, carry):
        for j in range(hidden // chunk // 2):
            first = i * (hidden // 2) + j * chunk
            at = pl.ds(pl.multiple_of(first, 128), chunk)
            pre = dot_nn(n2_ref[...], w1_ref[:, at]) + bias_line_ref[:, at]
            grad_act = dot_nt(cot_ref[...], w2_ref[at, :])
            cdf = 0.5 + 0.5 * lax.erf(pre * inv_root_two)
            act = (pre * cdf).astype(BF)
            slope = cdf + pre * jnp.exp(-0.5 * pre * pre) * inv_root_two_pi
            grad_pre = (grad_act * slope).astype(BF)
            b1g_ref[:, at] = column_sum(grad_pre.astype(F32))
            gp_ref[i, :, j * chunk : (j + 1) * chunk] = grad_pre
            mine = pl.ds(pl.multiple_of(i * (hidden // 4) + j * part, 128), part)
            for c in range(2):
                act_ref[c, :, mine] = jnp.concatenate(
                    [act[:, t : t + block] for t in range(c * block, chunk, 2 * block)], 1
                )
            mixed_ref[...] += dot_nn(act, w2_ref[at, :])
            gn_ref[...] += dot_nt(grad_pre, w1_ref[:, at])
        return carry

    lax.fori_loop(0, 2, chunks, 0)
    res_ref[...] = mixed_ref[...].astype(BF)
    for c, dst in enumerate((ak_out, as_out)):
        late.append((act_ref.at[(blk + c) % 2], dst))
    for c, dst in enumerate((gk_out, gs_out)):
        late.append((gp_ref.at[(blk + c) % 2], dst))
    late = [pltpu.make_async_copy(src, dst, late_sem.at[k]) for k, (src, dst) in enumerate(late)]
    for copy in late:
        copy.start()
    outs[8].start()
    outs[9].start()
    for out in outs:
        out.wait()
    for copy in late:
        copy.wait()


def front(plan, halo, blk, x, xo, seg, sego, pos, poso, cot, table, vectors, wqkv, wo, w1, w2):
    half, width = x.shape
    hidden = w1.shape[1]
    keys = half + halo
    heads = width // HD
    anywhere = pl.BlockSpec(memory_space=pl.ANY)
    operands = (x, xo, seg, sego, pos, poso, cot, table, *vectors, wqkv, wo, w1, w2)
    shapes = [
        ((half, width), F32),
        ((half, width), BF),
        ((half, width), BF),
        ((half, width), BF),
        ((keys, width), BF),
        ((keys, width), BF),
        ((half, width), BF),
        ((heads, half, keys), BF),
        ((half, width), BF),
        ((half, hidden // 2), BF),
        ((half, hidden // 2), BF),
        ((half, hidden // 2), BF),
        ((half, hidden // 2), BF),
        ((half, width), BF),
        ((half, width), F32),
        ((half, width), F32),
        ((1, hidden), F32),
    ]
    return pl.pallas_call(
        functools.partial(front_kernel, hidden // plan.groups // 2),
        grid_spec=pltpu.PrefetchScalarGridSpec(
            num_scalar_prefetch=1,
            grid=(1,),
            in_specs=[anywhere] * len(operands),
            out_specs=[anywhere] * 16 + [whole((1, hidden))],
            scratch_shapes=[pltpu.VMEM(v.shape, v.dtype) for v in operands]
            + [
                pltpu.VMEM((half, width), F32),
                pltpu.VMEM((half, width), BF),
                pltpu.VMEM((keys, width), BF),
                pltpu.VMEM((half, width), BF),
                pltpu.VMEM((half, 128), BF),
                pltpu.VMEM((half, width), BF),
                pltpu.VMEM((keys, width), BF),
                pltpu.VMEM((keys, width), BF),
                pltpu.VMEM((half, keys), F32),
                pltpu.VMEM((half, width), BF),
                pltpu.VMEM((heads, half, keys), BF),
                pltpu.VMEM((half, width), F32),
                pltpu.VMEM((half, width), BF),
                pltpu.VMEM((2, half, hidden // 2), BF),
                pltpu.VMEM((2, half, hidden // 2), BF),
                pltpu.VMEM((half, width), F32),
                pltpu.VMEM((half, width), F32),
                pltpu.VMEM((half, width), BF),
                pltpu.VMEM((1, hidden), F32),
                pltpu.SemaphoreType.DMA((len(operands),)),
                pltpu.SemaphoreType.DMA((12,)),
                pltpu.SemaphoreType.DMA((4,)),
            ],
        ),
        out_shape=[jax.ShapeDtypeStruct(*s) for s in shapes],
        compiler_params=params(60),
        cost_estimate=cost(
            2 * half * width * (5 * width + 4 * hidden) + 4 * half * keys * width, 8 * width * hidden
        ),
        name="front",
    )(blk, *operands)


def mid_kernel(gn_hbm, h1_hbm, cot_hbm, wo_hbm, g2_hbm, gh_ref, gb_ref, ga_ref, sums_ref, *refs):
    gn_ref, h1_ref, cot_ref, wo_ref, g2_ref, sem = refs
    done(started(zip((gn_hbm, h1_hbm, cot_hbm, g2_hbm, wo_hbm), (gn_ref, h1_ref, cot_ref, g2_ref, wo_ref)), sem))
    normal, inv = normalise(h1_ref[...])
    total = gn_ref[...]
    cot = cot_ref[...].astype(F32)
    grad_hidden1 = cot + norm_back(total, normal, inv, line(g2_ref))
    gh_ref[...] = grad_hidden1
    branch = grad_hidden1.astype(BF)
    gb_ref[...] = branch
    ga_ref[...] = dot_nt(branch, wo_ref[...]).astype(BF)
    sums_ref[0:1, :] = column_sum(total * normal)
    sums_ref[1:2, :] = column_sum(total)
    sums_ref[2:3, :] = column_sum(branch.astype(F32))
    sums_ref[3:4, :] = column_sum(cot)


def mid(gn, h1, cot, wo, g2):
    half, width = h1.shape
    operands = (gn, h1, cot, wo, g2)
    shapes = [((half, width), F32), ((half, width), BF), ((half, width), BF), ((4, width), F32)]
    return pl.pallas_call(
        mid_kernel,
        grid=(1,),
        in_specs=[ANYWHERE] * 5,
        out_specs=[whole(v[0]) for v in shapes],
        out_shape=[jax.ShapeDtypeStruct(*v) for v in shapes],
        scratch_shapes=[pltpu.VMEM(v.shape, v.dtype) for v in operands] + [pltpu.SemaphoreType.DMA((5,))],
        compiler_params=params(60),
        cost_estimate=cost(1, 1),
        name="mid",
    )(*operands)


class Plan:
    def __init__(self, ndp):
        self.ndp = ndp
        self.groups = min(16, ndp)
        self.bits = self.groups.bit_length() - 1
        self.rest = ndp // self.groups
        wanted = {"feed": ((0, 1, 2, 3), (1, 2, 0, 3), (2, 0, 1, 3)), "attend": ((0, 1, 2, 3), (1, 0, 2, 3))}
        self.orders = {k: [[b for b in o if b < self.bits] for o in v] for k, v in wanted.items()}
        self.small = [b for b in (3, 2, 1, 0) if b < self.bits]

    def place(self, name, piece, p):
        code = 0
        for bit in self.orders[name][piece]:
            code = 2 * code + ((p >> bit) & 1)
        return divmod(self.groups - 1 - code, self.groups // 2)


def feed_weights_kernel(plan, own_ref, blk_ref, *refs):
    sources, refs = refs[:12], refs[-24:]
    outs, targets, stages = refs[:6], refs[6:18], refs[18:20]
    acc_ref, low_ref, in_sem, out_sem = refs[20:]
    n2_ref, n2o_ref, g_ref, go_ref, act_ref, acto_ref, cot_ref, coto_ref, att_ref, atto_ref, gb_ref, gbo_ref = targets
    own = own_ref[0]
    width = n2_ref.shape[1]
    cols = width // 2
    groups, per = plan.groups, plan.groups // 2
    chunk = g_ref.shape[1] // 2
    rows = width // groups
    unit = rows // 2
    at = pl.ds(pl.multiple_of(blk_ref[0] * cols, 128), cols)
    pairs = list(zip(sources[:10], targets)) + [(sources[10].at[:, at], gb_ref), (sources[11].at[:, at], gbo_ref)]
    loads = started(pairs, in_sem)

    def emit(number, p, value):
        piece, slot = divmod(number, 3)
        kept, place = plan.place("feed", piece, p)
        stages[kept][piece, place, slot] = value.astype(BF)

    done(loads[:4])
    for step in range(2):
        lanes = slice(step * chunk, (step + 1) * chunk)
        acc_ref[step] = dot_tn(n2_ref[...], g_ref[:, lanes]) + dot_tn(n2o_ref[...], go_ref[:, lanes])
        for p in range(groups):
            for k in range(2):
                source = pl.multiple_of((own ^ p) * rows + k * unit, 8)
                emit(5 + 2 * step + k, p, acc_ref[step, pl.ds(source, unit), :])
    done(loads[4:])
    low_ref[...] = dot_tn(att_ref[...], gb_ref[...]) + dot_tn(atto_ref[...], gbo_ref[...])
    for p in range(groups):
        source = pl.multiple_of((own ^ p) * rows, 16)
        block = low_ref[pl.ds(source, rows), :]
        emit(4, p, jnp.concatenate([block[:unit], block[unit:]], 1))
    sent = copies([(stages[kept].at[piece], outs[2 * piece + kept]) for piece in range(3) for kept in range(2)], out_sem)
    for copy in sent[4:]:
        copy.start()
    for step in range(2):
        lanes = pl.ds(pl.multiple_of(((own // per) ^ step) * chunk, 128), chunk)
        acc_ref[2 + step] = dot_tn(act_ref[:, lanes], cot_ref[...]) + dot_tn(acto_ref[:, lanes], coto_ref[...])
        for low in range(per):
            for k in range(4):
                source = pl.multiple_of(((own % per) ^ low) * (chunk // per) + k * unit, 8)
                emit(k, step * per + low, acc_ref[2 + step, pl.ds(source, unit), :])
    for copy in sent[:4]:
        copy.start()
    done(sent)


def feed_weights(plan, own, blk, *operands):
    half, width = operands[0].shape
    chunk, cols = operands[2].shape[1] // 2, width // 2
    part = jax.ShapeDtypeStruct((plan.groups // 2, 3, width // plan.groups // 2, width), BF)
    shapes = [v.shape for v in operands[:10]] + [(half, cols)] * 2

    return pl.pallas_call(
        functools.partial(feed_weights_kernel, plan),
        grid_spec=pltpu.PrefetchScalarGridSpec(
            num_scalar_prefetch=2,
            grid=(1,),
            in_specs=[ANYWHERE] * 12,
            out_specs=[ANYWHERE] * 6,
            scratch_shapes=[pltpu.VMEM(v, BF) for v in shapes]
            + [pltpu.VMEM((3,) + part.shape, BF)] * 2
            + [pltpu.VMEM((4, width, chunk), F32), pltpu.VMEM((width, cols), F32)]
            + [pltpu.SemaphoreType.DMA((12,)), pltpu.SemaphoreType.DMA((6,))],
        ),
        out_shape=(part,) * 6,
        compiler_params=params(60),
        cost_estimate=cost(1, 1),
        name="feed_weights",
    )(own, blk, *operands)


def attend_back_kernel(blk_ref, q_hbm, k_hbm, v_hbm, ga_hbm, p_hbm, *refs):
    outs, refs = refs[:6], refs[6:]
    q_ref, k_ref, v_ref, ga_ref, p_ref, d_ref, h_ref, sem, p_sem, out_sem = refs
    half, width = q_ref.shape
    cols = width // 2
    loads = started(
        [(q_hbm, q_ref), (k_hbm, k_ref), (v_hbm, v_ref), (ga_hbm, ga_ref)], sem
    )
    heads = p_ref.shape[0]
    per = 4
    probs_in = started([(p_hbm.at[k : k + per], p_ref.at[k : k + per]) for k in range(0, heads, per)], p_sem)
    done(loads + probs_in)
    pairs = heads // 4

    def one_side(side, carry):
        for pair in range(pairs):
            lanes = pl.ds(pl.multiple_of(side * cols + pair * 128, 128), 128)
            at = slice(pair * 128, pair * 128 + 128)
            q, k, grad = q_ref[:, lanes], k_ref[:, lanes], ga_ref[:, lanes]
            dqs, dks, dvs = [], [], []
            for head in range(2):
                grad_one = jnp.where(lanes_of(grad.shape, head), grad, jnp.zeros_like(grad))
                grad_probs = dot_nt(grad_one, v_ref[:, lanes])
                low = p_ref[2 * (side * pairs + pair) + head]
                probs = low.astype(F32)
                row = jnp.sum(probs * grad_probs, -1, keepdims=True)
                grad_scores = (probs * (grad_probs - row)).astype(BF)
                dqs.append(dot_nn(grad_scores, k))
                dks.append(dot_tn(q, grad_scores))
                dvs.append(dot_tn(grad, low))
            d_ref[side, 0, :, at] = (jnp.where(lanes_of(dqs[0].shape, 0), dqs[0], dqs[1]) * 0.125).astype(BF)
            first = lax.broadcasted_iota(jnp.int32, dks[0].shape, 0) < HD
            dk = jnp.where(first, dks[0], dks[1]).T.astype(BF)
            dv = jnp.where(first, dvs[0], dvs[1]).T.astype(BF)
            d_ref[side, 1, :, at] = dk[:half]
            d_ref[side, 2, :, at] = dv[:half]
            h_ref[side, 0, :, at] = dk[half:]
            h_ref[side, 1, :, at] = dv[half:]
        return carry

    lax.fori_loop(0, 2, one_side, 0)
    core = blk_ref[0]
    done(
        started(
            [
                (h_ref.at[1 - core], outs[0]),
                (h_ref.at[core], outs[1]),
                (d_ref.at[core], outs[2]),
                (d_ref.at[1 - core, 0], outs[3]),
                (d_ref.at[1 - core, 1], outs[4]),
                (d_ref.at[1 - core, 2], outs[5]),
            ],
            out_sem,
        )
    )


def attend_back(blk, q, k, v, probs, ga, *after):
    half, width = q.shape
    keys = k.shape[0]
    halo = keys - half
    cols = width // 2
    shapes = ((2, halo, cols),) * 2 + ((3, half, cols),) + ((half, cols),) * 3

    def body(blk_ref, *refs):
        ins, refs = refs[:5], refs[5 + len(after) :]
        attend_back_kernel(blk_ref, *ins, *refs)

    return pl.pallas_call(
        body,
        grid_spec=pltpu.PrefetchScalarGridSpec(
            num_scalar_prefetch=1,
            grid=(1,),
            in_specs=[ANYWHERE] * (5 + len(after)),
            out_specs=[ANYWHERE] * 6,
            scratch_shapes=[
                pltpu.VMEM((half, width), BF),
                pltpu.VMEM((keys, width), BF),
                pltpu.VMEM((keys, width), BF),
                pltpu.VMEM((half, width), BF),
                pltpu.VMEM(probs.shape, BF),
                pltpu.VMEM((2, 3, half, cols), BF),
                pltpu.VMEM((2, 2, halo, cols), BF),
                pltpu.SemaphoreType.DMA((4,)),
                pltpu.SemaphoreType.DMA((probs.shape[0] // 4,)),
                pltpu.SemaphoreType.DMA((6,)),
            ],
        ),
        out_shape=[jax.ShapeDtypeStruct(v, BF) for v in shapes],
        compiler_params=params(60),
        cost_estimate=cost(1, 1),
        name="attend_back",
    )(blk, q, k, v, ga, probs, *after)


def add_rows(ref, start, at, cols, extra):
    rows = pl.ds(start, extra.shape[0])
    part = ref[rows, pl.ds(at, cols)].astype(F32) + extra.astype(F32)
    ref[rows, pl.ds(at, cols)] = part.astype(BF)


def attend_weights_kernel(plan, own_ref, blk_ref, *refs):
    count = len(plan.orders["attend"])
    sources, outs, refs = refs[:8], refs[8 : 8 + 2 * count], refs[8 + 2 * count :]
    n1_ref, n1o_ref, hk_ref, ho_ref, mine_ref, other_ref, acc_ref, send_ref, keep_ref, sem, out_sem = refs
    half, width = n1_ref.shape
    halo = hk_ref.shape[1]
    cols = width // 2
    own, blk = own_ref[0], blk_ref[0]
    rows = width // plan.groups
    start = pl.multiple_of((1 - blk) * (half - halo), 16)
    start_other = pl.multiple_of(blk * (half - halo), 16)
    n1, n1o, d, hk, ho = sources[:5]
    pairs = [(d.at[k], mine_ref.at[:, k * cols : (k + 1) * cols]) for k in range(3)]
    pairs += [(sources[5 + k], other_ref.at[:, k * cols : (k + 1) * cols]) for k in range(3)]
    pairs += [(n1, n1_ref), (n1o, n1o_ref), (hk, hk_ref), (ho, ho_ref)]
    done(started(pairs, sem))
    for which in range(2):
        lane = (1 + which) * cols
        add_rows(mine_ref, start, lane, cols, ho_ref[which])
        add_rows(other_ref, start_other, lane, cols, hk_ref[which])
    part = rows // count
    stages = (send_ref, keep_ref)
    for at in (slice(0, width), slice(width, width + cols)):
        acc_ref[:, at] = dot_tn(n1_ref[...], mine_ref[:, at]) + dot_tn(n1o_ref[...], other_ref[:, at])
        for p in range(plan.groups):
            for piece in range(count):
                source = pl.multiple_of((own ^ p) * rows + piece * part, 8)
                kept, place = plan.place("attend", piece, p)
                stages[kept][piece, place, :, at] = acc_ref[pl.ds(source, part), at].astype(BF)
    done(
        started(
            [(stages[kept].at[piece], outs[2 * piece + kept]) for piece in range(count) for kept in range(2)], out_sem
        )
    )


def attend_weights(plan, own, blk, n1, n1o, d, hk, ho, do):
    half, width = n1.shape
    cols = width // 2
    count = len(plan.orders["attend"])
    part = jax.ShapeDtypeStruct((plan.groups // 2, width // plan.groups // count, 3 * cols), BF)
    return pl.pallas_call(
        functools.partial(attend_weights_kernel, plan),
        grid_spec=pltpu.PrefetchScalarGridSpec(
            num_scalar_prefetch=2,
            grid=(1,),
            in_specs=[ANYWHERE] * 8,
            out_specs=[ANYWHERE] * (2 * count),
            scratch_shapes=[pltpu.VMEM((half, width), BF)] * 2
            + [pltpu.VMEM(hk.shape, BF)] * 2
            + [pltpu.VMEM((half, 3 * cols), BF)] * 2
            + [pltpu.VMEM((width, 3 * cols), F32)]
            + [pltpu.VMEM((count,) + part.shape, BF)] * 2
            + [pltpu.SemaphoreType.DMA((10,)), pltpu.SemaphoreType.DMA((2 * count,))],
        ),
        out_shape=(part,) * (2 * count),
        compiler_params=params(60),
        cost_estimate=cost(1, 1),
        name="attend_weights",
    )(own, blk, n1, n1o, d, hk, ho, *do)


def front_back_kernel(places, blk_ref, *refs):
    sources, refs = refs[:13], refs[13:]
    gx_ref, small_mine, small_other = refs[:3]
    gj_ref, w_ref, h0_ref, gh_ref, g1_ref, pos_ref, sums_ref, b1_ref, ho_ref, hl_ref, small_ref, sem = refs[3:]
    half, width = h0_ref.shape
    halo = ho_ref.shape[1]
    cols = width // 2
    blk = blk_ref[0]
    start = pl.multiple_of((1 - blk) * (half - halo), 16)
    lanes = [[pl.multiple_of(which * width + core * cols, 128) for core in (blk, 1 - blk)] for which in range(3)]
    pairs = [(sources[0].at[k], gj_ref.at[:, pl.ds(lanes[k][0], cols)]) for k in range(3)]
    pairs += [(sources[1 + k], gj_ref.at[:, pl.ds(lanes[k][1], cols)]) for k in range(3)]
    pairs += list(zip(sources[4:], (ho_ref, hl_ref, w_ref, h0_ref, gh_ref, g1_ref, pos_ref, sums_ref, b1_ref)))
    loads = started(pairs, sem)
    done(loads[:9])
    for which in range(2):
        add_rows(gj_ref, start, lanes[1 + which][0], cols, ho_ref[which])
        add_rows(gj_ref, start, lanes[1 + which][1], cols, hl_ref[which])
    done(loads[9:])
    total = dot_nt(gj_ref[...], w_ref[...])
    small_ref[places + 2 : places + 3, :] = column_sum(gj_ref[:, :width].astype(F32))
    small_ref[places + 3 : places + 4, :] = column_sum(gj_ref[:, 2 * width :].astype(F32))
    normal, inv = normalise(h0_ref[...])
    small_ref[places : places + 1, :] = column_sum(total * normal)
    small_ref[places + 1 : places + 2, :] = column_sum(total)
    grad = (gh_ref[...] + norm_back(total, normal, inv, line(g1_ref))).astype(BF)
    gx_ref[...] = grad
    hot = (lax.broadcasted_iota(jnp.int32, (places, half), 0) == pos_ref[...]).astype(F32).astype(BF)
    small_ref[:places, :] = dot_nn(hot, grad)
    small_ref[places + 4 : places + 8, :] = sums_ref[...]
    for k in range(4):
        small_ref[places + 8 + k : places + 9 + k, :] = b1_ref[:, k * width : (k + 1) * width]
    for ref, core in ((small_mine, blk), (small_other, 1 - blk)):
        ref[0] = small_ref[:, pl.ds(pl.multiple_of(core * cols, 128), cols)].astype(BF)


def front_back(blk, d, ds, ho, hl, w, h0, gh, g1, pos, sums, b1, places):
    half, width = h0.shape
    extra = (1, places + 12, width // 2)
    rest = (w, h0, gh, g1, pos, sums, b1, ho, hl)
    return pl.pallas_call(
        functools.partial(front_back_kernel, places),
        grid_spec=pltpu.PrefetchScalarGridSpec(
            num_scalar_prefetch=1,
            grid=(1,),
            in_specs=[ANYWHERE] * 13,
            out_specs=[whole((half, width)), whole(extra), whole(extra)],
            scratch_shapes=[pltpu.VMEM((half, 3 * width), BF)]
            + [pltpu.VMEM(v.shape, v.dtype) for v in rest]
            + [pltpu.VMEM((places + 12, width), F32), pltpu.SemaphoreType.DMA((15,))],
        ),
        out_shape=(
            jax.ShapeDtypeStruct((half, width), BF),
            jax.ShapeDtypeStruct(extra, BF),
            jax.ShapeDtypeStruct(extra, BF),
        ),
        compiler_params=params(60),
        cost_estimate=cost(1, 1),
        name="front_back",
    )(blk, d, *ds, ho, hl, *rest[:7])


def swap(v):
    return lax.ppermute(v, "blk", [(0, 1), (1, 0)])


def across(v, ndp, flip):
    return lax.ppermute(v, "dp", [(i, i ^ flip) for i in range(ndp)])


def wide(v):
    return v.astype(F32)


def combine_kernel(plans, *refs):
    outs = refs[-len(plans) :]
    used = 0
    for out, plan in zip(outs, plans):
        at = 0
        for count, terms in plan:
            total = refs[used][...].astype(F32)
            for ref in refs[used + 1 : used + terms]:
                total = total + ref[...].astype(F32)
            used += terms
            out[at : at + count] = total.astype(out.dtype)
            at += count


def combine(arrays, plans, types, before=()):
    block = arrays[0].shape[1:]
    shapes = [(sum(count for count, _ in plan),) + block for plan in plans]
    if before:
        arrays = [behind(arrays[0], *before)] + list(arrays[1:])
    operands, specs, counts = [], [], []
    for plan in plans:
        counts.append([])
        for count, terms in plan:
            counts[-1].append((count, len(terms)))
            for index, start in terms:
                operands.append(arrays[index])
                specs.append(
                    pl.BlockSpec(
                        (count,) + block, functools.partial(lambda at, i: (at,) + (0,) * len(block), start // count)
                    )
                )
    return pl.pallas_call(
        functools.partial(combine_kernel, counts),
        grid=(1,),
        in_specs=specs,
        out_specs=[whole(v) for v in shapes],
        out_shape=[jax.ShapeDtypeStruct(v, t) for v, t in zip(shapes, types)],
        compiler_params=params(24),
        cost_estimate=cost(1, 1),
        name="combine",
    )(*operands)


class Pieces:
    def __init__(self, plan, name, parts):
        self.plan, self.orders, self.phase = plan, plan.orders[name], 0
        self.terms = [[(parts[2 * k + 1], 0, 0)] for k in range(len(self.orders))]
        self.at, self.left = 0, plan.groups // 2
        self.sent = parts[0]
        for k in range(len(self.orders)):
            self.terms[k].append((self.across(parts[2 * k], self.orders[k][0]), 0, 0))
        self.phase = 1

    def across(self, value, bit):
        return across(value, self.plan.ndp, self.plan.rest << bit)

    def collect(self):
        arrays, where = [], []
        for k in range(len(self.orders)):
            where.append([])
            for array, place, start in self.terms[k]:
                if not any(array is v for v in arrays):
                    arrays.append(array)
                index = [array is v for v in arrays].index(True)
                where[k].append((index, start + self.at - place))
        return arrays, where

    def step(self, *before):
        if self.phase >= self.plan.bits:
            return
        h = self.left // 2
        arrays, where = self.collect()
        bits = [order[self.phase] for order in self.orders]
        joined = len(set(bits)) == 1
        plans = [[(h, w)] for w in where]
        values = combine(arrays, [sum(plans, [])] if joined else plans, [BF] * len(self.orders), before)
        self.at, self.left = self.at + h, h
        self.sent = values[0]
        if joined:
            got = [self.across(values[0], bits[0])] * len(bits)
        else:
            got = [self.across(v, bit) for v, bit in zip(values, bits)]
        for k in range(len(self.orders)):
            self.terms[k].append((got[k], self.at, k * h if joined else 0))
        self.phase += 1

    def totals(self, *before):
        arrays, where = self.collect()
        return combine(arrays, [[(1, w) for w in where]], [F32], before)[0]


class Everywhere:
    def __init__(self, plan, mine, other):
        self.plan, self.phase = plan, 0
        self.flips = [plan.rest << b for b in plan.small] + [1 << b for b in range(plan.rest.bit_length() - 1)] + [None]
        self.sent, self.got = mine, swap(other)

    def step(self, *before):
        if self.phase >= len(self.flips):
            return
        (self.sent,) = combine([self.sent, self.got], [[(1, [(0, 0), (1, 0)])]], [BF], before)
        flip = self.flips[self.phase]
        self.got = swap(self.sent) if flip is None else across(self.sent, self.plan.ndp, flip)
        self.phase += 1

    def both(self):
        while self.phase < len(self.flips):
            self.step()
        return self.sent, self.got


def split_feed_kernel(blk_ref, value_ref, fc2_ref, mine, other):
    unit = value_ref.shape[2]
    units = [value_ref[k // 3, k % 3] for k in range(9)]
    cols = units[0].shape[1] // 2
    for k in range(4):
        fc2_ref[k * unit : (k + 1) * unit, :] = units[k]
    low_core = blk_ref[0] == 0
    for k in range(2):
        low, high = units[5 + 2 * k], units[6 + 2 * k]
        mine[k] = jnp.where(low_core, low, high)
        other[k] = jnp.where(low_core, high, low)
    low, high = units[4][:, :cols], units[4][:, cols:]
    mine[2, :, :cols] = jnp.where(low_core, low, high)
    other[2, :, :cols] = jnp.where(low_core, high, low)
    mine[2, :, cols:] = jnp.zeros_like(low)
    other[2, :, cols:] = jnp.zeros_like(low)


def split_feed(blk, value):
    _, _, unit, width = value.shape
    shapes = [(4 * unit, width), (3, unit, width), (3, unit, width)]
    return pl.pallas_call(
        split_feed_kernel,
        grid_spec=pltpu.PrefetchScalarGridSpec(
            num_scalar_prefetch=1, grid=(1,), in_specs=[whole(value.shape)], out_specs=[whole(v) for v in shapes]
        ),
        out_shape=[jax.ShapeDtypeStruct(v, F32) for v in shapes],
        compiler_params=params(24),
        cost_estimate=cost(1, 1),
        name="split_feed",
    )(blk, value)


def join_feed_kernel(blk_ref, mine_ref, got_ref, fc1_ref, out_ref):
    width = mine_ref.shape[2]
    cols = width // 2
    for ref, core in ((mine_ref, blk_ref[0]), (got_ref, 1 - blk_ref[0])):
        for k in range(2):
            fc1_ref[:, pl.ds(pl.multiple_of((core * 2 + k) * width, 128), width)] = ref[k]
        out_ref[:, pl.ds(pl.multiple_of(core * cols, 128), cols)] = ref[2, :, :cols]


def join_feed(blk, mine, got):
    _, rows, width = mine.shape
    shapes = [(rows, 4 * width), (rows, width)]
    return pl.pallas_call(
        join_feed_kernel,
        grid_spec=pltpu.PrefetchScalarGridSpec(
            num_scalar_prefetch=1,
            grid=(1,),
            in_specs=[whole(mine.shape)] * 2,
            out_specs=[whole(v) for v in shapes],
        ),
        out_shape=[jax.ShapeDtypeStruct(v, F32) for v in shapes],
        compiler_params=params(24),
        cost_estimate=cost(1, 1),
        name="join_feed",
    )(blk, mine, got)


def join_attend_kernel(blk_ref, mine_ref, got_ref, qkv_ref):
    cols = mine_ref.shape[1] // 3
    for ref, core in ((mine_ref, blk_ref[0]), (got_ref, 1 - blk_ref[0])):
        for k in range(3):
            at = pl.ds(pl.multiple_of((2 * k + core) * cols, 128), cols)
            qkv_ref[:, at] = ref[:, k * cols : (k + 1) * cols]


def join_attend(blk, mine, got):
    shape = (mine.shape[0], 2 * mine.shape[1])
    return pl.pallas_call(
        join_attend_kernel,
        grid_spec=pltpu.PrefetchScalarGridSpec(
            num_scalar_prefetch=1, grid=(1,), in_specs=[whole(mine.shape)] * 2, out_specs=whole(shape)
        ),
        out_shape=jax.ShapeDtypeStruct(shape, F32),
        compiler_params=params(24),
        cost_estimate=cost(1, 1),
        name="join_attend",
    )(blk, mine, got)


def split_attend_kernel(counts, blk_ref, *refs):
    mine, other, whole_ref = refs[-3:]
    part = whole_ref.shape[0] // len(counts)
    used = 0
    for piece, terms in enumerate(counts):
        total = refs[used][0].astype(F32)
        for ref in refs[used + 1 : used + terms]:
            total = total + ref[0].astype(F32)
        used += terms
        whole_ref[piece * part : (piece + 1) * part, :] = total
    half = mine.shape[0]
    low, high = whole_ref[:half, :], whole_ref[half:, :]
    low_core = blk_ref[0] == 0
    mine[...] = jnp.where(low_core, low, high)
    other[...] = jnp.where(low_core, high, low)


def split_attend(blk, pieces):
    arrays, where = pieces.collect()
    _, part, cols = arrays[0].shape
    shape = (len(where) * part // 2, cols)
    places = [(index, at) for terms in where for index, at in terms]
    return pl.pallas_call(
        functools.partial(split_attend_kernel, [len(terms) for terms in where]),
        grid_spec=pltpu.PrefetchScalarGridSpec(
            num_scalar_prefetch=1,
            grid=(1,),
            in_specs=[
                pl.BlockSpec((1, part, cols), functools.partial(lambda at, i, b: (at, 0, 0), at)) for _, at in places
            ],
            out_specs=[whole(shape)] * 2,
            scratch_shapes=[pltpu.VMEM((len(where) * part, cols), F32)],
        ),
        out_shape=[jax.ShapeDtypeStruct(shape, F32)] * 2,
        compiler_params=params(24),
        cost_estimate=cost(1, 1),
        name="split_attend",
    )(blk, *[arrays[index] for index, _ in places])


def join_small_kernel(blk_ref, mine_ref, got_ref, *outs):
    joined_ref = outs[-1]
    cols = mine_ref.shape[2]
    width = 2 * cols
    places = outs[0].shape[0]
    for ref, core in ((mine_ref, blk_ref[0]), (got_ref, 1 - blk_ref[0])):
        joined_ref[:, pl.ds(pl.multiple_of(core * cols, 128), cols)] = ref[0].astype(F32)
    outs[0][...] = joined_ref[:places, :]
    for k, out in enumerate(outs[1:9]):
        out[...] = joined_ref[places + k, :]
    for k in range(outs[9].shape[0] // width):
        outs[9][k * width : (k + 1) * width] = joined_ref[places + 8 + k, :]


def join_small(blk, mine, got, places, hidden):
    _, rows, cols = mine.shape
    width = 2 * cols
    shapes = [(places, width)] + [(width,)] * 8 + [(hidden,)]
    return pl.pallas_call(
        join_small_kernel,
        grid_spec=pltpu.PrefetchScalarGridSpec(
            num_scalar_prefetch=1,
            grid=(1,),
            in_specs=[whole(mine.shape)] * 2,
            out_specs=[whole(v) for v in shapes],
            scratch_shapes=[pltpu.VMEM((rows, width), F32)],
        ),
        out_shape=[jax.ShapeDtypeStruct(v, F32) for v in shapes],
        compiler_params=params(24),
        cost_estimate=cost(1, 1),
        name="join_small",
    )(blk, mine, got)


def behind(values, *others):
    return lax.optimization_barrier((values, others))[0]


def rest_of(plan, value, blk):
    groups = [[g * plan.rest + i for i in range(plan.rest)] for g in range(plan.groups)]
    value = lax.psum(value, "dp", axis_index_groups=groups)
    rows = value.shape[0] // (2 * plan.rest)
    return lax.dynamic_slice_in_dim(value, ((lax.axis_index("dp") % plan.rest) * 2 + blk) * rows, rows, axis=0)


def per_device(
    ndp, inputs, segments, positions, pos_table, ln1_gain, ln1_shift, qkv_weight, query_bias,
    value_bias, out_weight, out_bias, ln2_gain, ln2_shift, fc1_weight, fc1_bias, fc2_weight,
    fc2_bias, cotangent,
):
    plan = Plan(ndp)
    x, cot = inputs[0], cotangent[0]
    half, width = x.shape
    hidden = fc1_weight.shape[1]
    places = pos_table.shape[0]
    halo = next(h for h in range(SEG_MOST - 1, half + 1) if (half + h) % 128 == 0 and (half - h) % 16 == 0)
    blk = lax.axis_index("blk")
    dp = lax.axis_index("dp")
    blk1 = blk.astype(jnp.int32).reshape(1)
    own1 = (dp // plan.rest).astype(jnp.int32).reshape(1)

    x_other, seg_other, pos_other = swap(x), swap(segments), swap(positions)
    cot_other = swap(cot)
    vectors = (ln1_gain, ln1_shift, query_bias, value_bias, out_bias, ln2_gain, ln2_shift, fc1_bias, fc2_bias)
    (
        hidden0, n1, n1_other, q, k, v, att, probs, n2, grad_send, grad_keep, act_send, act_keep, result, gn2, hidden1,
        b1_grad,
    ) = front(
        plan, halo, blk1, x, x_other, segments, seg_other, positions, pos_other, cot, pos_table, vectors,
        qkv_weight, out_weight, fc1_weight, fc2_weight,
    )
    grad_other, act_other, n2_other = swap(grad_send), swap(act_send), swap(behind(n2, cot_other))
    gh1, gb, ga, sums = mid(gn2, hidden1, cot, out_weight, ln2_gain)
    att_other, gb_other = swap(att), swap(gb)
    parts = feed_weights(
        plan, own1, blk1, behind(n2, ga), n2_other, grad_keep, grad_other, act_keep, act_other, cot, cot_other, att, att_other, gb, gb_other,
    )
    feed_sums = Pieces(plan, "feed", parts)
    h_send, h_keep, d_keep, *d_send = attend_back(blk1, behind(q, parts[0]), k, v, probs, ga)
    h_other, h_late = swap(h_send), swap(h_keep)
    d_other = [swap(v) for v in d_send]
    grad_x, mine, other = front_back(
        blk1, d_keep, d_send, h_other, h_late, qkv_weight, hidden0, gh1, ln1_gain, positions, sums, b1_grad, places
    )
    small = Everywhere(plan, mine, other)
    feed_sums.step(grad_x)
    small.step(feed_sums.sent)
    parts = attend_weights(
        plan, own1, blk1, behind(n1, small.sent), n1_other, d_keep, h_keep, h_other, d_other
    )
    attend_sums = Pieces(plan, "attend", parts)
    before = parts[0]
    for item in (small, feed_sums, attend_sums, small, feed_sums, attend_sums, small, attend_sums, small):
        item.step(before)
        before = item.sent
    unit = width // plan.groups // 2
    value = feed_sums.totals()
    attend_mine, attend_sent = split_attend(blk1, attend_sums)
    if plan.rest == 1:
        fc2_grad, feed_mine, feed_sent = split_feed(blk1, value)
        feed_got = swap(feed_sent)
        qkv_grad = join_attend(blk1, attend_mine, swap(attend_sent))
        fc1_grad, out_grad = join_feed(blk1, feed_mine, feed_got)
    else:
        units = value.reshape(9, unit, width)
        fc2_grad = rest_of(plan, lax.all_gather(units[:4].reshape(-1, width), "blk", axis=0, tiled=True), blk)
        rows = jnp.concatenate([units[5:7].reshape(-1, width), units[7:].reshape(-1, width)], 1)
        fc1_grad = rest_of(plan, lax.all_gather(rows, "blk", axis=1, tiled=True), blk)
        rows = jnp.concatenate([units[4][:, : width // 2], units[4][:, width // 2 :]], 0)
        out_grad = rest_of(plan, lax.all_gather(rows, "blk", axis=1, tiled=True), blk)
        rows = jnp.where(blk == 0, jnp.stack([attend_mine, attend_sent]), jnp.stack([attend_sent, attend_mine]))
        rows = rows.reshape(2 * unit, 3, width // 2)
        qkv_grad = rest_of(plan, lax.all_gather(rows, "blk", axis=2, tiled=True).reshape(2 * unit, -1), blk)
    table, *vec, b1_all = join_small(blk1, *small.both(), places, hidden)
    return (
        result[None], grad_x[None], table, vec[0], vec[1], qkv_grad, vec[2], vec[3], out_grad,
        vec[6], vec[4], vec[5], fc1_grad, b1_all, fc2_grad, vec[7],
    )


def solution(mesh):
    split = P("dp", "blk", None)
    ids = P("dp", "blk")
    both = P(("dp", "blk"), None)
    none = P()
    return jax.shard_map(
        functools.partial(per_device, mesh.shape["dp"]),
        mesh=mesh,
        in_specs=(split, ids, ids) + (none,) * 14 + (split,),
        out_specs=(
            split, split, none, none, none, both, none, none, both, none, none, none, both, none, both, none,
        ),
        check_vma=False,
    )
```

profile of v0, /device:TPU:0, one launch (start us, length us, event | category | flops | bytes accessed | tf_op | source)
XLA Modules:
  0.0 141.9 jit_solution(82756916371340450)
XLA Ops:
  1.8 1.3 collective-permute-done.1.refs_3_
  3.1 0.6 copy-done.13
  3.9 25.8 %front.1 = (f32[392,768]{1,0:T(8,128)}, bf16[392,768]{1,0:T(8,128)(2,1)}, bf16[392,768]{1,0:T(8,128)(2,1)}, bf16[392,768]{1,0:T(8,128)(2,1)}, bf16[640,768]{1,0:...) custom-call(s32[1]{0:T(128)} %bitcast.blk_ref, ...), custom_call_target="tpu_custom_call" | custom-call | flops 10481565696 | bytes 18874368 | tf_op jit(solution)/shard_map/front/pallas_call | solution.py:267
  30.8 4.7 %mid.1 = (f32[392,768]{1,0:T(8,128)}, bf16[392,768]{1,0:T(8,128)(2,1)}, bf16[392,768]{1,0:T(8,128)(2,1)}, f32[4,768]{1,0:T(4,128)}) custom-call(f32[392,768]{1,0:T(8,128)} %get-tuple-element.99.gn_hbm, f32[392,768]{1,0:T(8,128)} %get-tuple-element.100.h1_hbm, bf16[392,768]{1,0:T(8,128)(2,1)} %bitcast.8, bf16[768,768]{1,0:T(8,128)(2,1)} %wo_hbm.1, f32[768]{0:T(1024)} %g2_hbm.1), custom_call_target="tpu_custom_call" | custom-call | flops 1 | bytes 1 | tf_op jit(solution)/shard_map/mid/pallas_call | solution.py:330
  36.5 1.4 collective-permute-done.8.refs_11_
  37.9 0.8 copy-done.10
  39.5 10.6 %feed_weights.1 = (bf16[8,3,24,768]{3,2,1,0:T(8,128)(2,1)}, bf16[8,3,24,768]{3,2,1,0:T(8,128)(2,1)}, bf16[8,3,24,768]{3,2,1,0:T(8,128)(2,1)}, bf16[8,3,24,768]{3...) custom-call(s32[1]{0:T(128)} %bitcast.4.own_ref, s32[1]{0:T(128)} %bitcast.blk_ref, ...), custom_call_target="tpu_custom_call" | custom-call | flops 1 | bytes 1 | tf_op jit(solution)/shard_map/feed_weights/pallas_call | solution.py:416
  50.2 3.0 %collective-permute-start.12 = (bf16[8,3,24,768]{3,2,1,0:T(8,128)(2,1)}, bf16[8,3,24,768]{3,2,1,0:T(8,128)(2,1)S(1)}, u32[]{:S(2)}, u32[]{:S(2)}) collective-permute-start(bf16[8,3,24,768]{3,2,1,0:T(8,128)(2,1)} %get-tuple-element.130), channel_id=1, source_target_pairs={{0,4},{2,6},{4,0},{6,2},{8,12},{10,14},{12,8},{14,10},{16,20},{18,... | collective-permute-start | bytes 2654216 | tf_op jit(solution)/shard_map/ppermute | solution.py:665
  53.1 1.6 %collective-permute-start.13 = (bf16[8,3,24,768]{3,2,1,0:T(8,128)(2,1)}, bf16[8,3,24,768]{3,2,1,0:T(8,128)(2,1)}, u32[]{:S(2)}, u32[]{:S(2)}) collective-permute-start(bf16[8,3,24,768]{3,2,1,0:T(8,128)(2,1)} %get-tuple-element.132), channel_id=1, source_target_pairs={{0,8},{2,10},{4,12},{6,14},{8,0},{10,2},{12,4},{14,6},{16,24},{18,... | collective-permute-start | bytes 2654216 | tf_op jit(solution)/shard_map/ppermute | solution.py:665
  54.7 1.5 %collective-permute-start.11 = (bf16[8,3,24,768]{3,2,1,0:T(8,128)(2,1)}, bf16[8,3,24,768]{3,2,1,0:T(8,128)(2,1)}, u32[]{:S(2)}, u32[]{:S(2)}) collective-permute-start(bf16[8,3,24,768]{3,2,1,0:T(8,128)(2,1)} %get-tuple-element.110), channel_id=1, source_target_pairs={{0,2},{2,0},{4,6},{6,4},{8,10},{10,8},{12,14},{14,12},{16,18},{18,... | collective-permute-start | bytes 2654216 | tf_op jit(solution)/shard_map/ppermute | solution.py:665
  56.2 14.6 %attend_back.1 = (bf16[2,248,384]{2,1,0:T(8,128)(2,1)}, bf16[2,248,384]{2,1,0:T(8,128)(2,1)}, bf16[3,392,384]{2,1,0:T(8,128)(2,1)}, bf16[392,384]{1,0:T(8,128)(2...) custom-call(s32[1]{0:T(128)} %bitcast.blk_ref, bf16[392,768]{1,0:T(8,128)(2,1)} %get-tuple-element.111.refs_0_, ...), custom_call_target="tpu_custom_call" | custom-call | flops 1 | bytes 1 | tf_op jit(solution)/shard_map/attend_back/pallas_call | solution.py:503
  71.4 1.4 collective-permute-done.9.refs_4_
  74.1 7.2 %front_back.1 = (bf16[392,768]{1,0:T(8,128)(2,1)}, bf16[1,208,384]{2,1,0:T(8,128)(2,1)}, bf16[1,208,384]{2,1,0:T(8,128)(2,1)}) custom-call(s32[1]{0:T(128)} %bitcast.blk_ref, bf16[3,392,384]{2,1,0:T(8,128)(2,1)} %get-tuple-element.115.refs_0_.refs_2_, bf16[392,384]{1,0:T(8,128)(2,1)} %get-tuple-element.116.refs_1_, ...), custom_call_target="tpu_custom_call" | custom-call | flops 1 | bytes 1 | tf_op jit(solution)/shard_map/front_back/pallas_call | solution.py:638
  81.6 2.4 %combine.12 = (bf16[4,3,24,768]{3,2,1,0:T(8,128)(2,1)}, bf16[4,3,24,768]{3,2,1,0:T(8,128)(2,1)}, bf16[4,3,24,768]{3,2,1,0:T(8,128)(2,1)}) custom-call(bf16[8,3,24,768]{3,2,1,0:T(8,128)(2,1)S(1)} %copy-done, bf16[8,3,24,768]{3,2,1,0:T(8,128)(2,1)} %collective-permute-done.11.refs_1_, bf16[8,3,24,768]{3,2,1,0:T(8,128)(2,1)S(1)} %copy-done.1, ...), custom_call_target="tpu_custom_call" | custom-call | flops 1 | bytes 1 | tf_op jit(solution)/shard_map/combine/pallas_call | solution.py:703
  84.0 0.7 combine.13.refs_0_
  84.7 2.6 %collective-permute-start.18 = (bf16[1,208,384]{2,1,0:T(8,128)(2,1)}, bf16[1,208,384]{2,1,0:T(8,128)(2,1)}, u32[]{:S(2)}, u32[]{:S(2)}) collective-permute-start(bf16[1,208,384]{2,1,0:T(8,128)(2,1)} %combine.13.refs_0_), channel_id=1, source_target_pairs={{0,16},{2,18},{4,20},{6,22},{8,24},{10,26},{12,28},{14,30},{16,0},... | collective-permute-start | bytes 479240 | tf_op jit(solution)/shard_map/ppermute | solution.py:665
  87.2 1.4 collective-permute-start.20
  88.6 1.5 %collective-permute-start.21 = (bf16[4,3,24,768]{3,2,1,0:T(8,128)(2,1)}, bf16[4,3,24,768]{3,2,1,0:T(8,128)(2,1)}, u32[]{:S(2)}, u32[]{:S(2)}) collective-permute-start(bf16[4,3,24,768]{3,2,1,0:T(8,128)(2,1)} %get-tuple-element.144), channel_id=1, source_target_pairs={{0,2},{2,0},{4,6},{6,4},{8,10},{10,8},{12,14},{14,12},{16,18},{18,... | collective-permute-start | bytes 1327112 | tf_op jit(solution)/shard_map/ppermute | solution.py:665
  90.1 1.5 %collective-permute-start.19 = (bf16[4,3,24,768]{3,2,1,0:T(8,128)(2,1)}, bf16[4,3,24,768]{3,2,1,0:T(8,128)(2,1)}, u32[]{:S(2)}, u32[]{:S(2)}) collective-permute-start(bf16[4,3,24,768]{3,2,1,0:T(8,128)(2,1)} %get-tuple-element.133), channel_id=1, source_target_pairs={{0,4},{2,6},{4,0},{6,2},{8,12},{10,14},{12,8},{14,10},{16,20},{18,... | collective-permute-start | bytes 1327112 | tf_op jit(solution)/shard_map/ppermute | solution.py:665
  91.7 5.9 %attend_weights.1 = (bf16[8,24,1152]{2,1,0:T(8,128)(2,1)}, bf16[8,24,1152]{2,1,0:T(8,128)(2,1)}, bf16[8,24,1152]{2,1,0:T(8,128)(2,1)}, bf16[8,24,1152]{2,1,0:T(8,128)(2,1)}) custom-call(s32[1]{0:T(128)} %bitcast.4.own_ref, s32[1]{0:T(128)} %bitcast.blk_ref, bf16[392,768]{1,0:T(8,128)(2,1)} %get-tuple-element.137.refs_0_, ...), custom_call_target="tpu_custom_call" | custom-call | flops 1 | bytes 1 | tf_op jit(solution)/shard_map/attend_weights/pallas_call | solution.py:577
  97.6 0.6 collective-permute-start.23
  98.7 1.0 combine.14.refs_0_
  99.8 2.7 %collective-permute-done.20.refs_5_.refs_6_.refs_7_ = bf16[4,3,24,768]{3,2,1,0:T(8,128)(2,1)S(1)} collective-permute-done((bf16[4,3,24,768]{3,2,1,0:T(8,128)(2,1)}, bf16[4,3,24,768]{3,2,1,0:T(8,128)(2,1)S(1)}, u32[]{:S(2)}, u32[]{:S(2)}) %collective-permute-start.20) | collective-permute-done | bytes 442400 | tf_op jit(solution)/shard_map/ppermute | solution.py:665
  102.4 0.9 collective-permute-start.24
  103.6 1.5 %combine.15 = (bf16[2,3,24,768]{3,2,1,0:T(8,128)(2,1)S(1)}, bf16[2,3,24,768]{3,2,1,0:T(8,128)(2,1)S(1)}, bf16[2,3,24,768]{3,2,1,0:T(8,128)(2,1)S(1)}) custom-call(bf16[8,3,24,768]{3,2,1,0:T(8,128)(2,1)S(1)} %copy-done, bf16[8,3,24,768]{3,2,1,0:T(8,128)(2,1)} %collective-permute-done.11.refs_1_, bf16[4,3,24,768]{3,2,1,0:T(8,128)(2,1)} %collective-permute-done.19.refs_2_, ...), custom_call_target="tpu_custom_call" | custom-call | flops 1 | bytes 1 | tf_op jit(solution)/shard_map/combine/pallas_call | solution.py:703
  105.1 0.8 collective-permute-start.26
  105.9 1.5 %collective-permute-start.27 = (bf16[2,3,24,768]{3,2,1,0:T(8,128)(2,1)S(1)}, bf16[2,3,24,768]{3,2,1,0:T(8,128)(2,1)S(1)}, u32[]{:S(2)}, u32[]{:S(2)}) collective-permute-start(bf16[2,3,24,768]{3,2,1,0:T(8,128)(2,1)S(1)} %get-tuple-element.153), channel_id=1, source_target_pairs={{0,4},{2,6},{4,0},{6,2},{8,12},{10,14},{12,8},{14,10},{16,20},{18,... | collective-permute-start | bytes 663560 | tf_op jit(solution)/shard_map/ppermute | solution.py:665
  107.4 5.5 %collective-permute-done.23.refs_3_.refs_4_.refs_5_.refs_6_ = bf16[8,24,1152]{2,1,0:T(8,128)(2,1)S(1)} collective-permute-done((bf16[8,24,1152]{2,1,0:T(8,128)(2,1)}, bf16[8,24,1152]{2,1,0:T(8,128)(2,1)S(1)}, u32[]{:S(2)}, u32[]{:S(2)}) %collective-permute-start.23) | collective-permute-done | bytes 442400 | tf_op jit(solution)/shard_map/ppermute | solution.py:665
  113.5 0.8 collective-permute-start.29
  114.3 1.3 collective-permute-start.28
  115.7 0.5 collective-permute-done.26.refs_7_.refs_8_
  116.2 1.4 %collective-permute-done.27.refs_11_.refs_13_ = bf16[2,3,24,768]{3,2,1,0:T(8,128)(2,1)S(1)} collective-permute-done((bf16[2,3,24,768]{3,2,1,0:T(8,128)(2,1)S(1)}, bf16[2,3,24,768]{3,2,1,0:T(8,128)(2,1)S(1)}, u32[]{:S(2)}, u32[]{:S(2)}) %collective-permute-start.27) | collective-permute-done | bytes 221216 | tf_op jit(solution)/shard_map/ppermute | solution.py:665
  117.7 1.2 collective-permute-done.25.refs_3_
  118.9 1.2 combine.18
  120.5 1.5 %collective-permute-start.30 = (bf16[1,208,384]{2,1,0:T(8,128)(2,1)S(1)}, bf16[1,208,384]{2,1,0:T(8,128)(2,1)S(1)}, u32[]{:S(2)}, u32[]{:S(2)}) collective-permute-start(bf16[1,208,384]{2,1,0:T(8,128)(2,1)S(1)} %combine.17.refs_0_), channel_id=1, source_target_pairs={{0,4},{2,6},{4,0},{6,2},{8,12},{10,14},{12,8},{14,10},{16,20},{18,... | collective-permute-start | bytes 479240 | tf_op jit(solution)/shard_map/ppermute | solution.py:665
  122.4 0.7 collective-permute-start.31
  123.1 2.7 %collective-permute-done.30.refs_1_ = bf16[1,208,384]{2,1,0:T(8,128)(2,1)S(1)} collective-permute-done((bf16[1,208,384]{2,1,0:T(8,128)(2,1)S(1)}, bf16[1,208,384]{2,1,0:T(8,128)(2,1)S(1)}, u32[]{:S(2)}, u32[]{:S(2)}) %collective-permute-start.30) | collective-permute-done | bytes 159776 | tf_op jit(solution)/shard_map/ppermute | solution.py:665
  125.8 0.6 collective-permute-start.32
  126.4 3.5 %collective-permute-done.31.refs_3_.refs_7_.refs_8_ = bf16[4,24,1152]{2,1,0:T(8,128)(2,1)S(1)} collective-permute-done((bf16[4,24,1152]{2,1,0:T(8,128)(2,1)S(1)}, bf16[4,24,1152]{2,1,0:T(8,128)(2,1)S(1)}, u32[]{:S(2)}, u32[]{:S(2)}) %collective-permute-start.31) | collective-permute-done | bytes 221216 | tf_op jit(solution)/shard_map/ppermute | solution.py:665
  130.0 2.9 %collective-permute-start.34 = (bf16[2,24,1152]{2,1,0:T(8,128)(2,1)S(1)}, bf16[2,24,1152]{2,1,0:T(8,128)(2,1)S(1)}, u32[]{:S(2)}, u32[]{:S(2)}) collective-permute-start(bf16[2,24,1152]{2,1,0:T(8,128)(2,1)S(1)} %combine.21), channel_id=1, source_target_pairs={{0,16},{2,18},{4,20},{6,22},{8,24},{10,26},{12,28},{14,30},{16,0},... | collective-permute-start | bytes 331784 | tf_op jit(solution)/shard_map/ppermute | solution.py:665
  132.9 2.8 %collective-permute-done.36.refs_4_.refs_9_.refs_14_ = bf16[3,3,24,768]{3,2,1,0:T(8,128)(2,1)S(1)} collective-permute-done((bf16[3,3,24,768]{3,2,1,0:T(8,128)(2,1)S(1)}, bf16[3,3,24,768]{3,2,1,0:T(8,128)(2,1)S(1)}, u32[]{:S(2)}, u32[]{:S(2)}) %collective-permute-start.36) | collective-permute-done | bytes 331808 | tf_op jit(solution)/shard_map/ppermute | solution.py:665
  135.7 1.3 combine.23.value_ref
  137.0 0.8 split_feed.1
  137.8 0.6 collective-permute-start.33
  138.6 0.9 collective-permute-done.33.got_ref
  139.5 0.9 join_small.1
  140.4 0.7 join_attend.1
  141.1 0.8 join_feed.1
  (81 shorter events, 8.8 us)
Async XLA Ops:
  0.6 2.4 %collective-permute-start = (bf16[392,768]{1,0:T(8,128)(2,1)}, bf16[392,768]{1,0:T(8,128)(2,1)S(1)}, u32[]{:S(2)}, u32[]{:S(2)}) collective-permute-start(bf16[392,768]{1,0:T(8,128)(2,1)} %bitcast.10), channel_id=1, source_target_pairs={{0,1},{1,0},{2,3},{3,2},{4,5},{5,4},{6,7},{7,6},{8,9},{9,8},{10,11... | collective-permute-start | bytes 1806344 | tf_op jit(solution)/shard_map/ppermute | solution.py:661
  1.2 1.9 %collective-permute-start.1 = (s32[1,392]{1,0:T(1,128)}, s32[1,392]{1,0:T(1,128)S(1)}, u32[]{:S(2)}, u32[]{:S(2)}) collective-permute-start(s32[1,392]{1,0:T(1,128)} %refs_2_.1), channel_id=1, source_target_pairs={{0,1},{1,0},{2,3},{3,2},{4,5},{5,4},{6,7},{7,6},{8,9},{9,8},{10,11... | collective-permute-start | bytes 4712 | tf_op jit(solution)/shard_map/ppermute | solution.py:661
  1.2 1.8 %collective-permute-start.2 = (s32[1,392]{1,0:T(1,128)}, s32[1,392]{1,0:T(1,128)S(1)}, u32[]{:S(2)}, u32[]{:S(2)}) collective-permute-start(s32[1,392]{1,0:T(1,128)} %refs_10_.3), channel_id=1, source_target_pairs={{0,1},{1,0},{2,3},{3,2},{4,5},{5,4},{6,7},{7,6},{8,9},{9,8},{10,11... | collective-permute-start | bytes 4712 | tf_op jit(solution)/shard_map/ppermute | solution.py:661
  1.7 28.6 %collective-permute-start.3 = (bf16[392,768]{1,0:T(8,128)(2,1)}, bf16[392,768]{1,0:T(8,128)(2,1)S(1)}, u32[]{:S(2)}, u32[]{:S(2)}) collective-permute-start(bf16[392,768]{1,0:T(8,128)(2,1)} %bitcast.6), channel_id=1, source_target_pairs={{0,1},{1,0},{2,3},{3,2},{4,5},{5,4},{6,7},{7,6},{8,9},{9,8},{10,11... | collective-permute-start | bytes 1806344 | tf_op jit(solution)/shard_map/ppermute | solution.py:661
  29.7 8.1 %collective-permute-start.5 = (bf16[392,1536]{1,0:T(8,128)(2,1)}, bf16[392,1536]{1,0:T(8,128)(2,1)S(1)}, u32[]{:S(2)}, u32[]{:S(2)}) collective-permute-start(bf16[392,1536]{1,0:T(8,128)(2,1)} %get-tuple-element.105), channel_id=1, source_target_pairs={{0,1},{1,0},{2,3},{3,2},{4,5},{5,4},{6,7},{7,6},{8,9},{9,8},{10,11... | collective-permute-start | bytes 3612680 | tf_op jit(solution)/shard_map/ppermute | solution.py:661
  30.2 7.7 %collective-permute-start.6 = (bf16[392,1536]{1,0:T(8,128)(2,1)}, bf16[392,1536]{1,0:T(8,128)(2,1)S(1)}, u32[]{:S(2)}, u32[]{:S(2)}) collective-permute-start(bf16[392,1536]{1,0:T(8,128)(2,1)} %get-tuple-element.107), channel_id=1, source_target_pairs={{0,1},{1,0},{2,3},{3,2},{4,5},{5,4},{6,7},{7,6},{8,9},{9,8},{10,11... | collective-permute-start | bytes 3612680 | tf_op jit(solution)/shard_map/ppermute | solution.py:661
  30.3 5.2 %copy-start.9 = (bf16[392,768]{1,0:T(8,128)(2,1)}, bf16[392,768]{1,0:T(8,128)(2,1)S(1)}, u32[]{:S(2)}) copy-start(bf16[392,768]{1,0:T(8,128)(2,1)S(1)} %collective-permute-done.3.refs_7_) | copy-start | bytes 1806340
  30.3 5.7 %collective-permute-start.4 = (bf16[392,768]{1,0:T(8,128)(2,1)}, bf16[392,768]{1,0:T(8,128)(2,1)}, u32[]{:S(2)}, u32[]{:S(2)}) collective-permute-start(bf16[392,768]{1,0:T(8,128)(2,1)} %get-tuple-element.103.refs_0_), channel_id=1, source_target_pairs={{0,1},{1,0},{2,3},{3,2},{4,5},{5,4},{6,7},{7,6},{8,9},{9,8},{10,11... | collective-permute-start | bytes 1806344 | tf_op jit(solution)/shard_map/ppermute | solution.py:661
  30.7 5.8 %collective-permute-start.7 = (bf16[392,768]{1,0:T(8,128)(2,1)}, bf16[392,768]{1,0:T(8,128)(2,1)}, u32[]{:S(2)}, u32[]{:S(2)}) collective-permute-start(bf16[392,768]{1,0:T(8,128)(2,1)} %get-tuple-element.108.refs_8_), channel_id=1, source_target_pairs={{0,1},{1,0},{2,3},{3,2},{4,5},{5,4},{6,7},{7,6},{8,9},{9,8},{10,11... | collective-permute-start | bytes 1806344 | tf_op jit(solution)/shard_map/ppermute | solution.py:661
  35.5 2.3 %collective-permute-start.8 = (bf16[392,768]{1,0:T(8,128)(2,1)}, bf16[392,768]{1,0:T(8,128)(2,1)S(1)}, u32[]{:S(2)}, u32[]{:S(2)}) collective-permute-start(bf16[392,768]{1,0:T(8,128)(2,1)} %get-tuple-element.109.refs_10_), channel_id=1, source_target_pairs={{0,1},{1,0},{2,3},{3,2},{4,5},{5,4},{6,7},{7,6},{8,9},{9,8},{10,11... | collective-permute-start | bytes 1806344 | tf_op jit(solution)/shard_map/ppermute | solution.py:661
  37.9 1.2 copy-start.7
  37.9 1.7 %copy-start.8 = (bf16[392,1536]{1,0:T(8,128)(2,1)}, bf16[392,1536]{1,0:T(8,128)(2,1)S(1)}, u32[]{:S(2)}) copy-start(bf16[392,1536]{1,0:T(8,128)(2,1)S(1)} %collective-permute-done.6.refs_5_) | copy-start | bytes 3612676
  50.2 23.3 %collective-permute-start.12 = (bf16[8,3,24,768]{3,2,1,0:T(8,128)(2,1)}, bf16[8,3,24,768]{3,2,1,0:T(8,128)(2,1)S(1)}, u32[]{:S(2)}, u32[]{:S(2)}) collective-permute-start(bf16[8,3,24,768]{3,2,1,0:T(8,128)(2,1)} %get-tuple-element.130), channel_id=1, source_target_pairs={{0,4},{2,6},{4,0},{6,2},{8,12},{10,14},{12,8},{14,10},{16,20},{18,... | collective-permute-start | bytes 2654216 | tf_op jit(solution)/shard_map/ppermute | solution.py:665
  53.1 28.2 %collective-permute-start.13 = (bf16[8,3,24,768]{3,2,1,0:T(8,128)(2,1)}, bf16[8,3,24,768]{3,2,1,0:T(8,128)(2,1)}, u32[]{:S(2)}, u32[]{:S(2)}) collective-permute-start(bf16[8,3,24,768]{3,2,1,0:T(8,128)(2,1)} %get-tuple-element.132), channel_id=1, source_target_pairs={{0,8},{2,10},{4,12},{6,14},{8,0},{10,2},{12,4},{14,6},{16,24},{18,... | collective-permute-start | bytes 2654216 | tf_op jit(solution)/shard_map/ppermute | solution.py:665
  54.7 26.9 %collective-permute-start.11 = (bf16[8,3,24,768]{3,2,1,0:T(8,128)(2,1)}, bf16[8,3,24,768]{3,2,1,0:T(8,128)(2,1)}, u32[]{:S(2)}, u32[]{:S(2)}) collective-permute-start(bf16[8,3,24,768]{3,2,1,0:T(8,128)(2,1)} %get-tuple-element.110), channel_id=1, source_target_pairs={{0,2},{2,0},{4,6},{6,4},{8,10},{10,8},{12,14},{14,12},{16,18},{18,... | collective-permute-start | bytes 2654216 | tf_op jit(solution)/shard_map/ppermute | solution.py:665
  70.8 2.0 %collective-permute-start.9 = (bf16[2,248,384]{2,1,0:T(8,128)(2,1)}, bf16[2,248,384]{2,1,0:T(8,128)(2,1)S(1)}, u32[]{:S(2)}, u32[]{:S(2)}) collective-permute-start(bf16[2,248,384]{2,1,0:T(8,128)(2,1)} %get-tuple-element.119), channel_id=1, source_target_pairs={{0,1},{1,0},{2,3},{3,2},{4,5},{5,4},{6,7},{7,6},{8,9},{9,8},{10,11... | collective-permute-start | bytes 1142792 | tf_op jit(solution)/shard_map/ppermute | solution.py:661
  70.9 2.4 %collective-permute-start.10 = (bf16[2,248,384]{2,1,0:T(8,128)(2,1)}, bf16[2,248,384]{2,1,0:T(8,128)(2,1)S(1)}, u32[]{:S(2)}, u32[]{:S(2)}) collective-permute-start(bf16[2,248,384]{2,1,0:T(8,128)(2,1)} %get-tuple-element.120.refs_3_), channel_id=1, source_target_pairs={{0,1},{1,0},{2,3},{3,2},{4,5},{5,4},{6,7},{7,6},{8,9},{9,8},{10,11... | collective-permute-start | bytes 1142792 | tf_op jit(solution)/shard_map/ppermute | solution.py:661
  72.8 1.3 copy-start.6
  72.8 15.9 %collective-permute-start.15 = (bf16[392,384]{1,0:T(8,128)(2,1)}, bf16[392,384]{1,0:T(8,128)(2,1)}, u32[]{:S(2)}, u32[]{:S(2)}) collective-permute-start(bf16[392,384]{1,0:T(8,128)(2,1)} %get-tuple-element.116.refs_1_), channel_id=1, source_target_pairs={{0,1},{1,0},{2,3},{3,2},{4,5},{5,4},{6,7},{7,6},{8,9},{9,8},{10,11... | collective-permute-start | bytes 903176 | tf_op jit(solution)/shard_map/ppermute | solution.py:661
  73.3 16.8 %collective-permute-start.16 = (bf16[392,384]{1,0:T(8,128)(2,1)}, bf16[392,384]{1,0:T(8,128)(2,1)}, u32[]{:S(2)}, u32[]{:S(2)}) collective-permute-start(bf16[392,384]{1,0:T(8,128)(2,1)} %get-tuple-element.117.refs_2_), channel_id=1, source_target_pairs={{0,1},{1,0},{2,3},{3,2},{4,5},{5,4},{6,7},{7,6},{8,9},{9,8},{10,11... | collective-permute-start | bytes 903176 | tf_op jit(solution)/shard_map/ppermute | solution.py:661
  73.5 18.2 %collective-permute-start.17 = (bf16[392,384]{1,0:T(8,128)(2,1)}, bf16[392,384]{1,0:T(8,128)(2,1)}, u32[]{:S(2)}, u32[]{:S(2)}) collective-permute-start(bf16[392,384]{1,0:T(8,128)(2,1)} %get-tuple-element.118.refs_3_), channel_id=1, source_target_pairs={{0,1},{1,0},{2,3},{3,2},{4,5},{5,4},{6,7},{7,6},{8,9},{9,8},{10,11... | collective-permute-start | bytes 903176 | tf_op jit(solution)/shard_map/ppermute | solution.py:661
  74.1 7.5 %copy-start = (bf16[8,3,24,768]{3,2,1,0:T(8,128)(2,1)S(1)}, bf16[8,3,24,768]{3,2,1,0:T(8,128)(2,1)}, u32[]{:S(2)}) copy-start(bf16[8,3,24,768]{3,2,1,0:T(8,128)(2,1)} %get-tuple-element.151.refs_0_) | copy-start | bytes 2654212
  74.1 7.5 %copy-start.1 = (bf16[8,3,24,768]{3,2,1,0:T(8,128)(2,1)S(1)}, bf16[8,3,24,768]{3,2,1,0:T(8,128)(2,1)}, u32[]{:S(2)}) copy-start(bf16[8,3,24,768]{3,2,1,0:T(8,128)(2,1)} %get-tuple-element.129.refs_2_.refs_3_.refs_4_.refs_5_) | copy-start | bytes 2654212
  74.1 7.5 %copy-start.2 = (bf16[8,3,24,768]{3,2,1,0:T(8,128)(2,1)S(1)}, bf16[8,3,24,768]{3,2,1,0:T(8,128)(2,1)}, u32[]{:S(2)}) copy-start(bf16[8,3,24,768]{3,2,1,0:T(8,128)(2,1)} %get-tuple-element.131.refs_4_.refs_6_.refs_8_.refs_10_) | copy-start | bytes 2654212
  81.4 2.6 %collective-permute-start.14 = (bf16[1,208,384]{2,1,0:T(8,128)(2,1)}, bf16[1,208,384]{2,1,0:T(8,128)(2,1)S(1)}, u32[]{:S(2)}, u32[]{:S(2)}) collective-permute-start(bf16[1,208,384]{2,1,0:T(8,128)(2,1)} %get-tuple-element.135), channel_id=1, source_target_pairs={{0,1},{1,0},{2,3},{3,2},{4,5},{5,4},{6,7},{7,6},{8,9},{9,8},{10,11... | collective-permute-start | bytes 479240 | tf_op jit(solution)/shard_map/ppermute | solution.py:661
  81.6 2.4 %copy-start.5 = (bf16[1,208,384]{2,1,0:T(8,128)(2,1)S(1)}, bf16[1,208,384]{2,1,0:T(8,128)(2,1)}, u32[]{:S(2)}) copy-start(bf16[1,208,384]{2,1,0:T(8,128)(2,1)} %get-tuple-element.134.refs_0_) | copy-start | bytes 479236
  84.7 13.5 %collective-permute-start.18 = (bf16[1,208,384]{2,1,0:T(8,128)(2,1)}, bf16[1,208,384]{2,1,0:T(8,128)(2,1)}, u32[]{:S(2)}, u32[]{:S(2)}) collective-permute-start(bf16[1,208,384]{2,1,0:T(8,128)(2,1)} %combine.13.refs_0_), channel_id=1, source_target_pairs={{0,16},{2,18},{4,20},{6,22},{8,24},{10,26},{12,28},{14,30},{16,0},... | collective-permute-start | bytes 479240 | tf_op jit(solution)/shard_map/ppermute | solution.py:665
  87.2 15.2 %collective-permute-start.20 = (bf16[4,3,24,768]{3,2,1,0:T(8,128)(2,1)}, bf16[4,3,24,768]{3,2,1,0:T(8,128)(2,1)S(1)}, u32[]{:S(2)}, u32[]{:S(2)}) collective-permute-start(bf16[4,3,24,768]{3,2,1,0:T(8,128)(2,1)} %get-tuple-element.143), channel_id=1, source_target_pairs={{0,8},{2,10},{4,12},{6,14},{8,0},{10,2},{12,4},{14,6},{16,24},{18,... | collective-permute-start | bytes 1327112 | tf_op jit(solution)/shard_map/ppermute | solution.py:665
  88.6 14.7 %collective-permute-start.21 = (bf16[4,3,24,768]{3,2,1,0:T(8,128)(2,1)}, bf16[4,3,24,768]{3,2,1,0:T(8,128)(2,1)}, u32[]{:S(2)}, u32[]{:S(2)}) collective-permute-start(bf16[4,3,24,768]{3,2,1,0:T(8,128)(2,1)} %get-tuple-element.144), channel_id=1, source_target_pairs={{0,2},{2,0},{4,6},{6,4},{8,10},{10,8},{12,14},{14,12},{16,18},{18,... | collective-permute-start | bytes 1327112 | tf_op jit(solution)/shard_map/ppermute | solution.py:665
  90.1 13.4 %collective-permute-start.19 = (bf16[4,3,24,768]{3,2,1,0:T(8,128)(2,1)}, bf16[4,3,24,768]{3,2,1,0:T(8,128)(2,1)}, u32[]{:S(2)}, u32[]{:S(2)}) collective-permute-start(bf16[4,3,24,768]{3,2,1,0:T(8,128)(2,1)} %get-tuple-element.133), channel_id=1, source_target_pairs={{0,4},{2,6},{4,0},{6,2},{8,12},{10,14},{12,8},{14,10},{16,20},{18,... | collective-permute-start | bytes 1327112 | tf_op jit(solution)/shard_map/ppermute | solution.py:665
  97.6 15.3 %collective-permute-start.23 = (bf16[8,24,1152]{2,1,0:T(8,128)(2,1)}, bf16[8,24,1152]{2,1,0:T(8,128)(2,1)S(1)}, u32[]{:S(2)}, u32[]{:S(2)}) collective-permute-start(bf16[8,24,1152]{2,1,0:T(8,128)(2,1)} %get-tuple-element.148), channel_id=1, source_target_pairs={{0,4},{2,6},{4,0},{6,2},{8,12},{10,14},{12,8},{14,10},{16,20},{18,... | collective-permute-start | bytes 1327112 | tf_op jit(solution)/shard_map/ppermute | solution.py:665
  98.2 15.2 %collective-permute-start.22 = (bf16[8,24,1152]{2,1,0:T(8,128)(2,1)}, bf16[8,24,1152]{2,1,0:T(8,128)(2,1)S(1)}, u32[]{:S(2)}, u32[]{:S(2)}) collective-permute-start(bf16[8,24,1152]{2,1,0:T(8,128)(2,1)} %get-tuple-element.139), channel_id=1, source_target_pairs={{0,2},{2,0},{4,6},{6,4},{8,10},{10,8},{12,14},{14,12},{16,18},{18,... | collective-permute-start | bytes 1327112 | tf_op jit(solution)/shard_map/ppermute | solution.py:665
  99.7 13.6 %copy-start.3 = (bf16[8,24,1152]{2,1,0:T(8,128)(2,1)S(1)}, bf16[8,24,1152]{2,1,0:T(8,128)(2,1)}, u32[]{:S(2)}) copy-start(bf16[8,24,1152]{2,1,0:T(8,128)(2,1)} %get-tuple-element.157.refs_0_) | copy-start | bytes 1327108
  99.7 13.6 %copy-start.4 = (bf16[8,24,1152]{2,1,0:T(8,128)(2,1)S(1)}, bf16[8,24,1152]{2,1,0:T(8,128)(2,1)}, u32[]{:S(2)}) copy-start(bf16[8,24,1152]{2,1,0:T(8,128)(2,1)} %get-tuple-element.147.refs_2_.refs_3_.refs_4_.refs_5_) | copy-start | bytes 1327108
  102.4 11.8 %collective-permute-start.24 = (bf16[1,208,384]{2,1,0:T(8,128)(2,1)S(1)}, bf16[1,208,384]{2,1,0:T(8,128)(2,1)S(1)}, u32[]{:S(2)}, u32[]{:S(2)}) collective-permute-start(bf16[1,208,384]{2,1,0:T(8,128)(2,1)S(1)} %combine.14.refs_0_), channel_id=1, source_target_pairs={{0,8},{2,10},{4,12},{6,14},{8,0},{10,2},{12,4},{14,6},{16,24},{18,... | collective-permute-start | bytes 479240 | tf_op jit(solution)/shard_map/ppermute | solution.py:665
  105.1 11.2 %collective-permute-start.26 = (bf16[2,3,24,768]{3,2,1,0:T(8,128)(2,1)S(1)}, bf16[2,3,24,768]{3,2,1,0:T(8,128)(2,1)S(1)}, u32[]{:S(2)}, u32[]{:S(2)}) collective-permute-start(bf16[2,3,24,768]{3,2,1,0:T(8,128)(2,1)S(1)} %get-tuple-element.152), channel_id=1, source_target_pairs={{0,2},{2,0},{4,6},{6,4},{8,10},{10,8},{12,14},{14,12},{16,18},{18,... | collective-permute-start | bytes 663560 | tf_op jit(solution)/shard_map/ppermute | solution.py:665
  105.9 11.8 %collective-permute-start.27 = (bf16[2,3,24,768]{3,2,1,0:T(8,128)(2,1)S(1)}, bf16[2,3,24,768]{3,2,1,0:T(8,128)(2,1)S(1)}, u32[]{:S(2)}, u32[]{:S(2)}) collective-permute-start(bf16[2,3,24,768]{3,2,1,0:T(8,128)(2,1)S(1)} %get-tuple-element.153), channel_id=1, source_target_pairs={{0,4},{2,6},{4,0},{6,2},{8,12},{10,14},{12,8},{14,10},{16,20},{18,... | collective-permute-start | bytes 663560 | tf_op jit(solution)/shard_map/ppermute | solution.py:665
  112.9 5.9 %collective-permute-start.25 = (bf16[2,3,24,768]{3,2,1,0:T(8,128)(2,1)S(1)}, bf16[2,3,24,768]{3,2,1,0:T(8,128)(2,1)S(1)}, u32[]{:S(2)}, u32[]{:S(2)}) collective-permute-start(bf16[2,3,24,768]{3,2,1,0:T(8,128)(2,1)S(1)} %get-tuple-element.145), channel_id=1, source_target_pairs={{0,8},{2,10},{4,12},{6,14},{8,0},{10,2},{12,4},{14,6},{16,24},{18,... | collective-permute-start | bytes 663560 | tf_op jit(solution)/shard_map/ppermute | solution.py:665
  113.5 8.5 %collective-permute-start.29 = (bf16[4,24,1152]{2,1,0:T(8,128)(2,1)S(1)}, bf16[4,24,1152]{2,1,0:T(8,128)(2,1)S(1)}, u32[]{:S(2)}, u32[]{:S(2)}) collective-permute-start(bf16[4,24,1152]{2,1,0:T(8,128)(2,1)S(1)} %get-tuple-element.155), channel_id=1, source_target_pairs={{0,2},{2,0},{4,6},{6,4},{8,10},{10,8},{12,14},{14,12},{16,18},{18,... | collective-permute-start | bytes 663560 | tf_op jit(solution)/shard_map/ppermute | solution.py:665
  114.3 8.0 %collective-permute-start.28 = (bf16[4,24,1152]{2,1,0:T(8,128)(2,1)S(1)}, bf16[4,24,1152]{2,1,0:T(8,128)(2,1)S(1)}, u32[]{:S(2)}, u32[]{:S(2)}) collective-permute-start(bf16[4,24,1152]{2,1,0:T(8,128)(2,1)S(1)} %get-tuple-element.149), channel_id=1, source_target_pairs={{0,4},{2,6},{4,0},{6,2},{8,12},{10,14},{12,8},{14,10},{16,20},{18,... | collective-permute-start | bytes 663560 | tf_op jit(solution)/shard_map/ppermute | solution.py:665
  120.1 15.6 %collective-permute-start.36 = (bf16[3,3,24,768]{3,2,1,0:T(8,128)(2,1)S(1)}, bf16[3,3,24,768]{3,2,1,0:T(8,128)(2,1)S(1)}, u32[]{:S(2)}, u32[]{:S(2)}) collective-permute-start(bf16[3,3,24,768]{3,2,1,0:T(8,128)(2,1)S(1)} %combine.18), channel_id=1, source_target_pairs={{0,16},{2,18},{4,20},{6,22},{8,24},{10,26},{12,28},{14,30},{16,0},... | collective-permute-start | bytes 995336 | tf_op jit(solution)/shard_map/ppermute | solution.py:665
  120.5 5.3 %collective-permute-start.30 = (bf16[1,208,384]{2,1,0:T(8,128)(2,1)S(1)}, bf16[1,208,384]{2,1,0:T(8,128)(2,1)S(1)}, u32[]{:S(2)}, u32[]{:S(2)}) collective-permute-start(bf16[1,208,384]{2,1,0:T(8,128)(2,1)S(1)} %combine.17.refs_0_), channel_id=1, source_target_pairs={{0,4},{2,6},{4,0},{6,2},{8,12},{10,14},{12,8},{14,10},{16,20},{18,... | collective-permute-start | bytes 479240 | tf_op jit(solution)/shard_map/ppermute | solution.py:665
  122.4 7.6 %collective-permute-start.31 = (bf16[4,24,1152]{2,1,0:T(8,128)(2,1)S(1)}, bf16[4,24,1152]{2,1,0:T(8,128)(2,1)S(1)}, u32[]{:S(2)}, u32[]{:S(2)}) collective-permute-start(bf16[4,24,1152]{2,1,0:T(8,128)(2,1)S(1)} %combine.19), channel_id=1, source_target_pairs={{0,8},{2,10},{4,12},{6,14},{8,0},{10,2},{12,4},{14,6},{16,24},{18,... | collective-permute-start | bytes 663560 | tf_op jit(solution)/shard_map/ppermute | solution.py:665
  125.8 11.9 %collective-permute-start.32 = (bf16[1,208,384]{2,1,0:T(8,128)(2,1)S(1)}, bf16[1,208,384]{2,1,0:T(8,128)(2,1)S(1)}, u32[]{:S(2)}, u32[]{:S(2)}) collective-permute-start(bf16[1,208,384]{2,1,0:T(8,128)(2,1)S(1)} %combine.20.refs_0_), channel_id=1, source_target_pairs={{0,2},{2,0},{4,6},{6,4},{8,10},{10,8},{12,14},{14,12},{16,18},{18,... | collective-permute-start | bytes 479240 | tf_op jit(solution)/shard_map/ppermute | solution.py:665
  130.0 8.4 %collective-permute-start.34 = (bf16[2,24,1152]{2,1,0:T(8,128)(2,1)S(1)}, bf16[2,24,1152]{2,1,0:T(8,128)(2,1)S(1)}, u32[]{:S(2)}, u32[]{:S(2)}) collective-permute-start(bf16[2,24,1152]{2,1,0:T(8,128)(2,1)S(1)} %combine.21), channel_id=1, source_target_pairs={{0,16},{2,18},{4,20},{6,22},{8,24},{10,26},{12,28},{14,30},{16,0},... | collective-permute-start | bytes 331784 | tf_op jit(solution)/shard_map/ppermute | solution.py:665
  137.8 3.4 %collective-permute-start.37 = (f32[3,24,768]{2,1,0:T(8,128)S(1)}, f32[3,24,768]{2,1,0:T(8,128)S(1)}, u32[]{:S(2)}, u32[]{:S(2)}) collective-permute-start(f32[3,24,768]{2,1,0:T(8,128)S(1)} %get-tuple-element.167), channel_id=1, source_target_pairs={{0,1},{1,0},{2,3},{3,2},{4,5},{5,4},{6,7},{7,6},{8,9},{9,8},{10,11... | collective-permute-start | bytes 663560 | tf_op jit(solution)/shard_map/ppermute | solution.py:661
  137.8 1.7 %collective-permute-start.33 = (bf16[1,208,384]{2,1,0:T(8,128)(2,1)S(1)}, bf16[1,208,384]{2,1,0:T(8,128)(2,1)S(1)}, u32[]{:S(2)}, u32[]{:S(2)}) collective-permute-start(bf16[1,208,384]{2,1,0:T(8,128)(2,1)S(1)} %combine.22.mine_ref), channel_id=1, source_target_pairs={{0,1},{1,0},{2,3},{3,2},{4,5},{5,4},{6,7},{7,6},{8,9},{9,8},{10,11... | collective-permute-start | bytes 479240 | tf_op jit(solution)/shard_map/ppermute | solution.py:661
  138.5 1.9 %collective-permute-start.35 = (f32[24,1152]{1,0:T(8,128)S(1)}, f32[24,1152]{1,0:T(8,128)S(1)}, u32[]{:S(2)}, u32[]{:S(2)}) collective-permute-start(f32[24,1152]{1,0:T(8,128)S(1)} %get-tuple-element.163), channel_id=1, source_target_pairs={{0,1},{1,0},{2,3},{3,2},{4,5},{5,4},{6,7},{7,6},{8,9},{9,8},{10,11... | collective-permute-start | bytes 331784 | tf_op jit(solution)/shard_map/ppermute | solution.py:661
  (5 other events, 3.6 us)
where the time goes:
time: 142 us
  Pallas kernels  80.7 us (57%)
  starting transfers between devices  30.8 us (22%)
  waiting for transfers between devices  26.7 us (19%)
  local copies, waits for them, and re-layouts  2.76 us (2%)
    ppermute x20, starting transfers between devices, across(): return lax.ppermute(v, 'dp', [(i, i ^ flip) for i in range(ndp)])  26.1 us
    pallas_call x1, Pallas kernels, front(): pl.pallas_call(functools.partial(front_kernel, hidden // plan.groups // 2...  25.8 us
    ppermute x20, waiting for transfers between devices, across(): return lax.ppermute(v, 'dp', [(i, i ^ flip) for i in range(ndp)])  20.9 us
    pallas_call x1, Pallas kernels, attend_back(): pl.pallas_call(body, grid_spec=pltpu.PrefetchScalarGridSpec(num_scalar_pr...  14.6 us
    pallas_call x1, Pallas kernels, feed_weights(): pl.pallas_call(functools.partial(feed_weights_kernel, plan), grid_spec=pl...  10.6 us
    pallas_call x12, Pallas kernels, combine(): pl.pallas_call(functools.partial(combine_kernel, counts), grid=(1,), in_s...  8.47 us
    pallas_call x1, Pallas kernels, front_back(): pl.pallas_call(functools.partial(front_back_kernel, places), grid_spec=pl...  7.25 us
    pallas_call x1, Pallas kernels, attend_weights(): pl.pallas_call(functools.partial(attend_weights_kernel, plan), grid_spec=...  5.93 us
  transfers between devices with their start and end apart: 38, of which 16 were waited for; matrix products, arithmetic and copies ran while one was open for 0% of the time, Pallas kernels for 49%

commit v1 on v0

--- a/solution.py
+++ b/solution.py
@@ -348,7 +348,7 @@
         self.rest = ndp // self.groups
         wanted = {"feed": ((0, 1, 2, 3), (1, 2, 0, 3), (2, 0, 1, 3)), "attend": ((0, 1, 2, 3), (1, 0, 2, 3))}
         self.orders = {k: [[b for b in o if b < self.bits] for o in v] for k, v in wanted.items()}
-        self.small = [b for b in (3, 2, 1, 0) if b < self.bits]
+        self.small = [b for b in (2, 3, 1, 0) if b < self.bits]
 
     def place(self, name, piece, p):
         code = 0
@@ -441,12 +441,16 @@
         [(q_hbm, q_ref), (k_hbm, k_ref), (v_hbm, v_ref), (ga_hbm, ga_ref)], sem
     )
     heads = p_ref.shape[0]
-    per = 4
+    per = heads // 2
     probs_in = started([(p_hbm.at[k : k + per], p_ref.at[k : k + per]) for k in range(0, heads, per)], p_sem)
-    done(loads + probs_in)
+    done(loads + probs_in[:1])
     pairs = heads // 4
 
     def one_side(side, carry):
+        @pl.when(side == 1)
+        def _():
+            probs_in[1].wait()
+
         for pair in range(pairs):
             lanes = pl.ds(pl.multiple_of(side * cols + pair * 128, 128), 128)
             at = slice(pair * 128, pair * 128 + 128)
@@ -516,7 +520,7 @@
                 pltpu.VMEM((2, 3, half, cols), BF),
                 pltpu.VMEM((2, 2, halo, cols), BF),
                 pltpu.SemaphoreType.DMA((4,)),
-                pltpu.SemaphoreType.DMA((probs.shape[0] // 4,)),
+                pltpu.SemaphoreType.DMA((2,)),
                 pltpu.SemaphoreType.DMA((6,)),
             ],
         ),
@@ -605,15 +609,17 @@
     blk = blk_ref[0]
     start = pl.multiple_of((1 - blk) * (half - halo), 16)
     lanes = [[pl.multiple_of(which * width + core * cols, 128) for core in (blk, 1 - blk)] for which in range(3)]
-    pairs = [(sources[0].at[k], gj_ref.at[:, pl.ds(lanes[k][0], cols)]) for k in range(3)]
+    pairs = [(sources[4 + 2], w_ref)]
+    pairs += [(sources[0].at[k], gj_ref.at[:, pl.ds(lanes[k][0], cols)]) for k in range(3)]
     pairs += [(sources[1 + k], gj_ref.at[:, pl.ds(lanes[k][1], cols)]) for k in range(3)]
-    pairs += list(zip(sources[4:], (ho_ref, hl_ref, w_ref, h0_ref, gh_ref, g1_ref, pos_ref, sums_ref, b1_ref)))
+    pairs += [(sources[4], ho_ref), (sources[5], hl_ref)]
+    pairs += list(zip(sources[7:], (h0_ref, gh_ref, g1_ref, pos_ref, sums_ref, b1_ref)))
     loads = started(pairs, sem)
-    done(loads[:9])
+    done(loads[1:9])
     for which in range(2):
         add_rows(gj_ref, start, lanes[1 + which][0], cols, ho_ref[which])
         add_rows(gj_ref, start, lanes[1 + which][1], cols, hl_ref[which])
-    done(loads[9:])
+    done(loads[:1] + loads[9:])
     total = dot_nt(gj_ref[...], w_ref[...])
     small_ref[places + 2 : places + 3, :] = column_sum(gj_ref[:, :width].astype(F32))
     small_ref[places + 3 : places + 4, :] = column_sum(gj_ref[:, 2 * width :].astype(F32))
@@ -780,10 +786,17 @@
         return self.sent, self.got
 
 
-def split_feed_kernel(blk_ref, value_ref, fc2_ref, mine, other):
-    unit = value_ref.shape[2]
-    units = [value_ref[k // 3, k % 3] for k in range(9)]
-    cols = units[0].shape[1] // 2
+def split_feed_kernel(counts, blk_ref, *refs):
+    fc2_ref, mine, other = refs[-3:]
+    units = []
+    used = 0
+    for terms in counts:
+        total = refs[used][0].astype(F32)
+        for ref in refs[used + 1 : used + terms]:
+            total = total + ref[0].astype(F32)
+        used += terms
+        units += [total[k] for k in range(3)]
+    unit, cols = mine.shape[1], mine.shape[2] // 2
     for k in range(4):
         fc2_ref[k * unit : (k + 1) * unit, :] = units[k]
     low_core = blk_ref[0] == 0
@@ -798,19 +811,27 @@
     other[2, :, cols:] = jnp.zeros_like(low)
 
 
-def split_feed(blk, value):
-    _, _, unit, width = value.shape
+def split_feed(blk, pieces):
+    arrays, where = pieces.collect()
+    block = (1,) + arrays[0].shape[1:]
+    unit, width = block[2:]
     shapes = [(4 * unit, width), (3, unit, width), (3, unit, width)]
-    return pl.pallas_call(
-        split_feed_kernel,
+    places = [(index, at) for terms in where for index, at in terms]
+    return pl.pallas_call(
+        functools.partial(split_feed_kernel, [len(terms) for terms in where]),
         grid_spec=pltpu.PrefetchScalarGridSpec(
-            num_scalar_prefetch=1, grid=(1,), in_specs=[whole(value.shape)], out_specs=[whole(v) for v in shapes]
+            num_scalar_prefetch=1,
+            grid=(1,),
+            in_specs=[
+                pl.BlockSpec(block, functools.partial(lambda at, i, b: (at, 0, 0, 0), at)) for _, at in places
+            ],
+            out_specs=[whole(v) for v in shapes],
         ),
         out_shape=[jax.ShapeDtypeStruct(v, F32) for v in shapes],
         compiler_params=params(24),
         cost_estimate=cost(1, 1),
         name="split_feed",
-    )(blk, value)
+    )(blk, *[arrays[index] for index, _ in places])
 
 
 def join_feed_kernel(blk_ref, mine_ref, got_ref, fc1_ref, out_ref):
@@ -934,6 +955,33 @@
         cost_estimate=cost(1, 1),
         name="join_small",
     )(blk, mine, got)
+
+
+def join(blk, attend_mine, attend_got, feed_mine, feed_got, mine, got, places, hidden):
+    unit, cols = attend_mine.shape
+    rows, width = mine.shape[1], feed_mine.shape[2]
+    shapes = [(unit, 2 * cols), (unit, 4 * width), (unit, width), (places, width)] + [(width,)] * 8 + [(hidden,)]
+    operands = (attend_mine, attend_got, feed_mine, feed_got, mine, got)
+
+    def kernel(blk_ref, *refs):
+        join_attend_kernel(blk_ref, refs[0], refs[1], refs[6])
+        join_feed_kernel(blk_ref, refs[2], refs[3], refs[7], refs[8])
+        join_small_kernel(blk_ref, refs[4], refs[5], *refs[9:])
+
+    return pl.pallas_call(
+        kernel,
+        grid_spec=pltpu.PrefetchScalarGridSpec(
+            num_scalar_prefetch=1,
+            grid=(1,),
+            in_specs=[whole(v.shape) for v in operands],
+            out_specs=[whole(v) for v in shapes],
+            scratch_shapes=[pltpu.VMEM((rows, width), F32)],
+        ),
+        out_shape=[jax.ShapeDtypeStruct(v, F32) for v in shapes],
+        compiler_params=params(24),
+        cost_estimate=cost(1, 1),
+        name="join",
+    )(blk, *operands)
 
 
 def behind(values, *others):
@@ -998,15 +1046,15 @@
         item.step(before)
         before = item.sent
     unit = width // plan.groups // 2
-    value = feed_sums.totals()
     attend_mine, attend_sent = split_attend(blk1, attend_sums)
     if plan.rest == 1:
-        fc2_grad, feed_mine, feed_sent = split_feed(blk1, value)
+        fc2_grad, feed_mine, feed_sent = split_feed(blk1, feed_sums)
         feed_got = swap(feed_sent)
-        qkv_grad = join_attend(blk1, attend_mine, swap(attend_sent))
-        fc1_grad, out_grad = join_feed(blk1, feed_mine, feed_got)
+        qkv_grad, fc1_grad, out_grad, table, *vec, b1_all = join(
+            blk1, attend_mine, swap(attend_sent), feed_mine, feed_got, *small.both(), places, hidden
+        )
     else:
-        units = value.reshape(9, unit, width)
+        units = feed_sums.totals().reshape(9, unit, width)
         fc2_grad = rest_of(plan, lax.all_gather(units[:4].reshape(-1, width), "blk", axis=0, tiled=True), blk)
         rows = jnp.concatenate([units[5:7].reshape(-1, width), units[7:].reshape(-1, width)], 1)
         fc1_grad = rest_of(plan, lax.all_gather(rows, "blk", axis=1, tiled=True), blk)
@@ -1015,7 +1063,7 @@
         rows = jnp.where(blk == 0, jnp.stack([attend_mine, attend_sent]), jnp.stack([attend_sent, attend_mine]))
         rows = rows.reshape(2 * unit, 3, width // 2)
         qkv_grad = rest_of(plan, lax.all_gather(rows, "blk", axis=2, tiled=True).reshape(2 * unit, -1), blk)
-    table, *vec, b1_all = join_small(blk1, *small.both(), places, hidden)
+        table, *vec, b1_all = join_small(blk1, *small.both(), places, hidden)
     return (
         result[None], grad_x[None], table, vec[0], vec[1], qkv_grad, vec[2], vec[3], out_grad,
         vec[6], vec[4], vec[5], fc1_grad, b1_all, fc2_grad, vec[7],

time: 142 us -> 139 us (0.979)
  waiting for transfers between devices: 26.7 us -> 22.2 us
  starting transfers between devices: 30.8 us -> 35 us
  Pallas kernels: 80.7 us -> 78.2 us
    ppermute x20, waiting for transfers between devices: 20.9 us -> 15.9 us  [across(): return lax.ppermute(v, 'dp', [(i, i ^ flip) for i in range(ndp)])]
    ppermute x20, starting transfers between devices: 26.1 us -> 30.3 us  [across(): return lax.ppermute(v, 'dp', [(i, i ^ flip) for i in range(ndp)])]
    pallas_call x12 -> x11, Pallas kernels: 8.47 us -> 7.2 us  [combine(): pl.pallas_call(functools.partial(combine_kernel, counts), grid=(1,), in_s...]
    pallas_call x4 -> x2, Pallas kernels: 3.16 us -> 2.92 us  [the longest x1 1.86 us: split_feed(): pl.pallas_call(functools.partial(split_feed_kernel, [len(terms) for terms...]
  transfers between devices with their start and end apart: 38 -> 38, of which waited for: 16 -> 15; matrix products, arithmetic and copies ran while one was open for 0% -> 0% of each run, Pallas kernels for 49% -> 48%
where the time goes in v1:
time: 139 us
  Pallas kernels  78.2 us (56%)
  starting transfers between devices  35 us (25%)
  waiting for transfers between devices  22.2 us (16%)
  local copies, waits for them, and re-layouts  2.52 us (2%)
    ppermute x20, starting transfers between devices, across(): return lax.ppermute(v, 'dp', [(i, i ^ flip) for i in range(ndp)])  30.3 us
    pallas_call x1, Pallas kernels, front(): pl.pallas_call(functools.partial(front_kernel, hidden // plan.groups // 2...  25.8 us
    ppermute x20, waiting for transfers between devices, across(): return lax.ppermute(v, 'dp', [(i, i ^ flip) for i in range(ndp)])  15.9 us
    pallas_call x1, Pallas kernels, attend_back(): pl.pallas_call(body, grid_spec=pltpu.PrefetchScalarGridSpec(num_scalar_pr...  13.6 us
    pallas_call x1, Pallas kernels, feed_weights(): pl.pallas_call(functools.partial(feed_weights_kernel, plan), grid_spec=pl...  10.6 us
    pallas_call x1, Pallas kernels, front_back(): pl.pallas_call(functools.partial(front_back_kernel, places), grid_spec=pl...  7.27 us
    pallas_call x11, Pallas kernels, combine(): pl.pallas_call(functools.partial(combine_kernel, counts), grid=(1,), in_s...  7.2 us
    ppermute x18, waiting for transfers between devices, swap(): return lax.ppermute(v, 'blk', [(0, 1), (1, 0)])  6.26 us
  transfers between devices with their start and end apart: 38, of which 15 were waited for; matrix products, arithmetic and copies ran while one was open for 0% of the time, Pallas kernels for 48%

profile of v1, /device:TPU:0, one launch (start us, length us, event | category | flops | bytes accessed | tf_op | source)
XLA Modules:
  0.0 138.9 jit_solution(6384395378800433776)
XLA Ops:
  0.6 0.5 collective-permute-start
  1.8 1.3 collective-permute-done.1.refs_3_
  3.1 0.6 copy-done.13
  3.9 25.8 %front.1 = (f32[392,768]{1,0:T(8,128)}, bf16[392,768]{1,0:T(8,128)(2,1)}, bf16[392,768]{1,0:T(8,128)(2,1)}, bf16[392,768]{1,0:T(8,128)(2,1)}, bf16[640,768]{1,0:...) custom-call(s32[1]{0:T(128)} %bitcast.blk_ref, ...), custom_call_target="tpu_custom_call" | custom-call | flops 10481565696 | bytes 18874368 | tf_op jit(solution)/shard_map/front/pallas_call | solution.py:267
  30.8 4.7 %mid.1 = (f32[392,768]{1,0:T(8,128)}, bf16[392,768]{1,0:T(8,128)(2,1)}, bf16[392,768]{1,0:T(8,128)(2,1)}, f32[4,768]{1,0:T(4,128)}) custom-call(f32[392,768]{1,0:T(8,128)} %get-tuple-element.100.gn_hbm, f32[392,768]{1,0:T(8,128)} %get-tuple-element.101.h1_hbm, bf16[392,768]{1,0:T(8,128)(2,1)} %bitcast.8, bf16[768,768]{1,0:T(8,128)(2,1)} %wo_hbm.1, f32[768]{0:T(1024)} %g2_hbm.1), custom_call_target="tpu_custom_call" | custom-call | flops 1 | bytes 1 | tf_op jit(solution)/shard_map/mid/pallas_call | solution.py:330
  36.5 1.4 collective-permute-done.8.refs_11_
  37.9 0.8 copy-done.10
  39.5 10.6 %feed_weights.1 = (bf16[8,3,24,768]{3,2,1,0:T(8,128)(2,1)}, bf16[8,3,24,768]{3,2,1,0:T(8,128)(2,1)}, bf16[8,3,24,768]{3,2,1,0:T(8,128)(2,1)}, bf16[8,3,24,768]{3...) custom-call(s32[1]{0:T(128)} %bitcast.4.own_ref, s32[1]{0:T(128)} %bitcast.blk_ref, ...), custom_call_target="tpu_custom_call" | custom-call | flops 1 | bytes 1 | tf_op jit(solution)/shard_map/feed_weights/pallas_call | solution.py:416
  50.2 3.0 %collective-permute-start.12 = (bf16[8,3,24,768]{3,2,1,0:T(8,128)(2,1)}, bf16[8,3,24,768]{3,2,1,0:T(8,128)(2,1)S(1)}, u32[]{:S(2)}, u32[]{:S(2)}) collective-permute-start(bf16[8,3,24,768]{3,2,1,0:T(8,128)(2,1)} %get-tuple-element.132), channel_id=1, source_target_pairs={{0,4},{2,6},{4,0},{6,2},{8,12},{10,14},{12,8},{14,10},{16,20},{18,... | collective-permute-start | bytes 2654216 | tf_op jit(solution)/shard_map/ppermute | solution.py:671
  53.1 1.6 %collective-permute-start.13 = (bf16[8,3,24,768]{3,2,1,0:T(8,128)(2,1)}, bf16[8,3,24,768]{3,2,1,0:T(8,128)(2,1)}, u32[]{:S(2)}, u32[]{:S(2)}) collective-permute-start(bf16[8,3,24,768]{3,2,1,0:T(8,128)(2,1)} %get-tuple-element.134), channel_id=1, source_target_pairs={{0,8},{2,10},{4,12},{6,14},{8,0},{10,2},{12,4},{14,6},{16,24},{18,... | collective-permute-start | bytes 2654216 | tf_op jit(solution)/shard_map/ppermute | solution.py:671
  54.7 1.5 %collective-permute-start.11 = (bf16[8,3,24,768]{3,2,1,0:T(8,128)(2,1)}, bf16[8,3,24,768]{3,2,1,0:T(8,128)(2,1)}, u32[]{:S(2)}, u32[]{:S(2)}) collective-permute-start(bf16[8,3,24,768]{3,2,1,0:T(8,128)(2,1)} %get-tuple-element.111), channel_id=1, source_target_pairs={{0,2},{2,0},{4,6},{6,4},{8,10},{10,8},{12,14},{14,12},{16,18},{18,... | collective-permute-start | bytes 2654216 | tf_op jit(solution)/shard_map/ppermute | solution.py:671
  56.2 13.6 %attend_back.1 = (bf16[2,248,384]{2,1,0:T(8,128)(2,1)}, bf16[2,248,384]{2,1,0:T(8,128)(2,1)}, bf16[3,392,384]{2,1,0:T(8,128)(2,1)}, bf16[392,384]{1,0:T(8,128)(2...) custom-call(s32[1]{0:T(128)} %bitcast.blk_ref, bf16[392,768]{1,0:T(8,128)(2,1)} %get-tuple-element.112.refs_0_, ...), custom_call_target="tpu_custom_call" | custom-call | flops 1 | bytes 1 | tf_op jit(solution)/shard_map/attend_back/pallas_call | solution.py:507
  69.9 0.5 collective-permute-start.10
  70.4 1.4 %collective-permute-done.9.refs_4_ = bf16[2,248,384]{2,1,0:T(8,128)(2,1)S(1)} collective-permute-done((bf16[2,248,384]{2,1,0:T(8,128)(2,1)}, bf16[2,248,384]{2,1,0:T(8,128)(2,1)S(1)}, u32[]{:S(2)}, u32[]{:S(2)}) %collective-permute-start.9) | collective-permute-done | bytes 380960 | tf_op jit(solution)/shard_map/ppermute | solution.py:667
  72.5 0.8 collective-permute-done.12.refs_3_.refs_4_.refs_5_.refs_6_
  73.3 7.3 %front_back.1 = (bf16[392,768]{1,0:T(8,128)(2,1)}, bf16[1,208,384]{2,1,0:T(8,128)(2,1)}, bf16[1,208,384]{2,1,0:T(8,128)(2,1)}) custom-call(s32[1]{0:T(128)} %bitcast.blk_ref, bf16[3,392,384]{2,1,0:T(8,128)(2,1)} %get-tuple-element.116.refs_0_.refs_2_, bf16[392,384]{1,0:T(8,128)(2,1)} %get-tuple-element.117.refs_1_, ...), custom_call_target="tpu_custom_call" | custom-call | flops 1 | bytes 1 | tf_op jit(solution)/shard_map/front_back/pallas_call | solution.py:644
  80.6 0.6 collective-permute-start.14
  81.2 2.4 %combine.11 = (bf16[4,3,24,768]{3,2,1,0:T(8,128)(2,1)}, bf16[4,3,24,768]{3,2,1,0:T(8,128)(2,1)}, bf16[4,3,24,768]{3,2,1,0:T(8,128)(2,1)}) custom-call(bf16[8,3,24,768]{3,2,1,0:T(8,128)(2,1)S(1)} %copy-done, bf16[8,3,24,768]{3,2,1,0:T(8,128)(2,1)} %collective-permute-done.11.refs_1_, bf16[8,3,24,768]{3,2,1,0:T(8,128)(2,1)S(1)} %copy-done.1, ...), custom_call_target="tpu_custom_call" | custom-call | flops 1 | bytes 1 | tf_op jit(solution)/shard_map/combine/pallas_call | solution.py:709
  83.6 0.7 combine.12.refs_0_
  84.3 1.8 %collective-permute-start.19 = (bf16[1,208,384]{2,1,0:T(8,128)(2,1)}, bf16[1,208,384]{2,1,0:T(8,128)(2,1)}, u32[]{:S(2)}, u32[]{:S(2)}) collective-permute-start(bf16[1,208,384]{2,1,0:T(8,128)(2,1)} %combine.12.refs_0_), channel_id=1, source_target_pairs={{0,8},{2,10},{4,12},{6,14},{8,0},{10,2},{12,4},{14,6},{16,24},{18,... | collective-permute-start | bytes 479240 | tf_op jit(solution)/shard_map/ppermute | solution.py:671
  86.3 1.7 %collective-permute-start.22 = (bf16[4,3,24,768]{3,2,1,0:T(8,128)(2,1)}, bf16[4,3,24,768]{3,2,1,0:T(8,128)(2,1)}, u32[]{:S(2)}, u32[]{:S(2)}) collective-permute-start(bf16[4,3,24,768]{3,2,1,0:T(8,128)(2,1)} %get-tuple-element.145), channel_id=1, source_target_pairs={{0,2},{2,0},{4,6},{6,4},{8,10},{10,8},{12,14},{14,12},{16,18},{18,... | collective-permute-start | bytes 1327112 | tf_op jit(solution)/shard_map/ppermute | solution.py:671
  88.0 1.5 %collective-permute-start.20 = (bf16[4,3,24,768]{3,2,1,0:T(8,128)(2,1)}, bf16[4,3,24,768]{3,2,1,0:T(8,128)(2,1)}, u32[]{:S(2)}, u32[]{:S(2)}) collective-permute-start(bf16[4,3,24,768]{3,2,1,0:T(8,128)(2,1)} %get-tuple-element.135), channel_id=1, source_target_pairs={{0,4},{2,6},{4,0},{6,2},{8,12},{10,14},{12,8},{14,10},{16,20},{18,... | collective-permute-start | bytes 1327112 | tf_op jit(solution)/shard_map/ppermute | solution.py:671
  89.6 5.9 %attend_weights.1 = (bf16[8,24,1152]{2,1,0:T(8,128)(2,1)}, bf16[8,24,1152]{2,1,0:T(8,128)(2,1)}, bf16[8,24,1152]{2,1,0:T(8,128)(2,1)}, bf16[8,24,1152]{2,1,0:T(8,128)(2,1)}) custom-call(s32[1]{0:T(128)} %bitcast.4.own_ref, s32[1]{0:T(128)} %bitcast.blk_ref, bf16[392,768]{1,0:T(8,128)(2,1)} %get-tuple-element.138.refs_0_, ...), custom_call_target="tpu_custom_call" | custom-call | flops 1 | bytes 1 | tf_op jit(solution)/shard_map/attend_weights/pallas_call | solution.py:581
  95.5 0.6 collective-permute-start.23
  96.4 1.0 combine.13.refs_0_
  97.4 2.7 %collective-permute-done.21.refs_5_.refs_6_.refs_7_ = bf16[4,3,24,768]{3,2,1,0:T(8,128)(2,1)S(1)} collective-permute-done((bf16[4,3,24,768]{3,2,1,0:T(8,128)(2,1)}, bf16[4,3,24,768]{3,2,1,0:T(8,128)(2,1)S(1)}, u32[]{:S(2)}, u32[]{:S(2)}) %collective-permute-start.21) | collective-permute-done | bytes 442400 | tf_op jit(solution)/shard_map/ppermute | solution.py:671
  100.1 2.7 %collective-permute-start.25 = (bf16[1,208,384]{2,1,0:T(8,128)(2,1)S(1)}, bf16[1,208,384]{2,1,0:T(8,128)(2,1)S(1)}, u32[]{:S(2)}, u32[]{:S(2)}) collective-permute-start(bf16[1,208,384]{2,1,0:T(8,128)(2,1)S(1)} %combine.13.refs_0_), channel_id=1, source_target_pairs={{0,16},{2,18},{4,20},{6,22},{8,24},{10,26},{12,28},{14,30},{16,0},... | collective-permute-start | bytes 479240 | tf_op jit(solution)/shard_map/ppermute | solution.py:671
  102.8 1.5 %combine.14 = (bf16[2,3,24,768]{3,2,1,0:T(8,128)(2,1)S(1)}, bf16[2,3,24,768]{3,2,1,0:T(8,128)(2,1)S(1)}, bf16[2,3,24,768]{3,2,1,0:T(8,128)(2,1)S(1)}) custom-call(bf16[8,3,24,768]{3,2,1,0:T(8,128)(2,1)S(1)} %copy-done, bf16[8,3,24,768]{3,2,1,0:T(8,128)(2,1)} %collective-permute-done.11.refs_1_, bf16[4,3,24,768]{3,2,1,0:T(8,128)(2,1)} %collective-permute-done.20.refs_2_, ...), custom_call_target="tpu_custom_call" | custom-call | flops 1 | bytes 1 | tf_op jit(solution)/shard_map/combine/pallas_call | solution.py:709
  104.3 1.6 %collective-permute-start.27 = (bf16[2,3,24,768]{3,2,1,0:T(8,128)(2,1)S(1)}, bf16[2,3,24,768]{3,2,1,0:T(8,128)(2,1)S(1)}, u32[]{:S(2)}, u32[]{:S(2)}) collective-permute-start(bf16[2,3,24,768]{3,2,1,0:T(8,128)(2,1)S(1)} %get-tuple-element.153), channel_id=1, source_target_pairs={{0,2},{2,0},{4,6},{6,4},{8,10},{10,8},{12,14},{14,12},{16,18},{18,... | collective-permute-start | bytes 663560 | tf_op jit(solution)/shard_map/ppermute | solution.py:671
  105.9 1.5 %collective-permute-start.28 = (bf16[2,3,24,768]{3,2,1,0:T(8,128)(2,1)S(1)}, bf16[2,3,24,768]{3,2,1,0:T(8,128)(2,1)S(1)}, u32[]{:S(2)}, u32[]{:S(2)}) collective-permute-start(bf16[2,3,24,768]{3,2,1,0:T(8,128)(2,1)S(1)} %get-tuple-element.154), channel_id=1, source_target_pairs={{0,4},{2,6},{4,0},{6,2},{8,12},{10,14},{12,8},{14,10},{16,20},{18,... | collective-permute-start | bytes 663560 | tf_op jit(solution)/shard_map/ppermute | solution.py:671
  107.4 3.3 %collective-permute-done.23.refs_3_.refs_4_.refs_5_.refs_6_ = bf16[8,24,1152]{2,1,0:T(8,128)(2,1)S(1)} collective-permute-done((bf16[8,24,1152]{2,1,0:T(8,128)(2,1)}, bf16[8,24,1152]{2,1,0:T(8,128)(2,1)S(1)}, u32[]{:S(2)}, u32[]{:S(2)}) %collective-permute-start.23) | collective-permute-done | bytes 442400 | tf_op jit(solution)/shard_map/ppermute | solution.py:671
  110.7 1.6 %collective-permute-start.26 = (bf16[2,3,24,768]{3,2,1,0:T(8,128)(2,1)S(1)}, bf16[2,3,24,768]{3,2,1,0:T(8,128)(2,1)S(1)}, u32[]{:S(2)}, u32[]{:S(2)}) collective-permute-start(bf16[2,3,24,768]{3,2,1,0:T(8,128)(2,1)S(1)} %get-tuple-element.146), channel_id=1, source_target_pairs={{0,8},{2,10},{4,12},{6,14},{8,0},{10,2},{12,4},{14,6},{16,24},{18,... | collective-permute-start | bytes 663560 | tf_op jit(solution)/shard_map/ppermute | solution.py:671
  112.4 0.6 collective-permute-start.29
  113.0 1.5 %collective-permute-start.24 = (bf16[4,24,1152]{2,1,0:T(8,128)(2,1)S(1)}, bf16[4,24,1152]{2,1,0:T(8,128)(2,1)S(1)}, u32[]{:S(2)}, u32[]{:S(2)}) collective-permute-start(bf16[4,24,1152]{2,1,0:T(8,128)(2,1)S(1)} %get-tuple-element.150), channel_id=1, source_target_pairs={{0,4},{2,6},{4,0},{6,2},{8,12},{10,14},{12,8},{14,10},{16,20},{18,... | collective-permute-start | bytes 663560 | tf_op jit(solution)/shard_map/ppermute | solution.py:671
  114.6 0.9 collective-permute-done.28.refs_11_.refs_13_
  115.5 1.2 collective-permute-done.26.refs_3_
  116.6 1.2 combine.17
  117.9 3.3 %collective-permute-start.34 = (bf16[3,3,24,768]{3,2,1,0:T(8,128)(2,1)S(1)}, bf16[3,3,24,768]{3,2,1,0:T(8,128)(2,1)S(1)}, u32[]{:S(2)}, u32[]{:S(2)}) collective-permute-start(bf16[3,3,24,768]{3,2,1,0:T(8,128)(2,1)S(1)} %combine.17), channel_id=1, source_target_pairs={{0,16},{2,18},{4,20},{6,22},{8,24},{10,26},{12,28},{14,30},{16,0},... | collective-permute-start | bytes 995336 | tf_op jit(solution)/shard_map/ppermute | solution.py:671
  121.2 1.5 %collective-permute-start.31 = (bf16[1,208,384]{2,1,0:T(8,128)(2,1)S(1)}, bf16[1,208,384]{2,1,0:T(8,128)(2,1)S(1)}, u32[]{:S(2)}, u32[]{:S(2)}) collective-permute-start(bf16[1,208,384]{2,1,0:T(8,128)(2,1)S(1)} %combine.16.refs_0_), channel_id=1, source_target_pairs={{0,4},{2,6},{4,0},{6,2},{8,12},{10,14},{12,8},{14,10},{16,20},{18,... | collective-permute-start | bytes 479240 | tf_op jit(solution)/shard_map/ppermute | solution.py:671
  122.8 1.1 collective-permute-start.30
  123.9 2.6 %collective-permute-done.31.refs_1_ = bf16[1,208,384]{2,1,0:T(8,128)(2,1)S(1)} collective-permute-done((bf16[1,208,384]{2,1,0:T(8,128)(2,1)S(1)}, bf16[1,208,384]{2,1,0:T(8,128)(2,1)S(1)}, u32[]{:S(2)}, u32[]{:S(2)}) %collective-permute-start.31) | collective-permute-done | bytes 159776 | tf_op jit(solution)/shard_map/ppermute | solution.py:671
  126.6 3.3 %collective-permute-done.30.refs_3_.refs_7_.refs_8_ = bf16[4,24,1152]{2,1,0:T(8,128)(2,1)S(1)} collective-permute-done((bf16[4,24,1152]{2,1,0:T(8,128)(2,1)S(1)}, bf16[4,24,1152]{2,1,0:T(8,128)(2,1)S(1)}, u32[]{:S(2)}, u32[]{:S(2)}) %collective-permute-start.30) | collective-permute-done | bytes 221216 | tf_op jit(solution)/shard_map/ppermute | solution.py:671
  129.9 2.6 %collective-permute-start.32 = (bf16[2,24,1152]{2,1,0:T(8,128)(2,1)S(1)}, bf16[2,24,1152]{2,1,0:T(8,128)(2,1)S(1)}, u32[]{:S(2)}, u32[]{:S(2)}) collective-permute-start(bf16[2,24,1152]{2,1,0:T(8,128)(2,1)S(1)} %combine.20), channel_id=1, source_target_pairs={{0,16},{2,18},{4,20},{6,22},{8,24},{10,26},{12,28},{14,30},{16,0},... | collective-permute-start | bytes 331784 | tf_op jit(solution)/shard_map/ppermute | solution.py:671
  132.6 1.1 collective-permute-done.34.refs_4_.refs_9_.refs_14_
  133.7 1.9 %split_feed.1 = (f32[96,768]{1,0:T(8,128)}, f32[3,24,768]{2,1,0:T(8,128)S(1)}, f32[3,24,768]{2,1,0:T(8,128)S(1)}) custom-call(s32[1]{0:T(128)} %bitcast.blk_ref, bf16[8,3,24,768]{3,2,1,0:T(8,128)(2,1)S(1)} %copy-done, bf16[8,3,24,768]{3,2,1,0:T(8,128)(2,1)} %collective-permute-done.11.refs_1_, bf16[4,3,24,768]{3,2,1,0:T(8,128)(2,1)} %collective-permute-done.20.refs_2_, ...), custom_call_target="tpu_custom_call" | custom-call | flops 1 | bytes 1 | tf_op jit(solution)/shard_map/split_feed/pallas_call | solution.py:820
  135.6 0.6 collective-permute-start.37
  136.4 0.9 collective-permute-done.37.refs_5_
  137.7 1.1 join.1
  (78 shorter events, 6.1 us)
Async XLA Ops:
  0.6 2.4 %collective-permute-start = (bf16[392,768]{1,0:T(8,128)(2,1)}, bf16[392,768]{1,0:T(8,128)(2,1)S(1)}, u32[]{:S(2)}, u32[]{:S(2)}) collective-permute-start(bf16[392,768]{1,0:T(8,128)(2,1)} %bitcast.10), channel_id=1, source_target_pairs={{0,1},{1,0},{2,3},{3,2},{4,5},{5,4},{6,7},{7,6},{8,9},{9,8},{10,11... | collective-permute-start | bytes 1806344 | tf_op jit(solution)/shard_map/ppermute | solution.py:667
  1.2 1.9 %collective-permute-start.1 = (s32[1,392]{1,0:T(1,128)}, s32[1,392]{1,0:T(1,128)S(1)}, u32[]{:S(2)}, u32[]{:S(2)}) collective-permute-start(s32[1,392]{1,0:T(1,128)} %refs_2_.1), channel_id=1, source_target_pairs={{0,1},{1,0},{2,3},{3,2},{4,5},{5,4},{6,7},{7,6},{8,9},{9,8},{10,11... | collective-permute-start | bytes 4712 | tf_op jit(solution)/shard_map/ppermute | solution.py:667
  1.2 1.8 %collective-permute-start.2 = (s32[1,392]{1,0:T(1,128)}, s32[1,392]{1,0:T(1,128)S(1)}, u32[]{:S(2)}, u32[]{:S(2)}) collective-permute-start(s32[1,392]{1,0:T(1,128)} %refs_10_.3), channel_id=1, source_target_pairs={{0,1},{1,0},{2,3},{3,2},{4,5},{5,4},{6,7},{7,6},{8,9},{9,8},{10,11... | collective-permute-start | bytes 4712 | tf_op jit(solution)/shard_map/ppermute | solution.py:667
  1.7 28.6 %collective-permute-start.3 = (bf16[392,768]{1,0:T(8,128)(2,1)}, bf16[392,768]{1,0:T(8,128)(2,1)S(1)}, u32[]{:S(2)}, u32[]{:S(2)}) collective-permute-start(bf16[392,768]{1,0:T(8,128)(2,1)} %bitcast.6), channel_id=1, source_target_pairs={{0,1},{1,0},{2,3},{3,2},{4,5},{5,4},{6,7},{7,6},{8,9},{9,8},{10,11... | collective-permute-start | bytes 1806344 | tf_op jit(solution)/shard_map/ppermute | solution.py:667
  29.7 8.1 %collective-permute-start.5 = (bf16[392,1536]{1,0:T(8,128)(2,1)}, bf16[392,1536]{1,0:T(8,128)(2,1)S(1)}, u32[]{:S(2)}, u32[]{:S(2)}) collective-permute-start(bf16[392,1536]{1,0:T(8,128)(2,1)} %get-tuple-element.106), channel_id=1, source_target_pairs={{0,1},{1,0},{2,3},{3,2},{4,5},{5,4},{6,7},{7,6},{8,9},{9,8},{10,11... | collective-permute-start | bytes 3612680 | tf_op jit(solution)/shard_map/ppermute | solution.py:667
  30.2 7.7 %collective-permute-start.6 = (bf16[392,1536]{1,0:T(8,128)(2,1)}, bf16[392,1536]{1,0:T(8,128)(2,1)S(1)}, u32[]{:S(2)}, u32[]{:S(2)}) collective-permute-start(bf16[392,1536]{1,0:T(8,128)(2,1)} %get-tuple-element.108), channel_id=1, source_target_pairs={{0,1},{1,0},{2,3},{3,2},{4,5},{5,4},{6,7},{7,6},{8,9},{9,8},{10,11... | collective-permute-start | bytes 3612680 | tf_op jit(solution)/shard_map/ppermute | solution.py:667
  30.3 5.2 %copy-start.9 = (bf16[392,768]{1,0:T(8,128)(2,1)}, bf16[392,768]{1,0:T(8,128)(2,1)S(1)}, u32[]{:S(2)}) copy-start(bf16[392,768]{1,0:T(8,128)(2,1)S(1)} %collective-permute-done.3.refs_7_) | copy-start | bytes 1806340
  30.3 5.7 %collective-permute-start.4 = (bf16[392,768]{1,0:T(8,128)(2,1)}, bf16[392,768]{1,0:T(8,128)(2,1)}, u32[]{:S(2)}, u32[]{:S(2)}) collective-permute-start(bf16[392,768]{1,0:T(8,128)(2,1)} %get-tuple-element.104.refs_0_), channel_id=1, source_target_pairs={{0,1},{1,0},{2,3},{3,2},{4,5},{5,4},{6,7},{7,6},{8,9},{9,8},{10,11... | collective-permute-start | bytes 1806344 | tf_op jit(solution)/shard_map/ppermute | solution.py:667
  30.7 5.8 %collective-permute-start.7 = (bf16[392,768]{1,0:T(8,128)(2,1)}, bf16[392,768]{1,0:T(8,128)(2,1)}, u32[]{:S(2)}, u32[]{:S(2)}) collective-permute-start(bf16[392,768]{1,0:T(8,128)(2,1)} %get-tuple-element.109.refs_8_), channel_id=1, source_target_pairs={{0,1},{1,0},{2,3},{3,2},{4,5},{5,4},{6,7},{7,6},{8,9},{9,8},{10,11... | collective-permute-start | bytes 1806344 | tf_op jit(solution)/shard_map/ppermute | solution.py:667
  35.5 2.3 %collective-permute-start.8 = (bf16[392,768]{1,0:T(8,128)(2,1)}, bf16[392,768]{1,0:T(8,128)(2,1)S(1)}, u32[]{:S(2)}, u32[]{:S(2)}) collective-permute-start(bf16[392,768]{1,0:T(8,128)(2,1)} %get-tuple-element.110.refs_10_), channel_id=1, source_target_pairs={{0,1},{1,0},{2,3},{3,2},{4,5},{5,4},{6,7},{7,6},{8,9},{9,8},{10,11... | collective-permute-start | bytes 1806344 | tf_op jit(solution)/shard_map/ppermute | solution.py:667
  37.8 1.2 copy-start.7
  37.9 1.7 %copy-start.8 = (bf16[392,1536]{1,0:T(8,128)(2,1)}, bf16[392,1536]{1,0:T(8,128)(2,1)S(1)}, u32[]{:S(2)}) copy-start(bf16[392,1536]{1,0:T(8,128)(2,1)S(1)} %collective-permute-done.6.refs_5_) | copy-start | bytes 3612676
  50.2 23.1 %collective-permute-start.12 = (bf16[8,3,24,768]{3,2,1,0:T(8,128)(2,1)}, bf16[8,3,24,768]{3,2,1,0:T(8,128)(2,1)S(1)}, u32[]{:S(2)}, u32[]{:S(2)}) collective-permute-start(bf16[8,3,24,768]{3,2,1,0:T(8,128)(2,1)} %get-tuple-element.132), channel_id=1, source_target_pairs={{0,4},{2,6},{4,0},{6,2},{8,12},{10,14},{12,8},{14,10},{16,20},{18,... | collective-permute-start | bytes 2654216 | tf_op jit(solution)/shard_map/ppermute | solution.py:671
  53.1 27.5 %collective-permute-start.13 = (bf16[8,3,24,768]{3,2,1,0:T(8,128)(2,1)}, bf16[8,3,24,768]{3,2,1,0:T(8,128)(2,1)}, u32[]{:S(2)}, u32[]{:S(2)}) collective-permute-start(bf16[8,3,24,768]{3,2,1,0:T(8,128)(2,1)} %get-tuple-element.134), channel_id=1, source_target_pairs={{0,8},{2,10},{4,12},{6,14},{8,0},{10,2},{12,4},{14,6},{16,24},{18,... | collective-permute-start | bytes 2654216 | tf_op jit(solution)/shard_map/ppermute | solution.py:671
  54.7 26.5 %collective-permute-start.11 = (bf16[8,3,24,768]{3,2,1,0:T(8,128)(2,1)}, bf16[8,3,24,768]{3,2,1,0:T(8,128)(2,1)}, u32[]{:S(2)}, u32[]{:S(2)}) collective-permute-start(bf16[8,3,24,768]{3,2,1,0:T(8,128)(2,1)} %get-tuple-element.111), channel_id=1, source_target_pairs={{0,2},{2,0},{4,6},{6,4},{8,10},{10,8},{12,14},{14,12},{16,18},{18,... | collective-permute-start | bytes 2654216 | tf_op jit(solution)/shard_map/ppermute | solution.py:671
  69.8 2.0 %collective-permute-start.9 = (bf16[2,248,384]{2,1,0:T(8,128)(2,1)}, bf16[2,248,384]{2,1,0:T(8,128)(2,1)S(1)}, u32[]{:S(2)}, u32[]{:S(2)}) collective-permute-start(bf16[2,248,384]{2,1,0:T(8,128)(2,1)} %get-tuple-element.120), channel_id=1, source_target_pairs={{0,1},{1,0},{2,3},{3,2},{4,5},{5,4},{6,7},{7,6},{8,9},{9,8},{10,11... | collective-permute-start | bytes 1142792 | tf_op jit(solution)/shard_map/ppermute | solution.py:667
  69.9 2.4 %collective-permute-start.10 = (bf16[2,248,384]{2,1,0:T(8,128)(2,1)}, bf16[2,248,384]{2,1,0:T(8,128)(2,1)S(1)}, u32[]{:S(2)}, u32[]{:S(2)}) collective-permute-start(bf16[2,248,384]{2,1,0:T(8,128)(2,1)} %get-tuple-element.121.refs_3_), channel_id=1, source_target_pairs={{0,1},{1,0},{2,3},{3,2},{4,5},{5,4},{6,7},{7,6},{8,9},{9,8},{10,11... | collective-permute-start | bytes 1142792 | tf_op jit(solution)/shard_map/ppermute | solution.py:667
  71.8 1.5 %copy-start.6 = (bf16[2,248,384]{2,1,0:T(8,128)(2,1)}, bf16[2,248,384]{2,1,0:T(8,128)(2,1)S(1)}, u32[]{:S(2)}) copy-start(bf16[2,248,384]{2,1,0:T(8,128)(2,1)S(1)} %collective-permute-done.9.refs_4_) | copy-start | bytes 1142788
  71.8 14.5 %collective-permute-start.15 = (bf16[392,384]{1,0:T(8,128)(2,1)}, bf16[392,384]{1,0:T(8,128)(2,1)}, u32[]{:S(2)}, u32[]{:S(2)}) collective-permute-start(bf16[392,384]{1,0:T(8,128)(2,1)} %get-tuple-element.117.refs_1_), channel_id=1, source_target_pairs={{0,1},{1,0},{2,3},{3,2},{4,5},{5,4},{6,7},{7,6},{8,9},{9,8},{10,11... | collective-permute-start | bytes 903176 | tf_op jit(solution)/shard_map/ppermute | solution.py:667
  72.3 15.7 %collective-permute-start.16 = (bf16[392,384]{1,0:T(8,128)(2,1)}, bf16[392,384]{1,0:T(8,128)(2,1)}, u32[]{:S(2)}, u32[]{:S(2)}) collective-permute-start(bf16[392,384]{1,0:T(8,128)(2,1)} %get-tuple-element.118.refs_2_), channel_id=1, source_target_pairs={{0,1},{1,0},{2,3},{3,2},{4,5},{5,4},{6,7},{7,6},{8,9},{9,8},{10,11... | collective-permute-start | bytes 903176 | tf_op jit(solution)/shard_map/ppermute | solution.py:667
  73.3 16.3 %collective-permute-start.17 = (bf16[392,384]{1,0:T(8,128)(2,1)}, bf16[392,384]{1,0:T(8,128)(2,1)}, u32[]{:S(2)}, u32[]{:S(2)}) collective-permute-start(bf16[392,384]{1,0:T(8,128)(2,1)} %get-tuple-element.119.refs_3_), channel_id=1, source_target_pairs={{0,1},{1,0},{2,3},{3,2},{4,5},{5,4},{6,7},{7,6},{8,9},{9,8},{10,11... | collective-permute-start | bytes 903176 | tf_op jit(solution)/shard_map/ppermute | solution.py:667
  73.3 7.9 %copy-start = (bf16[8,3,24,768]{3,2,1,0:T(8,128)(2,1)S(1)}, bf16[8,3,24,768]{3,2,1,0:T(8,128)(2,1)}, u32[]{:S(2)}) copy-start(bf16[8,3,24,768]{3,2,1,0:T(8,128)(2,1)} %get-tuple-element.152.refs_0_) | copy-start | bytes 2654212
  73.3 7.9 %copy-start.1 = (bf16[8,3,24,768]{3,2,1,0:T(8,128)(2,1)S(1)}, bf16[8,3,24,768]{3,2,1,0:T(8,128)(2,1)}, u32[]{:S(2)}) copy-start(bf16[8,3,24,768]{3,2,1,0:T(8,128)(2,1)} %get-tuple-element.131.refs_2_.refs_3_.refs_4_.refs_5_) | copy-start | bytes 2654212
  73.3 7.9 %copy-start.2 = (bf16[8,3,24,768]{3,2,1,0:T(8,128)(2,1)S(1)}, bf16[8,3,24,768]{3,2,1,0:T(8,128)(2,1)}, u32[]{:S(2)}) copy-start(bf16[8,3,24,768]{3,2,1,0:T(8,128)(2,1)} %get-tuple-element.133.refs_4_.refs_6_.refs_8_.refs_10_) | copy-start | bytes 2654212
  80.6 2.9 %collective-permute-start.14 = (bf16[1,208,384]{2,1,0:T(8,128)(2,1)}, bf16[1,208,384]{2,1,0:T(8,128)(2,1)S(1)}, u32[]{:S(2)}, u32[]{:S(2)}) collective-permute-start(bf16[1,208,384]{2,1,0:T(8,128)(2,1)} %get-tuple-element.137), channel_id=1, source_target_pairs={{0,1},{1,0},{2,3},{3,2},{4,5},{5,4},{6,7},{7,6},{8,9},{9,8},{10,11... | collective-permute-start | bytes 479240 | tf_op jit(solution)/shard_map/ppermute | solution.py:667
  81.2 2.4 %copy-start.5 = (bf16[1,208,384]{2,1,0:T(8,128)(2,1)S(1)}, bf16[1,208,384]{2,1,0:T(8,128)(2,1)}, u32[]{:S(2)}) copy-start(bf16[1,208,384]{2,1,0:T(8,128)(2,1)} %get-tuple-element.136.refs_0_) | copy-start | bytes 479236
  84.3 11.8 %collective-permute-start.19 = (bf16[1,208,384]{2,1,0:T(8,128)(2,1)}, bf16[1,208,384]{2,1,0:T(8,128)(2,1)}, u32[]{:S(2)}, u32[]{:S(2)}) collective-permute-start(bf16[1,208,384]{2,1,0:T(8,128)(2,1)} %combine.12.refs_0_), channel_id=1, source_target_pairs={{0,8},{2,10},{4,12},{6,14},{8,0},{10,2},{12,4},{14,6},{16,24},{18,... | collective-permute-start | bytes 479240 | tf_op jit(solution)/shard_map/ppermute | solution.py:671
  86.1 14.0 %collective-permute-start.21 = (bf16[4,3,24,768]{3,2,1,0:T(8,128)(2,1)}, bf16[4,3,24,768]{3,2,1,0:T(8,128)(2,1)S(1)}, u32[]{:S(2)}, u32[]{:S(2)}) collective-permute-start(bf16[4,3,24,768]{3,2,1,0:T(8,128)(2,1)} %get-tuple-element.144), channel_id=1, source_target_pairs={{0,8},{2,10},{4,12},{6,14},{8,0},{10,2},{12,4},{14,6},{16,24},{18,... | collective-permute-start | bytes 1327112 | tf_op jit(solution)/shard_map/ppermute | solution.py:671
  86.3 16.5 %collective-permute-start.22 = (bf16[4,3,24,768]{3,2,1,0:T(8,128)(2,1)}, bf16[4,3,24,768]{3,2,1,0:T(8,128)(2,1)}, u32[]{:S(2)}, u32[]{:S(2)}) collective-permute-start(bf16[4,3,24,768]{3,2,1,0:T(8,128)(2,1)} %get-tuple-element.145), channel_id=1, source_target_pairs={{0,2},{2,0},{4,6},{6,4},{8,10},{10,8},{12,14},{14,12},{16,18},{18,... | collective-permute-start | bytes 1327112 | tf_op jit(solution)/shard_map/ppermute | solution.py:671
  88.0 14.8 %collective-permute-start.20 = (bf16[4,3,24,768]{3,2,1,0:T(8,128)(2,1)}, bf16[4,3,24,768]{3,2,1,0:T(8,128)(2,1)}, u32[]{:S(2)}, u32[]{:S(2)}) collective-permute-start(bf16[4,3,24,768]{3,2,1,0:T(8,128)(2,1)} %get-tuple-element.135), channel_id=1, source_target_pairs={{0,4},{2,6},{4,0},{6,2},{8,12},{10,14},{12,8},{14,10},{16,20},{18,... | collective-permute-start | bytes 1327112 | tf_op jit(solution)/shard_map/ppermute | solution.py:671
  95.5 15.2 %collective-permute-start.23 = (bf16[8,24,1152]{2,1,0:T(8,128)(2,1)}, bf16[8,24,1152]{2,1,0:T(8,128)(2,1)S(1)}, u32[]{:S(2)}, u32[]{:S(2)}) collective-permute-start(bf16[8,24,1152]{2,1,0:T(8,128)(2,1)} %get-tuple-element.149), channel_id=1, source_target_pairs={{0,4},{2,6},{4,0},{6,2},{8,12},{10,14},{12,8},{14,10},{16,20},{18,... | collective-permute-start | bytes 1327112 | tf_op jit(solution)/shard_map/ppermute | solution.py:671
  96.1 16.2 %collective-permute-start.18 = (bf16[8,24,1152]{2,1,0:T(8,128)(2,1)}, bf16[8,24,1152]{2,1,0:T(8,128)(2,1)S(1)}, u32[]{:S(2)}, u32[]{:S(2)}) collective-permute-start(bf16[8,24,1152]{2,1,0:T(8,128)(2,1)} %get-tuple-element.141), channel_id=1, source_target_pairs={{0,2},{2,0},{4,6},{6,4},{8,10},{10,8},{12,14},{14,12},{16,18},{18,... | collective-permute-start | bytes 1327112 | tf_op jit(solution)/shard_map/ppermute | solution.py:671
  97.4 14.9 %copy-start.3 = (bf16[8,24,1152]{2,1,0:T(8,128)(2,1)S(1)}, bf16[8,24,1152]{2,1,0:T(8,128)(2,1)}, u32[]{:S(2)}) copy-start(bf16[8,24,1152]{2,1,0:T(8,128)(2,1)} %get-tuple-element.158.refs_0_) | copy-start | bytes 1327108
  97.4 14.9 %copy-start.4 = (bf16[8,24,1152]{2,1,0:T(8,128)(2,1)S(1)}, bf16[8,24,1152]{2,1,0:T(8,128)(2,1)}, u32[]{:S(2)}) copy-start(bf16[8,24,1152]{2,1,0:T(8,128)(2,1)} %get-tuple-element.148.refs_2_.refs_3_.refs_4_.refs_5_) | copy-start | bytes 1327108
  100.1 12.9 %collective-permute-start.25 = (bf16[1,208,384]{2,1,0:T(8,128)(2,1)S(1)}, bf16[1,208,384]{2,1,0:T(8,128)(2,1)S(1)}, u32[]{:S(2)}, u32[]{:S(2)}) collective-permute-start(bf16[1,208,384]{2,1,0:T(8,128)(2,1)S(1)} %combine.13.refs_0_), channel_id=1, source_target_pairs={{0,16},{2,18},{4,20},{6,22},{8,24},{10,26},{12,28},{14,30},{16,0},... | collective-permute-start | bytes 479240 | tf_op jit(solution)/shard_map/ppermute | solution.py:671
  104.3 10.3 %collective-permute-start.27 = (bf16[2,3,24,768]{3,2,1,0:T(8,128)(2,1)S(1)}, bf16[2,3,24,768]{3,2,1,0:T(8,128)(2,1)S(1)}, u32[]{:S(2)}, u32[]{:S(2)}) collective-permute-start(bf16[2,3,24,768]{3,2,1,0:T(8,128)(2,1)S(1)} %get-tuple-element.153), channel_id=1, source_target_pairs={{0,2},{2,0},{4,6},{6,4},{8,10},{10,8},{12,14},{14,12},{16,18},{18,... | collective-permute-start | bytes 663560 | tf_op jit(solution)/shard_map/ppermute | solution.py:671
  105.9 9.6 %collective-permute-start.28 = (bf16[2,3,24,768]{3,2,1,0:T(8,128)(2,1)S(1)}, bf16[2,3,24,768]{3,2,1,0:T(8,128)(2,1)S(1)}, u32[]{:S(2)}, u32[]{:S(2)}) collective-permute-start(bf16[2,3,24,768]{3,2,1,0:T(8,128)(2,1)S(1)} %get-tuple-element.154), channel_id=1, source_target_pairs={{0,4},{2,6},{4,0},{6,2},{8,12},{10,14},{12,8},{14,10},{16,20},{18,... | collective-permute-start | bytes 663560 | tf_op jit(solution)/shard_map/ppermute | solution.py:671
  110.7 5.9 %collective-permute-start.26 = (bf16[2,3,24,768]{3,2,1,0:T(8,128)(2,1)S(1)}, bf16[2,3,24,768]{3,2,1,0:T(8,128)(2,1)S(1)}, u32[]{:S(2)}, u32[]{:S(2)}) collective-permute-start(bf16[2,3,24,768]{3,2,1,0:T(8,128)(2,1)S(1)} %get-tuple-element.146), channel_id=1, source_target_pairs={{0,8},{2,10},{4,12},{6,14},{8,0},{10,2},{12,4},{14,6},{16,24},{18,... | collective-permute-start | bytes 663560 | tf_op jit(solution)/shard_map/ppermute | solution.py:671
  112.4 10.3 %collective-permute-start.29 = (bf16[4,24,1152]{2,1,0:T(8,128)(2,1)S(1)}, bf16[4,24,1152]{2,1,0:T(8,128)(2,1)S(1)}, u32[]{:S(2)}, u32[]{:S(2)}) collective-permute-start(bf16[4,24,1152]{2,1,0:T(8,128)(2,1)S(1)} %get-tuple-element.156), channel_id=1, source_target_pairs={{0,2},{2,0},{4,6},{6,4},{8,10},{10,8},{12,14},{14,12},{16,18},{18,... | collective-permute-start | bytes 663560 | tf_op jit(solution)/shard_map/ppermute | solution.py:671
  113.0 9.7 %collective-permute-start.24 = (bf16[4,24,1152]{2,1,0:T(8,128)(2,1)S(1)}, bf16[4,24,1152]{2,1,0:T(8,128)(2,1)S(1)}, u32[]{:S(2)}, u32[]{:S(2)}) collective-permute-start(bf16[4,24,1152]{2,1,0:T(8,128)(2,1)S(1)} %get-tuple-element.150), channel_id=1, source_target_pairs={{0,4},{2,6},{4,0},{6,2},{8,12},{10,14},{12,8},{14,10},{16,20},{18,... | collective-permute-start | bytes 663560 | tf_op jit(solution)/shard_map/ppermute | solution.py:671
  117.9 15.8 %collective-permute-start.34 = (bf16[3,3,24,768]{3,2,1,0:T(8,128)(2,1)S(1)}, bf16[3,3,24,768]{3,2,1,0:T(8,128)(2,1)S(1)}, u32[]{:S(2)}, u32[]{:S(2)}) collective-permute-start(bf16[3,3,24,768]{3,2,1,0:T(8,128)(2,1)S(1)} %combine.17), channel_id=1, source_target_pairs={{0,16},{2,18},{4,20},{6,22},{8,24},{10,26},{12,28},{14,30},{16,0},... | collective-permute-start | bytes 995336 | tf_op jit(solution)/shard_map/ppermute | solution.py:671
  121.2 5.3 %collective-permute-start.31 = (bf16[1,208,384]{2,1,0:T(8,128)(2,1)S(1)}, bf16[1,208,384]{2,1,0:T(8,128)(2,1)S(1)}, u32[]{:S(2)}, u32[]{:S(2)}) collective-permute-start(bf16[1,208,384]{2,1,0:T(8,128)(2,1)S(1)} %combine.16.refs_0_), channel_id=1, source_target_pairs={{0,4},{2,6},{4,0},{6,2},{8,12},{10,14},{12,8},{14,10},{16,20},{18,... | collective-permute-start | bytes 479240 | tf_op jit(solution)/shard_map/ppermute | solution.py:671
  122.8 7.1 %collective-permute-start.30 = (bf16[4,24,1152]{2,1,0:T(8,128)(2,1)S(1)}, bf16[4,24,1152]{2,1,0:T(8,128)(2,1)S(1)}, u32[]{:S(2)}, u32[]{:S(2)}) collective-permute-start(bf16[4,24,1152]{2,1,0:T(8,128)(2,1)S(1)} %combine.18), channel_id=1, source_target_pairs={{0,8},{2,10},{4,12},{6,14},{8,0},{10,2},{12,4},{14,6},{16,24},{18,... | collective-permute-start | bytes 663560 | tf_op jit(solution)/shard_map/ppermute | solution.py:671
  126.5 9.1 %collective-permute-start.36 = (bf16[1,208,384]{2,1,0:T(8,128)(2,1)S(1)}, bf16[1,208,384]{2,1,0:T(8,128)(2,1)S(1)}, u32[]{:S(2)}, u32[]{:S(2)}) collective-permute-start(bf16[1,208,384]{2,1,0:T(8,128)(2,1)S(1)} %combine.19.refs_0_), channel_id=1, source_target_pairs={{0,2},{2,0},{4,6},{6,4},{8,10},{10,8},{12,14},{14,12},{16,18},{18,... | collective-permute-start | bytes 479240 | tf_op jit(solution)/shard_map/ppermute | solution.py:671
  129.9 6.3 %collective-permute-start.32 = (bf16[2,24,1152]{2,1,0:T(8,128)(2,1)S(1)}, bf16[2,24,1152]{2,1,0:T(8,128)(2,1)S(1)}, u32[]{:S(2)}, u32[]{:S(2)}) collective-permute-start(bf16[2,24,1152]{2,1,0:T(8,128)(2,1)S(1)} %combine.20), channel_id=1, source_target_pairs={{0,16},{2,18},{4,20},{6,22},{8,24},{10,26},{12,28},{14,30},{16,0},... | collective-permute-start | bytes 331784 | tf_op jit(solution)/shard_map/ppermute | solution.py:671
  135.6 2.1 %collective-permute-start.35 = (f32[3,24,768]{2,1,0:T(8,128)S(1)}, f32[3,24,768]{2,1,0:T(8,128)S(1)}, u32[]{:S(2)}, u32[]{:S(2)}) collective-permute-start(f32[3,24,768]{2,1,0:T(8,128)S(1)} %get-tuple-element.162), channel_id=1, source_target_pairs={{0,1},{1,0},{2,3},{3,2},{4,5},{5,4},{6,7},{7,6},{8,9},{9,8},{10,11... | collective-permute-start | bytes 663560 | tf_op jit(solution)/shard_map/ppermute | solution.py:667
  135.6 1.7 %collective-permute-start.37 = (bf16[1,208,384]{2,1,0:T(8,128)(2,1)S(1)}, bf16[1,208,384]{2,1,0:T(8,128)(2,1)S(1)}, u32[]{:S(2)}, u32[]{:S(2)}) collective-permute-start(bf16[1,208,384]{2,1,0:T(8,128)(2,1)S(1)} %combine.21.refs_4_), channel_id=1, source_target_pairs={{0,1},{1,0},{2,3},{3,2},{4,5},{5,4},{6,7},{7,6},{8,9},{9,8},{10,11... | collective-permute-start | bytes 479240 | tf_op jit(solution)/shard_map/ppermute | solution.py:667
  136.3 1.4 collective-permute-start.33
  (5 other events, 3.8 us)

commit v2 on v1

--- a/solution.py
+++ b/solution.py
@@ -306,9 +306,13 @@
     )(blk, *operands)
 
 
-def mid_kernel(gn_hbm, h1_hbm, cot_hbm, wo_hbm, g2_hbm, gh_ref, gb_ref, ga_ref, sums_ref, *refs):
-    gn_ref, h1_ref, cot_ref, wo_ref, g2_ref, sem = refs
-    done(started(zip((gn_hbm, h1_hbm, cot_hbm, g2_hbm, wo_hbm), (gn_ref, h1_ref, cot_ref, g2_ref, wo_ref)), sem))
+def mid_kernel(blk_ref, gn_hbm, h1_hbm, cot_hbm, wo_hbm, g2_hbm, *refs):
+    gh_ref, keep_ref, send_ref, ga_ref, sums_ref = refs[:5]
+    gn_ref, h1_ref, cot_ref, wo_ref, g2_ref, gb_ref, sem = refs[5:]
+    width = gb_ref.shape[1]
+    cols = width // 2
+    loads = started(zip((gn_hbm, h1_hbm, cot_hbm, g2_hbm, wo_hbm), (gn_ref, h1_ref, cot_ref, g2_ref, wo_ref)), sem)
+    done(loads)
     normal, inv = normalise(h1_ref[...])
     total = gn_ref[...]
     cot = cot_ref[...].astype(F32)
@@ -316,6 +320,8 @@
     gh_ref[...] = grad_hidden1
     branch = grad_hidden1.astype(BF)
     gb_ref[...] = branch
+    for ref, core in ((keep_ref, blk_ref[0]), (send_ref, 1 - blk_ref[0])):
+        ref[...] = gb_ref[:, pl.ds(pl.multiple_of(core * cols, 128), cols)]
     ga_ref[...] = dot_nt(branch, wo_ref[...]).astype(BF)
     sums_ref[0:1, :] = column_sum(total * normal)
     sums_ref[1:2, :] = column_sum(total)
@@ -323,21 +329,26 @@
     sums_ref[3:4, :] = column_sum(cot)
 
 
-def mid(gn, h1, cot, wo, g2):
+def mid(blk, gn, h1, cot, wo, g2):
     half, width = h1.shape
     operands = (gn, h1, cot, wo, g2)
-    shapes = [((half, width), F32), ((half, width), BF), ((half, width), BF), ((4, width), F32)]
+    part = ((half, width // 2), BF)
+    shapes = [((half, width), F32), part, part, ((half, width), BF), ((4, width), F32)]
     return pl.pallas_call(
         mid_kernel,
-        grid=(1,),
-        in_specs=[ANYWHERE] * 5,
-        out_specs=[whole(v[0]) for v in shapes],
+        grid_spec=pltpu.PrefetchScalarGridSpec(
+            num_scalar_prefetch=1,
+            grid=(1,),
+            in_specs=[ANYWHERE] * 5,
+            out_specs=[whole(v[0]) for v in shapes],
+            scratch_shapes=[pltpu.VMEM(v.shape, v.dtype) for v in operands]
+            + [pltpu.VMEM((half, width), BF), pltpu.SemaphoreType.DMA((5,))],
+        ),
         out_shape=[jax.ShapeDtypeStruct(*v) for v in shapes],
-        scratch_shapes=[pltpu.VMEM(v.shape, v.dtype) for v in operands] + [pltpu.SemaphoreType.DMA((5,))],
         compiler_params=params(60),
         cost_estimate=cost(1, 1),
         name="mid",
-    )(*operands)
+    )(blk, *operands)
 
 
 class Plan:
@@ -369,8 +380,7 @@
     chunk = g_ref.shape[1] // 2
     rows = width // groups
     unit = rows // 2
-    at = pl.ds(pl.multiple_of(blk_ref[0] * cols, 128), cols)
-    pairs = list(zip(sources[:10], targets)) + [(sources[10].at[:, at], gb_ref), (sources[11].at[:, at], gbo_ref)]
+    pairs = list(zip(sources, targets))
     loads = started(pairs, in_sem)
 
     def emit(number, p, value):
@@ -434,22 +444,27 @@
 
 def attend_back_kernel(blk_ref, q_hbm, k_hbm, v_hbm, ga_hbm, p_hbm, *refs):
     outs, refs = refs[:6], refs[6:]
-    q_ref, k_ref, v_ref, ga_ref, p_ref, d_ref, h_ref, sem, p_sem, out_sem = refs
+    q_ref, k_ref, v_ref, ga_ref, p_ref, d_ref, h_ref, sem, out_sem = refs
     half, width = q_ref.shape
     cols = width // 2
-    loads = started(
-        [(q_hbm, q_ref), (k_hbm, k_ref), (v_hbm, v_ref), (ga_hbm, ga_ref)], sem
-    )
     heads = p_ref.shape[0]
     per = heads // 2
-    probs_in = started([(p_hbm.at[k : k + per], p_ref.at[k : k + per]) for k in range(0, heads, per)], p_sem)
-    done(loads + probs_in[:1])
+    fetch = []
+    for side in range(2):
+        at = slice(side * cols, (side + 1) * cols)
+        arrays = [(src.at[:, at], dst.at[:, at]) for src, dst in ((q_hbm, q_ref), (k_hbm, k_ref), (v_hbm, v_ref), (ga_hbm, ga_ref))]
+        fetch.append(copies(arrays + [(p_hbm.at[side * per : (side + 1) * per], p_ref.at[side * per : (side + 1) * per])], sem.at[side]))
+    for copy in fetch[0]:
+        copy.start()
+    done(fetch[0])
+    for copy in fetch[1]:
+        copy.start()
     pairs = heads // 4
 
     def one_side(side, carry):
         @pl.when(side == 1)
         def _():
-            probs_in[1].wait()
+            done(fetch[1])
 
         for pair in range(pairs):
             lanes = pl.ds(pl.multiple_of(side * cols + pair * 128, 128), 128)
@@ -519,8 +534,7 @@
                 pltpu.VMEM(probs.shape, BF),
                 pltpu.VMEM((2, 3, half, cols), BF),
                 pltpu.VMEM((2, 2, halo, cols), BF),
-                pltpu.SemaphoreType.DMA((4,)),
-                pltpu.SemaphoreType.DMA((2,)),
+                pltpu.SemaphoreType.DMA((2, 5)),
                 pltpu.SemaphoreType.DMA((6,)),
             ],
         ),
@@ -1022,8 +1036,8 @@
         qkv_weight, out_weight, fc1_weight, fc2_weight,
     )
     grad_other, act_other, n2_other = swap(grad_send), swap(act_send), swap(behind(n2, cot_other))
-    gh1, gb, ga, sums = mid(gn2, hidden1, cot, out_weight, ln2_gain)
-    att_other, gb_other = swap(att), swap(gb)
+    gh1, gb, gb_send, ga, sums = mid(blk1, gn2, hidden1, cot, out_weight, ln2_gain)
+    att_other, gb_other = swap(att), swap(gb_send)
     parts = feed_weights(
         plan, own1, blk1, behind(n2, ga), n2_other, grad_keep, grad_other, act_keep, act_other, cot, cot_other, att, att_other, gb, gb_other,
     )

time: 139 us -> 139 us (level)
  transfers between devices with their start and end apart: 38 -> 38, of which waited for: 15 -> 14; matrix products, arithmetic and copies ran while one was open for 0% -> 0% of each run, Pallas kernels for 48% -> 48%
where the time goes in v2:
time: 139 us; the launch traced here: 138 us
  Pallas kernels  78 us (56%)
  starting transfers between devices  34.9 us (25%)
  waiting for transfers between devices  22 us (16%)
  local copies, waits for them, and re-layouts  2.39 us (2%)
    ppermute x20, starting transfers between devices, across(): return lax.ppermute(v, 'dp', [(i, i ^ flip) for i in range(ndp)])  30.2 us
    pallas_call x1, Pallas kernels, front(): pl.pallas_call(functools.partial(front_kernel, hidden // plan.groups // 2...  25.8 us
    ppermute x20, waiting for transfers between devices, across(): return lax.ppermute(v, 'dp', [(i, i ^ flip) for i in range(ndp)])  16.2 us
    pallas_call x1, Pallas kernels, attend_back(): pl.pallas_call(body, grid_spec=pltpu.PrefetchScalarGridSpec(num_scalar_pr...  13.3 us
    pallas_call x1, Pallas kernels, feed_weights(): pl.pallas_call(functools.partial(feed_weights_kernel, plan), grid_spec=pl...  10.6 us
    pallas_call x1, Pallas kernels, front_back(): pl.pallas_call(functools.partial(front_back_kernel, places), grid_spec=pl...  7.27 us
    pallas_call x11, Pallas kernels, combine(): pl.pallas_call(functools.partial(combine_kernel, counts), grid=(1,), in_s...  7.2 us
    pallas_call x1, Pallas kernels, attend_weights(): pl.pallas_call(functools.partial(attend_weights_kernel, plan), grid_spec=...  5.93 us
  transfers between devices with their start and end apart: 38, of which 14 were waited for; matrix products, arithmetic and copies ran while one was open for 0% of the time, Pallas kernels for 48%

profile of v2, /device:TPU:0, one launch (start us, length us, event | category | flops | bytes accessed | tf_op | source)
XLA Modules:
  0.0 138.4 jit_solution(7473581655269539547)
XLA Ops:
  0.6 0.5 collective-permute-start
  1.8 1.3 collective-permute-done.1.refs_3_
  3.1 0.6 copy-done.13
  3.9 25.8 %front.1 = (f32[392,768]{1,0:T(8,128)}, bf16[392,768]{1,0:T(8,128)(2,1)}, bf16[392,768]{1,0:T(8,128)(2,1)}, bf16[392,768]{1,0:T(8,128)(2,1)}, bf16[640,768]{1,0:...) custom-call(s32[1]{0:T(128)} %bitcast.blk_ref, ...), custom_call_target="tpu_custom_call" | custom-call | flops 10481565696 | bytes 18874368 | tf_op jit(solution)/shard_map/front/pallas_call | solution.py:267
  30.8 4.8 %mid.1 = (f32[392,768]{1,0:T(8,128)}, bf16[392,384]{1,0:T(8,128)(2,1)}, bf16[392,384]{1,0:T(8,128)(2,1)}, bf16[392,768]{1,0:T(8,128)(2,1)}, f32[4,768]{1,0:T(4,128)}) custom-call(s32[1]{0:T(128)} %bitcast.blk_ref, f32[392,768]{1,0:T(8,128)} %get-tuple-element.101.gn_hbm, f32[392,768]{1,0:T(8,128)} %get-tuple-element.102.h1_hbm, bf16[392,768]{1,0:T(8,128)(2,1)} %bitcast.8, ...), custom_call_target="tpu_custom_call" | custom-call | flops 1 | bytes 1 | tf_op jit(solution)/shard_map/mid/pallas_call | solution.py:337
  36.0 1.4 %collective-permute-done.8.refs_11_ = bf16[392,384]{1,0:T(8,128)(2,1)S(1)} collective-permute-done((bf16[392,384]{1,0:T(8,128)(2,1)}, bf16[392,384]{1,0:T(8,128)(2,1)S(1)}, u32[]{:S(2)}, u32[]{:S(2)}) %collective-permute-start.8) | collective-permute-done | bytes 301088 | tf_op jit(solution)/shard_map/ppermute | solution.py:681
  37.5 0.7 copy-done.11
  39.1 10.6 %feed_weights.1 = (bf16[8,3,24,768]{3,2,1,0:T(8,128)(2,1)}, bf16[8,3,24,768]{3,2,1,0:T(8,128)(2,1)}, bf16[8,3,24,768]{3,2,1,0:T(8,128)(2,1)}, bf16[8,3,24,768]{3...) custom-call(s32[1]{0:T(128)} %bitcast.4.own_ref, s32[1]{0:T(128)} %bitcast.blk_ref, ...), custom_call_target="tpu_custom_call" | custom-call | flops 1 | bytes 1 | tf_op jit(solution)/shard_map/feed_weights/pallas_call | solution.py:426
  49.7 2.9 %collective-permute-start.12 = (bf16[8,3,24,768]{3,2,1,0:T(8,128)(2,1)}, bf16[8,3,24,768]{3,2,1,0:T(8,128)(2,1)S(1)}, u32[]{:S(2)}, u32[]{:S(2)}) collective-permute-start(bf16[8,3,24,768]{3,2,1,0:T(8,128)(2,1)} %get-tuple-element.134), channel_id=1, source_target_pairs={{0,4},{2,6},{4,0},{6,2},{8,12},{10,14},{12,8},{14,10},{16,20},{18,... | collective-permute-start | bytes 2654216 | tf_op jit(solution)/shard_map/ppermute | solution.py:685
  52.7 1.6 %collective-permute-start.13 = (bf16[8,3,24,768]{3,2,1,0:T(8,128)(2,1)}, bf16[8,3,24,768]{3,2,1,0:T(8,128)(2,1)}, u32[]{:S(2)}, u32[]{:S(2)}) collective-permute-start(bf16[8,3,24,768]{3,2,1,0:T(8,128)(2,1)} %get-tuple-element.136), channel_id=1, source_target_pairs={{0,8},{2,10},{4,12},{6,14},{8,0},{10,2},{12,4},{14,6},{16,24},{18,... | collective-permute-start | bytes 2654216 | tf_op jit(solution)/shard_map/ppermute | solution.py:685
  54.2 1.5 %collective-permute-start.11 = (bf16[8,3,24,768]{3,2,1,0:T(8,128)(2,1)}, bf16[8,3,24,768]{3,2,1,0:T(8,128)(2,1)}, u32[]{:S(2)}, u32[]{:S(2)}) collective-permute-start(bf16[8,3,24,768]{3,2,1,0:T(8,128)(2,1)} %get-tuple-element.113), channel_id=1, source_target_pairs={{0,2},{2,0},{4,6},{6,4},{8,10},{10,8},{12,14},{14,12},{16,18},{18,... | collective-permute-start | bytes 2654216 | tf_op jit(solution)/shard_map/ppermute | solution.py:685
  55.7 13.3 %attend_back.1 = (bf16[2,248,384]{2,1,0:T(8,128)(2,1)}, bf16[2,248,384]{2,1,0:T(8,128)(2,1)}, bf16[3,392,384]{2,1,0:T(8,128)(2,1)}, bf16[392,384]{1,0:T(8,128)(2...) custom-call(s32[1]{0:T(128)} %bitcast.blk_ref, bf16[392,768]{1,0:T(8,128)(2,1)} %get-tuple-element.114.refs_0_, ...), custom_call_target="tpu_custom_call" | custom-call | flops 1 | bytes 1 | tf_op jit(solution)/shard_map/attend_back/pallas_call | solution.py:522
  69.1 0.5 collective-permute-start.10
  69.6 1.4 %collective-permute-done.9.refs_4_ = bf16[2,248,384]{2,1,0:T(8,128)(2,1)S(1)} collective-permute-done((bf16[2,248,384]{2,1,0:T(8,128)(2,1)}, bf16[2,248,384]{2,1,0:T(8,128)(2,1)S(1)}, u32[]{:S(2)}, u32[]{:S(2)}) %collective-permute-start.9) | collective-permute-done | bytes 380960 | tf_op jit(solution)/shard_map/ppermute | solution.py:681
  71.7 1.1 collective-permute-done.12.refs_3_.refs_4_.refs_5_.refs_6_
  72.9 7.3 %front_back.1 = (bf16[392,768]{1,0:T(8,128)(2,1)}, bf16[1,208,384]{2,1,0:T(8,128)(2,1)}, bf16[1,208,384]{2,1,0:T(8,128)(2,1)}) custom-call(s32[1]{0:T(128)} %bitcast.blk_ref, bf16[3,392,384]{2,1,0:T(8,128)(2,1)} %get-tuple-element.118.refs_0_.refs_2_, bf16[392,384]{1,0:T(8,128)(2,1)} %get-tuple-element.119.refs_1_, ...), custom_call_target="tpu_custom_call" | custom-call | flops 1 | bytes 1 | tf_op jit(solution)/shard_map/front_back/pallas_call | solution.py:658
  80.2 0.6 collective-permute-start.14
  80.7 2.4 %combine.11 = (bf16[4,3,24,768]{3,2,1,0:T(8,128)(2,1)}, bf16[4,3,24,768]{3,2,1,0:T(8,128)(2,1)}, bf16[4,3,24,768]{3,2,1,0:T(8,128)(2,1)}) custom-call(bf16[8,3,24,768]{3,2,1,0:T(8,128)(2,1)S(1)} %copy-done, bf16[8,3,24,768]{3,2,1,0:T(8,128)(2,1)} %collective-permute-done.11.refs_1_, bf16[8,3,24,768]{3,2,1,0:T(8,128)(2,1)S(1)} %copy-done.1, ...), custom_call_target="tpu_custom_call" | custom-call | flops 1 | bytes 1 | tf_op jit(solution)/shard_map/combine/pallas_call | solution.py:723
  83.1 0.7 combine.12.refs_0_
  83.8 1.8 %collective-permute-start.19 = (bf16[1,208,384]{2,1,0:T(8,128)(2,1)}, bf16[1,208,384]{2,1,0:T(8,128)(2,1)}, u32[]{:S(2)}, u32[]{:S(2)}) collective-permute-start(bf16[1,208,384]{2,1,0:T(8,128)(2,1)} %combine.12.refs_0_), channel_id=1, source_target_pairs={{0,8},{2,10},{4,12},{6,14},{8,0},{10,2},{12,4},{14,6},{16,24},{18,... | collective-permute-start | bytes 479240 | tf_op jit(solution)/shard_map/ppermute | solution.py:685
  85.8 1.7 %collective-permute-start.22 = (bf16[4,3,24,768]{3,2,1,0:T(8,128)(2,1)}, bf16[4,3,24,768]{3,2,1,0:T(8,128)(2,1)}, u32[]{:S(2)}, u32[]{:S(2)}) collective-permute-start(bf16[4,3,24,768]{3,2,1,0:T(8,128)(2,1)} %get-tuple-element.147), channel_id=1, source_target_pairs={{0,2},{2,0},{4,6},{6,4},{8,10},{10,8},{12,14},{14,12},{16,18},{18,... | collective-permute-start | bytes 1327112 | tf_op jit(solution)/shard_map/ppermute | solution.py:685
  87.6 1.5 %collective-permute-start.20 = (bf16[4,3,24,768]{3,2,1,0:T(8,128)(2,1)}, bf16[4,3,24,768]{3,2,1,0:T(8,128)(2,1)}, u32[]{:S(2)}, u32[]{:S(2)}) collective-permute-start(bf16[4,3,24,768]{3,2,1,0:T(8,128)(2,1)} %get-tuple-element.137), channel_id=1, source_target_pairs={{0,4},{2,6},{4,0},{6,2},{8,12},{10,14},{12,8},{14,10},{16,20},{18,... | collective-permute-start | bytes 1327112 | tf_op jit(solution)/shard_map/ppermute | solution.py:685
  89.1 5.9 %attend_weights.1 = (bf16[8,24,1152]{2,1,0:T(8,128)(2,1)}, bf16[8,24,1152]{2,1,0:T(8,128)(2,1)}, bf16[8,24,1152]{2,1,0:T(8,128)(2,1)}, bf16[8,24,1152]{2,1,0:T(8,128)(2,1)}) custom-call(s32[1]{0:T(128)} %bitcast.4.own_ref, s32[1]{0:T(128)} %bitcast.blk_ref, bf16[392,768]{1,0:T(8,128)(2,1)} %get-tuple-element.140.refs_0_, ...), custom_call_target="tpu_custom_call" | custom-call | flops 1 | bytes 1 | tf_op jit(solution)/shard_map/attend_weights/pallas_call | solution.py:595
  95.0 0.6 collective-permute-start.23
  95.9 1.0 combine.13.refs_0_
  97.0 2.6 %collective-permute-done.21.refs_5_.refs_6_.refs_7_ = bf16[4,3,24,768]{3,2,1,0:T(8,128)(2,1)S(1)} collective-permute-done((bf16[4,3,24,768]{3,2,1,0:T(8,128)(2,1)}, bf16[4,3,24,768]{3,2,1,0:T(8,128)(2,1)S(1)}, u32[]{:S(2)}, u32[]{:S(2)}) %collective-permute-start.21) | collective-permute-done | bytes 442400 | tf_op jit(solution)/shard_map/ppermute | solution.py:685
  99.6 2.7 %collective-permute-start.25 = (bf16[1,208,384]{2,1,0:T(8,128)(2,1)S(1)}, bf16[1,208,384]{2,1,0:T(8,128)(2,1)S(1)}, u32[]{:S(2)}, u32[]{:S(2)}) collective-permute-start(bf16[1,208,384]{2,1,0:T(8,128)(2,1)S(1)} %combine.13.refs_0_), channel_id=1, source_target_pairs={{0,16},{2,18},{4,20},{6,22},{8,24},{10,26},{12,28},{14,30},{16,0},... | collective-permute-start | bytes 479240 | tf_op jit(solution)/shard_map/ppermute | solution.py:685
  102.4 1.5 %combine.14 = (bf16[2,3,24,768]{3,2,1,0:T(8,128)(2,1)S(1)}, bf16[2,3,24,768]{3,2,1,0:T(8,128)(2,1)S(1)}, bf16[2,3,24,768]{3,2,1,0:T(8,128)(2,1)S(1)}) custom-call(bf16[8,3,24,768]{3,2,1,0:T(8,128)(2,1)S(1)} %copy-done, bf16[8,3,24,768]{3,2,1,0:T(8,128)(2,1)} %collective-permute-done.11.refs_1_, bf16[4,3,24,768]{3,2,1,0:T(8,128)(2,1)} %collective-permute-done.20.refs_2_, ...), custom_call_target="tpu_custom_call" | custom-call | flops 1 | bytes 1 | tf_op jit(solution)/shard_map/combine/pallas_call | solution.py:723
  103.9 1.6 %collective-permute-start.27 = (bf16[2,3,24,768]{3,2,1,0:T(8,128)(2,1)S(1)}, bf16[2,3,24,768]{3,2,1,0:T(8,128)(2,1)S(1)}, u32[]{:S(2)}, u32[]{:S(2)}) collective-permute-start(bf16[2,3,24,768]{3,2,1,0:T(8,128)(2,1)S(1)} %get-tuple-element.155), channel_id=1, source_target_pairs={{0,2},{2,0},{4,6},{6,4},{8,10},{10,8},{12,14},{14,12},{16,18},{18,... | collective-permute-start | bytes 663560 | tf_op jit(solution)/shard_map/ppermute | solution.py:685
  105.4 1.5 %collective-permute-start.28 = (bf16[2,3,24,768]{3,2,1,0:T(8,128)(2,1)S(1)}, bf16[2,3,24,768]{3,2,1,0:T(8,128)(2,1)S(1)}, u32[]{:S(2)}, u32[]{:S(2)}) collective-permute-start(bf16[2,3,24,768]{3,2,1,0:T(8,128)(2,1)S(1)} %get-tuple-element.156), channel_id=1, source_target_pairs={{0,4},{2,6},{4,0},{6,2},{8,12},{10,14},{12,8},{14,10},{16,20},{18,... | collective-permute-start | bytes 663560 | tf_op jit(solution)/shard_map/ppermute | solution.py:685
  106.9 3.3 %collective-permute-done.23.refs_3_.refs_4_.refs_5_.refs_6_ = bf16[8,24,1152]{2,1,0:T(8,128)(2,1)S(1)} collective-permute-done((bf16[8,24,1152]{2,1,0:T(8,128)(2,1)}, bf16[8,24,1152]{2,1,0:T(8,128)(2,1)S(1)}, u32[]{:S(2)}, u32[]{:S(2)}) %collective-permute-start.23) | collective-permute-done | bytes 442400 | tf_op jit(solution)/shard_map/ppermute | solution.py:685
  110.2 1.6 %collective-permute-start.26 = (bf16[2,3,24,768]{3,2,1,0:T(8,128)(2,1)S(1)}, bf16[2,3,24,768]{3,2,1,0:T(8,128)(2,1)S(1)}, u32[]{:S(2)}, u32[]{:S(2)}) collective-permute-start(bf16[2,3,24,768]{3,2,1,0:T(8,128)(2,1)S(1)} %get-tuple-element.148), channel_id=1, source_target_pairs={{0,8},{2,10},{4,12},{6,14},{8,0},{10,2},{12,4},{14,6},{16,24},{18,... | collective-permute-start | bytes 663560 | tf_op jit(solution)/shard_map/ppermute | solution.py:685
  111.9 0.6 collective-permute-start.29
  112.5 1.5 %collective-permute-start.24 = (bf16[4,24,1152]{2,1,0:T(8,128)(2,1)S(1)}, bf16[4,24,1152]{2,1,0:T(8,128)(2,1)S(1)}, u32[]{:S(2)}, u32[]{:S(2)}) collective-permute-start(bf16[4,24,1152]{2,1,0:T(8,128)(2,1)S(1)} %get-tuple-element.152), channel_id=1, source_target_pairs={{0,4},{2,6},{4,0},{6,2},{8,12},{10,14},{12,8},{14,10},{16,20},{18,... | collective-permute-start | bytes 663560 | tf_op jit(solution)/shard_map/ppermute | solution.py:685
  114.1 0.9 collective-permute-done.28.refs_11_.refs_13_
  115.0 1.2 collective-permute-done.26.refs_3_
  116.2 1.2 combine.17
  117.4 3.4 %collective-permute-start.34 = (bf16[3,3,24,768]{3,2,1,0:T(8,128)(2,1)S(1)}, bf16[3,3,24,768]{3,2,1,0:T(8,128)(2,1)S(1)}, u32[]{:S(2)}, u32[]{:S(2)}) collective-permute-start(bf16[3,3,24,768]{3,2,1,0:T(8,128)(2,1)S(1)} %combine.17), channel_id=1, source_target_pairs={{0,16},{2,18},{4,20},{6,22},{8,24},{10,26},{12,28},{14,30},{16,0},... | collective-permute-start | bytes 995336 | tf_op jit(solution)/shard_map/ppermute | solution.py:685
  120.7 1.5 %collective-permute-start.31 = (bf16[1,208,384]{2,1,0:T(8,128)(2,1)S(1)}, bf16[1,208,384]{2,1,0:T(8,128)(2,1)S(1)}, u32[]{:S(2)}, u32[]{:S(2)}) collective-permute-start(bf16[1,208,384]{2,1,0:T(8,128)(2,1)S(1)} %combine.16.refs_0_), channel_id=1, source_target_pairs={{0,4},{2,6},{4,0},{6,2},{8,12},{10,14},{12,8},{14,10},{16,20},{18,... | collective-permute-start | bytes 479240 | tf_op jit(solution)/shard_map/ppermute | solution.py:685
  122.3 1.1 collective-permute-start.30
  123.4 2.6 %collective-permute-done.31.refs_1_ = bf16[1,208,384]{2,1,0:T(8,128)(2,1)S(1)} collective-permute-done((bf16[1,208,384]{2,1,0:T(8,128)(2,1)S(1)}, bf16[1,208,384]{2,1,0:T(8,128)(2,1)S(1)}, u32[]{:S(2)}, u32[]{:S(2)}) %collective-permute-start.31) | collective-permute-done | bytes 159776 | tf_op jit(solution)/shard_map/ppermute | solution.py:685
  126.1 3.3 %collective-permute-done.30.refs_3_.refs_7_.refs_8_ = bf16[4,24,1152]{2,1,0:T(8,128)(2,1)S(1)} collective-permute-done((bf16[4,24,1152]{2,1,0:T(8,128)(2,1)S(1)}, bf16[4,24,1152]{2,1,0:T(8,128)(2,1)S(1)}, u32[]{:S(2)}, u32[]{:S(2)}) %collective-permute-start.30) | collective-permute-done | bytes 221216 | tf_op jit(solution)/shard_map/ppermute | solution.py:685
  129.5 2.6 %collective-permute-start.32 = (bf16[2,24,1152]{2,1,0:T(8,128)(2,1)S(1)}, bf16[2,24,1152]{2,1,0:T(8,128)(2,1)S(1)}, u32[]{:S(2)}, u32[]{:S(2)}) collective-permute-start(bf16[2,24,1152]{2,1,0:T(8,128)(2,1)S(1)} %combine.20), channel_id=1, source_target_pairs={{0,16},{2,18},{4,20},{6,22},{8,24},{10,26},{12,28},{14,30},{16,0},... | collective-permute-start | bytes 331784 | tf_op jit(solution)/shard_map/ppermute | solution.py:685
  132.1 1.1 collective-permute-done.34.refs_4_.refs_9_.refs_14_
  133.2 1.9 %split_feed.1 = (f32[96,768]{1,0:T(8,128)}, f32[3,24,768]{2,1,0:T(8,128)S(1)}, f32[3,24,768]{2,1,0:T(8,128)S(1)}) custom-call(s32[1]{0:T(128)} %bitcast.blk_ref, bf16[8,3,24,768]{3,2,1,0:T(8,128)(2,1)S(1)} %copy-done, bf16[8,3,24,768]{3,2,1,0:T(8,128)(2,1)} %collective-permute-done.11.refs_1_, bf16[4,3,24,768]{3,2,1,0:T(8,128)(2,1)} %collective-permute-done.20.refs_2_, ...), custom_call_target="tpu_custom_call" | custom-call | flops 1 | bytes 1 | tf_op jit(solution)/shard_map/split_feed/pallas_call | solution.py:834
  135.2 0.6 collective-permute-start.37
  135.9 0.9 collective-permute-done.37.refs_5_
  137.2 1.1 join.1
  (78 shorter events, 5.7 us)
Async XLA Ops:
  0.6 2.4 %collective-permute-start = (bf16[392,768]{1,0:T(8,128)(2,1)}, bf16[392,768]{1,0:T(8,128)(2,1)S(1)}, u32[]{:S(2)}, u32[]{:S(2)}) collective-permute-start(bf16[392,768]{1,0:T(8,128)(2,1)} %bitcast.10), channel_id=1, source_target_pairs={{0,1},{1,0},{2,3},{3,2},{4,5},{5,4},{6,7},{7,6},{8,9},{9,8},{10,11... | collective-permute-start | bytes 1806344 | tf_op jit(solution)/shard_map/ppermute | solution.py:681
  1.2 1.9 %collective-permute-start.1 = (s32[1,392]{1,0:T(1,128)}, s32[1,392]{1,0:T(1,128)S(1)}, u32[]{:S(2)}, u32[]{:S(2)}) collective-permute-start(s32[1,392]{1,0:T(1,128)} %refs_2_.1), channel_id=1, source_target_pairs={{0,1},{1,0},{2,3},{3,2},{4,5},{5,4},{6,7},{7,6},{8,9},{9,8},{10,11... | collective-permute-start | bytes 4712 | tf_op jit(solution)/shard_map/ppermute | solution.py:681
  1.2 1.8 %collective-permute-start.2 = (s32[1,392]{1,0:T(1,128)}, s32[1,392]{1,0:T(1,128)S(1)}, u32[]{:S(2)}, u32[]{:S(2)}) collective-permute-start(s32[1,392]{1,0:T(1,128)} %refs_10_.3), channel_id=1, source_target_pairs={{0,1},{1,0},{2,3},{3,2},{4,5},{5,4},{6,7},{7,6},{8,9},{9,8},{10,11... | collective-permute-start | bytes 4712 | tf_op jit(solution)/shard_map/ppermute | solution.py:681
  1.7 28.6 %collective-permute-start.3 = (bf16[392,768]{1,0:T(8,128)(2,1)}, bf16[392,768]{1,0:T(8,128)(2,1)S(1)}, u32[]{:S(2)}, u32[]{:S(2)}) collective-permute-start(bf16[392,768]{1,0:T(8,128)(2,1)} %bitcast.6), channel_id=1, source_target_pairs={{0,1},{1,0},{2,3},{3,2},{4,5},{5,4},{6,7},{7,6},{8,9},{9,8},{10,11... | collective-permute-start | bytes 1806344 | tf_op jit(solution)/shard_map/ppermute | solution.py:681
  29.7 7.8 %collective-permute-start.5 = (bf16[392,1536]{1,0:T(8,128)(2,1)}, bf16[392,1536]{1,0:T(8,128)(2,1)S(1)}, u32[]{:S(2)}, u32[]{:S(2)}) collective-permute-start(bf16[392,1536]{1,0:T(8,128)(2,1)} %get-tuple-element.107), channel_id=1, source_target_pairs={{0,1},{1,0},{2,3},{3,2},{4,5},{5,4},{6,7},{7,6},{8,9},{9,8},{10,11... | collective-permute-start | bytes 3612680 | tf_op jit(solution)/shard_map/ppermute | solution.py:681
  30.2 7.4 %collective-permute-start.6 = (bf16[392,1536]{1,0:T(8,128)(2,1)}, bf16[392,1536]{1,0:T(8,128)(2,1)S(1)}, u32[]{:S(2)}, u32[]{:S(2)}) collective-permute-start(bf16[392,1536]{1,0:T(8,128)(2,1)} %get-tuple-element.109), channel_id=1, source_target_pairs={{0,1},{1,0},{2,3},{3,2},{4,5},{5,4},{6,7},{7,6},{8,9},{9,8},{10,11... | collective-permute-start | bytes 3612680 | tf_op jit(solution)/shard_map/ppermute | solution.py:681
  30.3 5.3 %copy-start.9 = (bf16[392,768]{1,0:T(8,128)(2,1)}, bf16[392,768]{1,0:T(8,128)(2,1)S(1)}, u32[]{:S(2)}) copy-start(bf16[392,768]{1,0:T(8,128)(2,1)S(1)} %collective-permute-done.3.refs_7_) | copy-start | bytes 1806340
  30.3 7.2 %collective-permute-start.4 = (bf16[392,768]{1,0:T(8,128)(2,1)}, bf16[392,768]{1,0:T(8,128)(2,1)}, u32[]{:S(2)}, u32[]{:S(2)}) collective-permute-start(bf16[392,768]{1,0:T(8,128)(2,1)} %get-tuple-element.105.refs_0_), channel_id=1, source_target_pairs={{0,1},{1,0},{2,3},{3,2},{4,5},{5,4},{6,7},{7,6},{8,9},{9,8},{10,11... | collective-permute-start | bytes 1806344 | tf_op jit(solution)/shard_map/ppermute | solution.py:681
  30.7 6.8 %collective-permute-start.7 = (bf16[392,768]{1,0:T(8,128)(2,1)}, bf16[392,768]{1,0:T(8,128)(2,1)}, u32[]{:S(2)}, u32[]{:S(2)}) collective-permute-start(bf16[392,768]{1,0:T(8,128)(2,1)} %get-tuple-element.110.refs_8_), channel_id=1, source_target_pairs={{0,1},{1,0},{2,3},{3,2},{4,5},{5,4},{6,7},{7,6},{8,9},{9,8},{10,11... | collective-permute-start | bytes 1806344 | tf_op jit(solution)/shard_map/ppermute | solution.py:681
  35.6 1.9 %collective-permute-start.8 = (bf16[392,384]{1,0:T(8,128)(2,1)}, bf16[392,384]{1,0:T(8,128)(2,1)S(1)}, u32[]{:S(2)}, u32[]{:S(2)}) collective-permute-start(bf16[392,384]{1,0:T(8,128)(2,1)} %get-tuple-element.112), channel_id=1, source_target_pairs={{0,1},{1,0},{2,3},{3,2},{4,5},{5,4},{6,7},{7,6},{8,9},{9,8},{10,11... | collective-permute-start | bytes 903176 | tf_op jit(solution)/shard_map/ppermute | solution.py:681
  37.5 1.5 %copy-start.8 = (bf16[392,1536]{1,0:T(8,128)(2,1)}, bf16[392,1536]{1,0:T(8,128)(2,1)S(1)}, u32[]{:S(2)}) copy-start(bf16[392,1536]{1,0:T(8,128)(2,1)S(1)} %collective-permute-done.6.refs_5_) | copy-start | bytes 3612676
  49.7 23.1 %collective-permute-start.12 = (bf16[8,3,24,768]{3,2,1,0:T(8,128)(2,1)}, bf16[8,3,24,768]{3,2,1,0:T(8,128)(2,1)S(1)}, u32[]{:S(2)}, u32[]{:S(2)}) collective-permute-start(bf16[8,3,24,768]{3,2,1,0:T(8,128)(2,1)} %get-tuple-element.134), channel_id=1, source_target_pairs={{0,4},{2,6},{4,0},{6,2},{8,12},{10,14},{12,8},{14,10},{16,20},{18,... | collective-permute-start | bytes 2654216 | tf_op jit(solution)/shard_map/ppermute | solution.py:685
  52.7 27.5 %collective-permute-start.13 = (bf16[8,3,24,768]{3,2,1,0:T(8,128)(2,1)}, bf16[8,3,24,768]{3,2,1,0:T(8,128)(2,1)}, u32[]{:S(2)}, u32[]{:S(2)}) collective-permute-start(bf16[8,3,24,768]{3,2,1,0:T(8,128)(2,1)} %get-tuple-element.136), channel_id=1, source_target_pairs={{0,8},{2,10},{4,12},{6,14},{8,0},{10,2},{12,4},{14,6},{16,24},{18,... | collective-permute-start | bytes 2654216 | tf_op jit(solution)/shard_map/ppermute | solution.py:685
  54.2 26.5 %collective-permute-start.11 = (bf16[8,3,24,768]{3,2,1,0:T(8,128)(2,1)}, bf16[8,3,24,768]{3,2,1,0:T(8,128)(2,1)}, u32[]{:S(2)}, u32[]{:S(2)}) collective-permute-start(bf16[8,3,24,768]{3,2,1,0:T(8,128)(2,1)} %get-tuple-element.113), channel_id=1, source_target_pairs={{0,2},{2,0},{4,6},{6,4},{8,10},{10,8},{12,14},{14,12},{16,18},{18,... | collective-permute-start | bytes 2654216 | tf_op jit(solution)/shard_map/ppermute | solution.py:685
  69.0 2.0 %collective-permute-start.9 = (bf16[2,248,384]{2,1,0:T(8,128)(2,1)}, bf16[2,248,384]{2,1,0:T(8,128)(2,1)S(1)}, u32[]{:S(2)}, u32[]{:S(2)}) collective-permute-start(bf16[2,248,384]{2,1,0:T(8,128)(2,1)} %get-tuple-element.122), channel_id=1, source_target_pairs={{0,1},{1,0},{2,3},{3,2},{4,5},{5,4},{6,7},{7,6},{8,9},{9,8},{10,11... | collective-permute-start | bytes 1142792 | tf_op jit(solution)/shard_map/ppermute | solution.py:681
  69.1 2.4 %collective-permute-start.10 = (bf16[2,248,384]{2,1,0:T(8,128)(2,1)}, bf16[2,248,384]{2,1,0:T(8,128)(2,1)S(1)}, u32[]{:S(2)}, u32[]{:S(2)}) collective-permute-start(bf16[2,248,384]{2,1,0:T(8,128)(2,1)} %get-tuple-element.123.refs_3_), channel_id=1, source_target_pairs={{0,1},{1,0},{2,3},{3,2},{4,5},{5,4},{6,7},{7,6},{8,9},{9,8},{10,11... | collective-permute-start | bytes 1142792 | tf_op jit(solution)/shard_map/ppermute | solution.py:681
  71.0 1.8 %copy-start.6 = (bf16[2,248,384]{2,1,0:T(8,128)(2,1)}, bf16[2,248,384]{2,1,0:T(8,128)(2,1)S(1)}, u32[]{:S(2)}) copy-start(bf16[2,248,384]{2,1,0:T(8,128)(2,1)S(1)} %collective-permute-done.9.refs_4_) | copy-start | bytes 1142788
  71.0 14.8 %collective-permute-start.15 = (bf16[392,384]{1,0:T(8,128)(2,1)}, bf16[392,384]{1,0:T(8,128)(2,1)}, u32[]{:S(2)}, u32[]{:S(2)}) collective-permute-start(bf16[392,384]{1,0:T(8,128)(2,1)} %get-tuple-element.119.refs_1_), channel_id=1, source_target_pairs={{0,1},{1,0},{2,3},{3,2},{4,5},{5,4},{6,7},{7,6},{8,9},{9,8},{10,11... | collective-permute-start | bytes 903176 | tf_op jit(solution)/shard_map/ppermute | solution.py:681
  71.6 1.3 copy-start.10
  71.6 16.0 %collective-permute-start.16 = (bf16[392,384]{1,0:T(8,128)(2,1)}, bf16[392,384]{1,0:T(8,128)(2,1)}, u32[]{:S(2)}, u32[]{:S(2)}) collective-permute-start(bf16[392,384]{1,0:T(8,128)(2,1)} %get-tuple-element.120.refs_2_), channel_id=1, source_target_pairs={{0,1},{1,0},{2,3},{3,2},{4,5},{5,4},{6,7},{7,6},{8,9},{9,8},{10,11... | collective-permute-start | bytes 903176 | tf_op jit(solution)/shard_map/ppermute | solution.py:681
  72.8 16.3 %collective-permute-start.17 = (bf16[392,384]{1,0:T(8,128)(2,1)}, bf16[392,384]{1,0:T(8,128)(2,1)}, u32[]{:S(2)}, u32[]{:S(2)}) collective-permute-start(bf16[392,384]{1,0:T(8,128)(2,1)} %get-tuple-element.121.refs_3_), channel_id=1, source_target_pairs={{0,1},{1,0},{2,3},{3,2},{4,5},{5,4},{6,7},{7,6},{8,9},{9,8},{10,11... | collective-permute-start | bytes 903176 | tf_op jit(solution)/shard_map/ppermute | solution.py:681
  72.8 7.9 %copy-start = (bf16[8,3,24,768]{3,2,1,0:T(8,128)(2,1)S(1)}, bf16[8,3,24,768]{3,2,1,0:T(8,128)(2,1)}, u32[]{:S(2)}) copy-start(bf16[8,3,24,768]{3,2,1,0:T(8,128)(2,1)} %get-tuple-element.154.refs_0_) | copy-start | bytes 2654212
  72.8 7.9 %copy-start.1 = (bf16[8,3,24,768]{3,2,1,0:T(8,128)(2,1)S(1)}, bf16[8,3,24,768]{3,2,1,0:T(8,128)(2,1)}, u32[]{:S(2)}) copy-start(bf16[8,3,24,768]{3,2,1,0:T(8,128)(2,1)} %get-tuple-element.133.refs_2_.refs_3_.refs_4_.refs_5_) | copy-start | bytes 2654212
  72.9 7.9 %copy-start.2 = (bf16[8,3,24,768]{3,2,1,0:T(8,128)(2,1)S(1)}, bf16[8,3,24,768]{3,2,1,0:T(8,128)(2,1)}, u32[]{:S(2)}) copy-start(bf16[8,3,24,768]{3,2,1,0:T(8,128)(2,1)} %get-tuple-element.135.refs_4_.refs_6_.refs_8_.refs_10_) | copy-start | bytes 2654212
  80.2 3.0 %collective-permute-start.14 = (bf16[1,208,384]{2,1,0:T(8,128)(2,1)}, bf16[1,208,384]{2,1,0:T(8,128)(2,1)S(1)}, u32[]{:S(2)}, u32[]{:S(2)}) collective-permute-start(bf16[1,208,384]{2,1,0:T(8,128)(2,1)} %get-tuple-element.139), channel_id=1, source_target_pairs={{0,1},{1,0},{2,3},{3,2},{4,5},{5,4},{6,7},{7,6},{8,9},{9,8},{10,11... | collective-permute-start | bytes 479240 | tf_op jit(solution)/shard_map/ppermute | solution.py:681
  80.7 2.4 %copy-start.5 = (bf16[1,208,384]{2,1,0:T(8,128)(2,1)S(1)}, bf16[1,208,384]{2,1,0:T(8,128)(2,1)}, u32[]{:S(2)}) copy-start(bf16[1,208,384]{2,1,0:T(8,128)(2,1)} %get-tuple-element.138.refs_0_) | copy-start | bytes 479236
  83.8 11.8 %collective-permute-start.19 = (bf16[1,208,384]{2,1,0:T(8,128)(2,1)}, bf16[1,208,384]{2,1,0:T(8,128)(2,1)}, u32[]{:S(2)}, u32[]{:S(2)}) collective-permute-start(bf16[1,208,384]{2,1,0:T(8,128)(2,1)} %combine.12.refs_0_), channel_id=1, source_target_pairs={{0,8},{2,10},{4,12},{6,14},{8,0},{10,2},{12,4},{14,6},{16,24},{18,... | collective-permute-start | bytes 479240 | tf_op jit(solution)/shard_map/ppermute | solution.py:685
  85.6 14.0 %collective-permute-start.21 = (bf16[4,3,24,768]{3,2,1,0:T(8,128)(2,1)}, bf16[4,3,24,768]{3,2,1,0:T(8,128)(2,1)S(1)}, u32[]{:S(2)}, u32[]{:S(2)}) collective-permute-start(bf16[4,3,24,768]{3,2,1,0:T(8,128)(2,1)} %get-tuple-element.146), channel_id=1, source_target_pairs={{0,8},{2,10},{4,12},{6,14},{8,0},{10,2},{12,4},{14,6},{16,24},{18,... | collective-permute-start | bytes 1327112 | tf_op jit(solution)/shard_map/ppermute | solution.py:685
  85.8 16.5 %collective-permute-start.22 = (bf16[4,3,24,768]{3,2,1,0:T(8,128)(2,1)}, bf16[4,3,24,768]{3,2,1,0:T(8,128)(2,1)}, u32[]{:S(2)}, u32[]{:S(2)}) collective-permute-start(bf16[4,3,24,768]{3,2,1,0:T(8,128)(2,1)} %get-tuple-element.147), channel_id=1, source_target_pairs={{0,2},{2,0},{4,6},{6,4},{8,10},{10,8},{12,14},{14,12},{16,18},{18,... | collective-permute-start | bytes 1327112 | tf_op jit(solution)/shard_map/ppermute | solution.py:685
  87.6 14.8 %collective-permute-start.20 = (bf16[4,3,24,768]{3,2,1,0:T(8,128)(2,1)}, bf16[4,3,24,768]{3,2,1,0:T(8,128)(2,1)}, u32[]{:S(2)}, u32[]{:S(2)}) collective-permute-start(bf16[4,3,24,768]{3,2,1,0:T(8,128)(2,1)} %get-tuple-element.137), channel_id=1, source_target_pairs={{0,4},{2,6},{4,0},{6,2},{8,12},{10,14},{12,8},{14,10},{16,20},{18,... | collective-permute-start | bytes 1327112 | tf_op jit(solution)/shard_map/ppermute | solution.py:685
  95.0 15.2 %collective-permute-start.23 = (bf16[8,24,1152]{2,1,0:T(8,128)(2,1)}, bf16[8,24,1152]{2,1,0:T(8,128)(2,1)S(1)}, u32[]{:S(2)}, u32[]{:S(2)}) collective-permute-start(bf16[8,24,1152]{2,1,0:T(8,128)(2,1)} %get-tuple-element.151), channel_id=1, source_target_pairs={{0,4},{2,6},{4,0},{6,2},{8,12},{10,14},{12,8},{14,10},{16,20},{18,... | collective-permute-start | bytes 1327112 | tf_op jit(solution)/shard_map/ppermute | solution.py:685
  95.6 16.2 %collective-permute-start.18 = (bf16[8,24,1152]{2,1,0:T(8,128)(2,1)}, bf16[8,24,1152]{2,1,0:T(8,128)(2,1)S(1)}, u32[]{:S(2)}, u32[]{:S(2)}) collective-permute-start(bf16[8,24,1152]{2,1,0:T(8,128)(2,1)} %get-tuple-element.143), channel_id=1, source_target_pairs={{0,2},{2,0},{4,6},{6,4},{8,10},{10,8},{12,14},{14,12},{16,18},{18,... | collective-permute-start | bytes 1327112 | tf_op jit(solution)/shard_map/ppermute | solution.py:685
  97.0 14.8 %copy-start.3 = (bf16[8,24,1152]{2,1,0:T(8,128)(2,1)S(1)}, bf16[8,24,1152]{2,1,0:T(8,128)(2,1)}, u32[]{:S(2)}) copy-start(bf16[8,24,1152]{2,1,0:T(8,128)(2,1)} %get-tuple-element.160.refs_0_) | copy-start | bytes 1327108
  97.0 14.8 %copy-start.4 = (bf16[8,24,1152]{2,1,0:T(8,128)(2,1)S(1)}, bf16[8,24,1152]{2,1,0:T(8,128)(2,1)}, u32[]{:S(2)}) copy-start(bf16[8,24,1152]{2,1,0:T(8,128)(2,1)} %get-tuple-element.150.refs_2_.refs_3_.refs_4_.refs_5_) | copy-start | bytes 1327108
  99.6 12.9 %collective-permute-start.25 = (bf16[1,208,384]{2,1,0:T(8,128)(2,1)S(1)}, bf16[1,208,384]{2,1,0:T(8,128)(2,1)S(1)}, u32[]{:S(2)}, u32[]{:S(2)}) collective-permute-start(bf16[1,208,384]{2,1,0:T(8,128)(2,1)S(1)} %combine.13.refs_0_), channel_id=1, source_target_pairs={{0,16},{2,18},{4,20},{6,22},{8,24},{10,26},{12,28},{14,30},{16,0},... | collective-permute-start | bytes 479240 | tf_op jit(solution)/shard_map/ppermute | solution.py:685
  103.9 10.2 %collective-permute-start.27 = (bf16[2,3,24,768]{3,2,1,0:T(8,128)(2,1)S(1)}, bf16[2,3,24,768]{3,2,1,0:T(8,128)(2,1)S(1)}, u32[]{:S(2)}, u32[]{:S(2)}) collective-permute-start(bf16[2,3,24,768]{3,2,1,0:T(8,128)(2,1)S(1)} %get-tuple-element.155), channel_id=1, source_target_pairs={{0,2},{2,0},{4,6},{6,4},{8,10},{10,8},{12,14},{14,12},{16,18},{18,... | collective-permute-start | bytes 663560 | tf_op jit(solution)/shard_map/ppermute | solution.py:685
  105.4 9.5 %collective-permute-start.28 = (bf16[2,3,24,768]{3,2,1,0:T(8,128)(2,1)S(1)}, bf16[2,3,24,768]{3,2,1,0:T(8,128)(2,1)S(1)}, u32[]{:S(2)}, u32[]{:S(2)}) collective-permute-start(bf16[2,3,24,768]{3,2,1,0:T(8,128)(2,1)S(1)} %get-tuple-element.156), channel_id=1, source_target_pairs={{0,4},{2,6},{4,0},{6,2},{8,12},{10,14},{12,8},{14,10},{16,20},{18,... | collective-permute-start | bytes 663560 | tf_op jit(solution)/shard_map/ppermute | solution.py:685
  110.2 5.9 %collective-permute-start.26 = (bf16[2,3,24,768]{3,2,1,0:T(8,128)(2,1)S(1)}, bf16[2,3,24,768]{3,2,1,0:T(8,128)(2,1)S(1)}, u32[]{:S(2)}, u32[]{:S(2)}) collective-permute-start(bf16[2,3,24,768]{3,2,1,0:T(8,128)(2,1)S(1)} %get-tuple-element.148), channel_id=1, source_target_pairs={{0,8},{2,10},{4,12},{6,14},{8,0},{10,2},{12,4},{14,6},{16,24},{18,... | collective-permute-start | bytes 663560 | tf_op jit(solution)/shard_map/ppermute | solution.py:685
  111.9 10.3 %collective-permute-start.29 = (bf16[4,24,1152]{2,1,0:T(8,128)(2,1)S(1)}, bf16[4,24,1152]{2,1,0:T(8,128)(2,1)S(1)}, u32[]{:S(2)}, u32[]{:S(2)}) collective-permute-start(bf16[4,24,1152]{2,1,0:T(8,128)(2,1)S(1)} %get-tuple-element.158), channel_id=1, source_target_pairs={{0,2},{2,0},{4,6},{6,4},{8,10},{10,8},{12,14},{14,12},{16,18},{18,... | collective-permute-start | bytes 663560 | tf_op jit(solution)/shard_map/ppermute | solution.py:685
  112.5 9.7 %collective-permute-start.24 = (bf16[4,24,1152]{2,1,0:T(8,128)(2,1)S(1)}, bf16[4,24,1152]{2,1,0:T(8,128)(2,1)S(1)}, u32[]{:S(2)}, u32[]{:S(2)}) collective-permute-start(bf16[4,24,1152]{2,1,0:T(8,128)(2,1)S(1)} %get-tuple-element.152), channel_id=1, source_target_pairs={{0,4},{2,6},{4,0},{6,2},{8,12},{10,14},{12,8},{14,10},{16,20},{18,... | collective-permute-start | bytes 663560 | tf_op jit(solution)/shard_map/ppermute | solution.py:685
  117.4 15.9 %collective-permute-start.34 = (bf16[3,3,24,768]{3,2,1,0:T(8,128)(2,1)S(1)}, bf16[3,3,24,768]{3,2,1,0:T(8,128)(2,1)S(1)}, u32[]{:S(2)}, u32[]{:S(2)}) collective-permute-start(bf16[3,3,24,768]{3,2,1,0:T(8,128)(2,1)S(1)} %combine.17), channel_id=1, source_target_pairs={{0,16},{2,18},{4,20},{6,22},{8,24},{10,26},{12,28},{14,30},{16,0},... | collective-permute-start | bytes 995336 | tf_op jit(solution)/shard_map/ppermute | solution.py:685
  120.7 5.3 %collective-permute-start.31 = (bf16[1,208,384]{2,1,0:T(8,128)(2,1)S(1)}, bf16[1,208,384]{2,1,0:T(8,128)(2,1)S(1)}, u32[]{:S(2)}, u32[]{:S(2)}) collective-permute-start(bf16[1,208,384]{2,1,0:T(8,128)(2,1)S(1)} %combine.16.refs_0_), channel_id=1, source_target_pairs={{0,4},{2,6},{4,0},{6,2},{8,12},{10,14},{12,8},{14,10},{16,20},{18,... | collective-permute-start | bytes 479240 | tf_op jit(solution)/shard_map/ppermute | solution.py:685
  122.3 7.1 %collective-permute-start.30 = (bf16[4,24,1152]{2,1,0:T(8,128)(2,1)S(1)}, bf16[4,24,1152]{2,1,0:T(8,128)(2,1)S(1)}, u32[]{:S(2)}, u32[]{:S(2)}) collective-permute-start(bf16[4,24,1152]{2,1,0:T(8,128)(2,1)S(1)} %combine.18), channel_id=1, source_target_pairs={{0,8},{2,10},{4,12},{6,14},{8,0},{10,2},{12,4},{14,6},{16,24},{18,... | collective-permute-start | bytes 663560 | tf_op jit(solution)/shard_map/ppermute | solution.py:685
  126.1 9.0 %collective-permute-start.36 = (bf16[1,208,384]{2,1,0:T(8,128)(2,1)S(1)}, bf16[1,208,384]{2,1,0:T(8,128)(2,1)S(1)}, u32[]{:S(2)}, u32[]{:S(2)}) collective-permute-start(bf16[1,208,384]{2,1,0:T(8,128)(2,1)S(1)} %combine.19.refs_0_), channel_id=1, source_target_pairs={{0,2},{2,0},{4,6},{6,4},{8,10},{10,8},{12,14},{14,12},{16,18},{18,... | collective-permute-start | bytes 479240 | tf_op jit(solution)/shard_map/ppermute | solution.py:685
  129.5 6.2 %collective-permute-start.32 = (bf16[2,24,1152]{2,1,0:T(8,128)(2,1)S(1)}, bf16[2,24,1152]{2,1,0:T(8,128)(2,1)S(1)}, u32[]{:S(2)}, u32[]{:S(2)}) collective-permute-start(bf16[2,24,1152]{2,1,0:T(8,128)(2,1)S(1)} %combine.20), channel_id=1, source_target_pairs={{0,16},{2,18},{4,20},{6,22},{8,24},{10,26},{12,28},{14,30},{16,0},... | collective-permute-start | bytes 331784 | tf_op jit(solution)/shard_map/ppermute | solution.py:685
  135.1 2.1 %collective-permute-start.35 = (f32[3,24,768]{2,1,0:T(8,128)S(1)}, f32[3,24,768]{2,1,0:T(8,128)S(1)}, u32[]{:S(2)}, u32[]{:S(2)}) collective-permute-start(f32[3,24,768]{2,1,0:T(8,128)S(1)} %get-tuple-element.164), channel_id=1, source_target_pairs={{0,1},{1,0},{2,3},{3,2},{4,5},{5,4},{6,7},{7,6},{8,9},{9,8},{10,11... | collective-permute-start | bytes 663560 | tf_op jit(solution)/shard_map/ppermute | solution.py:681
  135.2 1.7 %collective-permute-start.37 = (bf16[1,208,384]{2,1,0:T(8,128)(2,1)S(1)}, bf16[1,208,384]{2,1,0:T(8,128)(2,1)S(1)}, u32[]{:S(2)}, u32[]{:S(2)}) collective-permute-start(bf16[1,208,384]{2,1,0:T(8,128)(2,1)S(1)} %combine.21.refs_4_), channel_id=1, source_target_pairs={{0,1},{1,0},{2,3},{3,2},{4,5},{5,4},{6,7},{7,6},{8,9},{9,8},{10,11... | collective-permute-start | bytes 479240 | tf_op jit(solution)/shard_map/ppermute | solution.py:681
  135.8 1.4 collective-permute-start.33
  (5 other events, 3.8 us)
